TPU v7x, 256 devices: a whole 4x4x8 slice. The times are simulated.
256 devices in a mesh: gx: 4 (over x), gy: 8 (over z_hi, y), gz: 8 (over z_lo, core).
Axes of the slice: x: 4, y: 4, z: 8 (z_hi: 2, z_lo: 4; z = z_hi * 4 + z_lo), core: 2. Of those that a mesh axis runs over, the one named last changes fastest.
Arguments:
- features: bfloat16 [32768, 1536], P(('gx', 'gy', 'gz')), may hold values from -6 to 6
- species: int32 [32768], P(('gx', 'gy', 'gz')), may hold values from 0 to 88
- octant_lists: int32 [2, 2, 2, 2048], P(None, None, None, ('gx', 'gy', 'gz')), may hold values from 0 to 127
- neighbour_index: int32 [32, 32768], P(None, ('gx', 'gy', 'gz')), may hold values from 0 to 319
- neighbour_count: int32 [32768], P(('gx', 'gy', 'gz')), may hold values from 16 to 32
- edge_vectors: float32 [3, 32, 32768], P(None, None, ('gx', 'gy', 'gz')), may hold values from -2.3 to 2.3
- radial_in: bfloat16 [3, 8, 64], replicated, may hold values from -3 to 3
- species_emb: bfloat16 [3, 89, 64], replicated, may hold values from -6 to 6
- radial_mid: bfloat16 [3, 64, 64], replicated, may hold values from -0.5 to 0.5
- radial_out: bfloat16 [3, 64, 384], replicated, may hold values from -0.75 to 0.75
- mix_weight: bfloat16 [3, 4, 96, 96], replicated, may hold values from -0.625 to 0.625
- gate_weight: bfloat16 [3, 96, 96], replicated, may hold values from -0.625 to 0.625
- probe_in: bfloat16 [8, 64], replicated, may hold values from -3 to 3
- probe_mid: bfloat16 [64, 64], replicated, may hold values from -0.5 to 0.5
- probe_proj: bfloat16 [4, 96, 64], replicated, may hold values from -0.01953125 to 0.01953125
- probe_vectors: float32 [3, 32, 32768], P(None, None, ('gx', 'gy', 'gz')), may hold values from -2.3 to 2.3
- probe_index: int32 [32, 32768], P(None, ('gx', 'gy', 'gz')), may hold values from 0 to 319
- probe_count: int32 [32768], P(('gx', 'gy', 'gz')), may hold values from 16 to 32
- slab_index: int32 [32], replicated, may hold values from 0 to 7
Outputs:
- atom_features: bfloat16 [32768, 1536], P(('gx', 'gy', 'gz'))
- density: float32 [32768], P(('gx', 'gy', 'gz'))
Inputs may be any that keep to these rules, and one draw needn't show every extreme that they name: `neighbour_index`: rows 0 to 127 of a table are the brick's own atoms, then 24 * 8 ghost rows in the order of the steps. Slots k >= neighbour_count of an atom are padding. `probe_index`: slots k >= probe_count of a probe are padding; rows refer to the table of the slab brick of the probe's column.
All inputs are finite; a program needn't handle non-finite values.
Results may differ from a plain program's by a relative error of at most 0.019.
Values may be sent and summed in bfloat16 or wider, within the bound.
No kernel may reach another device: no remote copies, remote signals or barrier semaphores. Data moves between devices by JAX's collectives and lax.ppermute only.
A program may use at most 128 MiB of HBM per device.

v0:
```python
import math

import jax
import jax.numpy as jnp
import numpy as np
from jax import lax
from jax.sharding import PartitionSpec as P

C = 96
COMPS = 16
RH = 64
NB = 8
K = 32
KP = 32
LAYERS = 3


cutoff = 4.0
degree_of = np.repeat(np.arange(4), np.array([1, 3, 5, 7]))
degree_starts = (0, 1, 4, 9)
degree_widths = (1, 3, 5, 7)


def with_halo(block, sides, width):
    for axis, dim in sides:
        count = lax.axis_size(axis)
        forward = [(i, i + 1) for i in range(count - 1)]
        forward.append((count - 1, 0))
        backward = [(target, source) for source, target in forward]
        low = lax.ppermute(
            lax.slice_in_dim(block, block.shape[dim] - width, None, axis=dim), axis, forward
        )
        high = lax.ppermute(lax.slice_in_dim(block, 0, width, axis=dim), axis, backward)
        block = jnp.concatenate([low, block, high], axis=dim)
    return block


def spread(block, axis, owner):
    block = jnp.where(lax.axis_index(axis) == owner, block, jnp.zeros_like(block))
    return lax.psum(block, axis)


def harmonics(vectors):
    coord_x = vectors[0] * 0.5
    coord_y = vectors[1] * 0.5
    coord_z = vectors[2] * 0.5
    square = coord_x * coord_x + coord_y * coord_y + coord_z * coord_z
    zz_term = 5.0 * coord_z * coord_z - square
    comps_list = [
        jnp.ones_like(coord_x),
        math.sqrt(3.0) * coord_x,
        math.sqrt(3.0) * coord_y,
        math.sqrt(3.0) * coord_z,
        math.sqrt(15.0) * coord_x * coord_y,
        math.sqrt(15.0) * coord_y * coord_z,
        math.sqrt(5.0) / 2.0 * (3.0 * coord_z * coord_z - square),
        math.sqrt(15.0) * coord_x * coord_z,
        math.sqrt(15.0) / 2.0 * (coord_x * coord_x - coord_y * coord_y),
        math.sqrt(35.0 / 8.0) * coord_y * (3.0 * coord_x * coord_x - coord_y * coord_y),
        math.sqrt(105.0) * coord_x * coord_y * coord_z,
        math.sqrt(21.0 / 8.0) * coord_y * zz_term,
        math.sqrt(7.0) / 2.0 * coord_z * (5.0 * coord_z * coord_z - 3.0 * square),
        math.sqrt(21.0 / 8.0) * coord_x * zz_term,
        math.sqrt(105.0) / 2.0 * coord_z * (coord_x * coord_x - coord_y * coord_y),
        math.sqrt(35.0 / 8.0) * coord_x * (coord_x * coord_x - 3.0 * coord_y * coord_y),
    ]
    return jnp.stack(comps_list, axis=-1)


def geometry(vectors):
    square = jnp.sum(vectors * vectors, axis=0)
    envelope = (1.0 - square / (cutoff * cutoff)) ** 2
    radius = jnp.sqrt(square)
    centers = jnp.arange(NB, dtype=jnp.float32) * (cutoff / (NB - 1))
    sharpness = ((NB - 1) / cutoff) ** 2
    radial_basis = jnp.exp(-sharpness * (radius[..., None] - centers) ** 2).astype(jnp.bfloat16)
    return (radial_basis, envelope, harmonics(vectors))


def block_size():
    return 32


def degree_messages(gathered, radial4, harmonic):
    scalars = gathered[:, :, 0, :]
    pieces = []
    for degree in range(4):
        start = degree_starts[degree]
        width = degree_widths[degree]
        weight_here = radial4[:, :, degree, :]
        segment = gathered[:, :, start : start + width, :]
        piece = jnp.einsum(
            "krmc,krc->rmc", segment, weight_here, preferred_element_type=jnp.float32
        )
        if degree > 0:
            piece = piece + jnp.einsum(
                "krc,krm->rmc",
                scalars * weight_here,
                harmonic[:, :, start : start + width],
                preferred_element_type=jnp.float32,
            )
        pieces.append(piece)
    return jnp.concatenate(pieces, axis=1)


def update_rows(table_rows, own_rows, species, index_rows, count_rows, vector_rows, weights):
    radial_in, species_emb, radial_mid, radial_out, mix_weight, gate_weight = weights
    slot_count, row_count = index_rows.shape
    row_width = own_rows.shape[1]
    block_rows = block_size()
    blocks = row_count // block_rows
    own_blocks = own_rows.reshape(blocks, block_rows, row_width)
    species_blocks = species.reshape(blocks, block_rows)
    index_blocks = jnp.transpose(index_rows.reshape(slot_count, blocks, block_rows), (1, 0, 2))
    count_blocks = count_rows.reshape(blocks, block_rows)
    vector_blocks = jnp.transpose(
        vector_rows.reshape(3, slot_count, blocks, block_rows), (2, 0, 1, 3)
    )
    mix_full = mix_weight[degree_of]
    species_ids = jnp.arange(species_emb.shape[0], dtype=jnp.int32)

    def update_one_block(items):
        own_part, species_part, index_part, count_part, vector_part = items
        radial_basis, envelope, harmonic = geometry(vector_part)
        onehot = (species_part[:, None] == species_ids[None, :]).astype(jnp.bfloat16)
        embedded = jnp.dot(onehot, species_emb, preferred_element_type=jnp.float32)
        hidden_one = jnp.einsum(
            "krb,bh->krh", radial_basis, radial_in, preferred_element_type=jnp.float32
        )
        hidden_one = jax.nn.silu(hidden_one + embedded[None]).astype(jnp.bfloat16)
        hidden_two = jnp.einsum(
            "krh,hg->krg", hidden_one, radial_mid, preferred_element_type=jnp.float32
        )
        hidden_two = jax.nn.silu(hidden_two).astype(jnp.bfloat16)
        radial = jnp.einsum(
            "krg,go->kro", hidden_two, radial_out, preferred_element_type=jnp.float32
        )
        valid_mask = (
            jnp.arange(slot_count, dtype=jnp.int32)[:, None] < count_part[None, :]
        ).astype(jnp.float32)
        radial = radial * (envelope * valid_mask)[..., None]
        radial4 = radial.reshape(slot_count, block_rows, 4, C)
        gathered = jnp.take(table_rows, index_part, axis=0).reshape(
            slot_count, block_rows, COMPS, C
        )
        message = (degree_messages(gathered, radial4, harmonic) * K ** (-0.5)).astype(jnp.bfloat16)
        mixed_rows = jnp.einsum(
            "rmc,mcd->rmd", message, mix_full, preferred_element_type=jnp.float32
        )
        gate_values = jax.nn.sigmoid(
            jnp.dot(message[:, 0, :], gate_weight, preferred_element_type=jnp.float32)
        )
        previous = own_part.astype(jnp.float32).reshape(block_rows, COMPS, C)
        scalar_new = previous[:, :1, :] + jax.nn.silu(mixed_rows[:, :1, :])
        higher_new = previous[:, 1:, :] + gate_values[:, None, :] * mixed_rows[:, 1:, :]
        updated = jnp.concatenate([scalar_new, higher_new], axis=1)
        return updated.reshape(block_rows, row_width).astype(jnp.bfloat16)

    result = lax.map(
        update_one_block, (own_blocks, species_blocks, index_blocks, count_blocks, vector_blocks)
    )
    return result.reshape(row_count, row_width)


def faces(send_rows):
    padded = with_halo(send_rows, (("gx", 0), ("gy", 1), ("gz", 2)), 1)
    row_width = send_rows.shape[-1]
    face_parts = [
        padded[0, 1:3, 1:3],
        padded[3, 1:3, 1:3],
        padded[1:3, 0, 1:3],
        padded[1:3, 3, 1:3],
        padded[1:3, 1:3, 0],
        padded[1:3, 1:3, 3],
    ]
    return jnp.concatenate([face_part.reshape(-1, row_width) for face_part in face_parts], axis=0)


def project(table_rows, probe_proj):
    row_count = table_rows.shape[0]
    shaped = table_rows.reshape(row_count, COMPS, C)
    projected = jnp.einsum(
        "rmc,mch->rmh", shaped, probe_proj[degree_of], preferred_element_type=jnp.float32
    )
    return projected.astype(jnp.bfloat16).reshape(row_count, COMPS * RH)


def probe_rows(key_rows, probe_vectors, probe_index, probe_count, probe_in, probe_mid):
    slot_count, row_count = probe_index.shape
    block_rows = block_size()
    blocks = row_count // block_rows
    vector_blocks = jnp.transpose(
        probe_vectors.reshape(3, slot_count, blocks, block_rows), (2, 0, 1, 3)
    )
    index_blocks = jnp.transpose(probe_index.reshape(slot_count, blocks, block_rows), (1, 0, 2))
    count_blocks = probe_count.reshape(blocks, block_rows)

    def probe_one_block(items):
        vector_part, index_part, count_part = items
        radial_basis, envelope, harmonic = geometry(vector_part)
        probe_one = jnp.einsum(
            "kpb,bh->kph", radial_basis, probe_in, preferred_element_type=jnp.float32
        )
        probe_one = jax.nn.silu(probe_one).astype(jnp.bfloat16)
        probe_two = jnp.einsum(
            "kph,hg->kpg", probe_one, probe_mid, preferred_element_type=jnp.float32
        )
        probe_two = jax.nn.silu(probe_two).astype(jnp.bfloat16)
        gathered = jnp.take(key_rows, index_part, axis=0).reshape(slot_count, block_rows, COMPS, RH)
        inner_sum = jnp.einsum(
            "kpmh,kph->kpm", gathered, probe_two, preferred_element_type=jnp.float32
        )
        valid_mask = (
            jnp.arange(slot_count, dtype=jnp.int32)[:, None] < count_part[None, :]
        ).astype(jnp.float32)
        per_edge = jnp.sum(inner_sum * harmonic, axis=-1) * envelope * valid_mask
        return jnp.sum(per_edge, axis=0) * KP ** (-0.5)

    return lax.map(probe_one_block, (vector_blocks, index_blocks, count_blocks)).reshape(row_count)


def local(
    features,
    species,
    octant_lists,
    neighbour_index,
    neighbour_count,
    edge_vectors,
    radial_in,
    species_emb,
    radial_mid,
    radial_out,
    mix_weight,
    gate_weight,
    probe_in,
    probe_mid,
    probe_proj,
    probe_vectors,
    probe_index,
    probe_count,
    slab_index,
):
    picked = octant_lists.reshape(-1)
    ghost_count = octant_lists.shape[-1]
    row_width = features.shape[1]
    own_rows = features
    ghosts = faces(jnp.take(own_rows, picked, axis=0).reshape(2, 2, 2, ghost_count, row_width))
    for layer_step in range(LAYERS):
        weights = (
            radial_in[layer_step],
            species_emb[layer_step],
            radial_mid[layer_step],
            radial_out[layer_step],
            mix_weight[layer_step],
            gate_weight[layer_step],
        )
        table_rows = jnp.concatenate([own_rows, ghosts], axis=0)
        own_rows = update_rows(
            table_rows, own_rows, species, neighbour_index, neighbour_count, edge_vectors, weights
        )
        ghosts_next = faces(
            jnp.take(own_rows, picked, axis=0).reshape(2, 2, 2, ghost_count, row_width)
        )
        ghosts = ghosts_next
    table_rows = jnp.concatenate([own_rows, ghosts], axis=0)
    column = lax.axis_index("gx") * lax.axis_size("gy") + lax.axis_index("gy")
    root_index = slab_index[column]
    key_rows = spread(project(table_rows, probe_proj), "gz", root_index)
    density = probe_rows(key_rows, probe_vectors, probe_index, probe_count, probe_in, probe_mid)
    return (own_rows, density)


def solution(mesh):
    in_specs = (
        P(("gx", "gy", "gz"), None),
        P(("gx", "gy", "gz")),
        P(None, None, None, ("gx", "gy", "gz")),
        P(None, ("gx", "gy", "gz")),
        P(("gx", "gy", "gz")),
        P(None, None, ("gx", "gy", "gz")),
        P(),
        P(),
        P(),
        P(),
        P(),
        P(),
        P(),
        P(),
        P(),
        P(None, None, ("gx", "gy", "gz")),
        P(None, ("gx", "gy", "gz")),
        P(("gx", "gy", "gz")),
        P(),
    )
    out_specs = (P(("gx", "gy", "gz"), None), P(("gx", "gy", "gz")))
    return jax.shard_map(local, mesh=mesh, in_specs=in_specs, out_specs=out_specs, check_vma=False)
```

profile of v0, /device:TPU:1, one launch (start us, length us, event | category | flops | bytes accessed | tf_op | source)
XLA Modules:
  0.0 823.7 jit_solution(10982440180964982035)
XLA Ops:
  25.2 8.2 collective-permute-start.3
  37.3 7.0 collective-permute-start.4
  44.5 9.9 %collective-permute-done.4 = bf16[4,4,1,8,1536]{4,3,2,1,0:T(8,128)(2,1)S(1)} collective-permute-done((bf16[4,4,1,8,1536]{4,3,2,1,0:T(8,128)(2,1)S(1)}, bf16[4,4,1,8,1536]{4,3,2,1,0:T(8,128)(2,1)S(1)}, u32[]{:S(2)}, u32[]{:S(2)}) %collective-permute-start.4) | collective-permute-done | bytes 393248 | tf_op jit(solution)/shard_map/ppermute | solution.py:30
  56.4 166.6 %while.56 = (s32[]{:T(128)}, bf16[4,32,1536]{2,1,0:T(8,128)(2,1)}, bf16[4,32,1536]{2,1,0:T(8,128)(2,1)}, f32[4,3,32,32]{2,3,1,0:T(8,128)S(1)}, bf16[8,64]{1,0:T(...) while((s32[]{:T(128)}, bf16[4,32,1536]{2,1,0:T(8,128)(2,1)}, ...), condition=%wide.region_2.5_spmd.clone, body=%wide.region_0.4_spmd.clone.sunk | while | flops 81860392 | bytes 59827252 | solution.py:159
  65.9 5.6 gather_fusion.1
  75.4 7.8 reshape.2988
  107.6 5.6 gather_fusion.1
  117.1 7.8 reshape.2988
  149.2 5.6 gather_fusion.1
  158.8 7.8 reshape.2988
  190.9 5.6 gather_fusion.1
  200.4 7.8 reshape.2988
  230.4 7.5 collective-permute-start.9
  237.9 8.6 %collective-permute-done.8 = bf16[4,1,2,8,1536]{4,3,2,1,0:T(8,128)(2,1)S(1)} collective-permute-done((bf16[4,1,2,8,1536]{4,3,2,1,0:T(8,128)(2,1)S(1)}, bf16[4,1,2,8,1536]{4,3,2,1,0:T(8,128)(2,1)S(1)}, u32[]{:S(2)}, u32[]{:S(2)}) %collective-permute-start.8) | collective-permute-done | bytes 196640 | tf_op jit(solution)/shard_map/ppermute | solution.py:30
  249.1 4.7 collective-permute-done.10
  253.8 6.6 collective-permute-done.11
  261.2 171.7 %while.57 = (s32[]{:T(128)}, bf16[4,32,1536]{2,1,0:T(8,128)(2,1)}, bf16[4,32,1536]{2,1,0:T(8,128)(2,1)}, f32[4,3,32,32]{2,3,1,0:T(8,128)S(1)}, bf16[8,64]{1,0:T(...) while((s32[]{:T(128)}, bf16[4,32,1536]{2,1,0:T(8,128)(2,1)}, ...), condition=%wide.region_5.8_spmd.clone, body=%wide.region_3.7_spmd.clone.sunk | while | flops 81860392 | bytes 59727812 | solution.py:159
  272.1 5.6 gather_fusion.2
  281.6 7.8 reshape.2994
  315.0 5.6 gather_fusion.2
  324.5 7.8 reshape.2994
  357.9 5.6 gather_fusion.2
  367.4 7.8 reshape.2994
  400.8 5.6 gather_fusion.2
  410.4 7.8 reshape.2994
  440.8 7.6 collective-permute-start.15
  448.4 6.7 collective-permute-done.14
  457.5 5.9 collective-permute-done.16
  463.4 5.4 collective-permute-done.17
  469.6 171.8 %while.58 = (s32[]{:T(128)}, bf16[4,32,1536]{2,1,0:T(8,128)(2,1)}, bf16[4,32,1536]{2,1,0:T(8,128)(2,1)}, f32[4,3,32,32]{2,3,1,0:T(8,128)S(1)}, bf16[8,64]{1,0:T(...) while((s32[]{:T(128)}, bf16[4,32,1536]{2,1,0:T(8,128)(2,1)}, ...), condition=%wide.region_8.11_spmd.clone, body=%wide.region_6.10_spmd.clone.sunk | while | flops 81860392 | bytes 59727812 | solution.py:159
  480.5 5.6 gather_fusion.3
  490.0 7.8 reshape.3000
  523.4 5.6 gather_fusion.3
  533.0 7.8 reshape.3000
  566.4 5.6 gather_fusion.3
  575.9 7.8 reshape.3000
  609.3 5.6 gather_fusion.3
  618.8 7.8 reshape.3000
  649.4 7.5 collective-permute-start.21
  656.9 7.1 collective-permute-done.20
  673.5 4.2 collective-permute-done.23
  684.5 71.6 %all-reduce.2.cloned.1.call-done = bf16[320,1024]{1,0:T(8,128)(2,1)} async-done(((bf16[320,1024]{1,0:T(8,128)(2,1)}), bf16[320,1024]{1,0:T(8,128)(2,1)}) %all-reduce.2.cloned.1.call-update) | async-done | bytes 655376 | tf_op jit(solution)/shard_map/psum | solution.py:40
  756.1 59.9 %while.55 = (s32[]{:T(128)}, f32[4,32]{1,0:T(4,128)S(1)}, s32[4,32]{1,0:T(4,128)S(1)}, s32[4,32,32]{2,0,1:T(4,128)S(1)}, bf16[320,1024]{1,0:T(8,128)(2,1)}, /*in...) while((s32[]{:T(128)}, f32[4,32]{1,0:T(4,128)S(1)}, ...), condition=%wide.region_14.17_spmd, body=%wide.region_10.16_spmd.sunk | while | flops 13404170 | bytes 15143149 | solution.py:219
  757.9 4.1 gather_fusion
  766.0 4.6 fusion.279
  781.0 4.6 fusion.279
  795.9 4.6 fusion.279
  810.9 4.6 fusion.279
  (1140 shorter events, 451.7 us)
Async XLA Ops:
  7.2 658.8 %copy-start = (bf16[4,96,64]{1,2,0:T(8,128)(2,1)S(1)}, bf16[4,96,64]{1,2,0:T(8,128)(2,1)}, u32[]{:S(2)}) copy-start(bf16[4,96,64]{1,2,0:T(8,128)(2,1)} %param.50) | copy-start | bytes 147460
  7.2 11.0 %copy-start.43 = (s32[16]{0:T(128)S(1)}, s32[16]{0:T(128)}, u32[]{:S(2)}) copy-start(s32[16]{0:T(128)} %constant.656) | copy-start | bytes 196
  7.3 10.1 %copy-start.37 = (bf16[3,8,64]{2,1,0:T(8,128)(2,1)S(1)}, bf16[3,8,64]{2,1,0:T(8,128)(2,1)}, u32[]{:S(2)}) copy-start(bf16[3,8,64]{2,1,0:T(8,128)(2,1)} %param.42) | copy-start | bytes 9220
  7.3 10.7 %copy-start.40 = (s32[128]{0:T(128)S(1)}, s32[128]{0:T(128)}, u32[]{:S(2)}) copy-start(s32[128]{0:T(128)} %param.37) | copy-start | bytes 1540
  7.3 10.8 %copy-start.41 = (s32[128]{0:T(128)S(1)}, s32[128]{0:T(128)}, u32[]{:S(2)}) copy-start(s32[128]{0:T(128)} %param.40) | copy-start | bytes 1540
  7.3 748.8 %all-reduce.2.cloned.1.call-start = ((), (), s32[]{:S(2)}) async-start(), calls=%async_computation | async-start | bytes 1310720 | tf_op jit(solution)/shard_map/psum | solution.py:40
  10.4 13.3 %collective-permute-start = (bf16[1,2,2,8,1536]{4,3,2,1,0:T(8,128)(2,1)S(1)}, bf16[1,2,2,8,1536]{4,3,2,1,0:T(8,128)(2,1)S(1)}, u32[]{:S(2)}, u32[]{:S(2)}) collective-permute-start(bf16[1,2,2,8,1536]{4,3,2,1,0:T(8,128)(2,1)S(1)} %bitcast.1357), channel_id=1, source_target_pairs={{0,64},{64,128},{128,192},{192,0},{1,65},{65,129},{129,193},{193,1... | collective-permute-start | bytes 294920 | tf_op jit(solution)/shard_map/ppermute | solution.py:30
  12.5 11.2 %collective-permute-start.1 = (bf16[1,2,2,8,1536]{4,3,2,1,0:T(8,128)(2,1)S(1)}, bf16[1,2,2,8,1536]{4,3,2,1,0:T(8,128)(2,1)S(1)}, u32[]{:S(2)}, u32[]{:S(2)}) collective-permute-start(bf16[1,2,2,8,1536]{4,3,2,1,0:T(8,128)(2,1)S(1)} %bitcast.1356), channel_id=1, source_target_pairs={{64,0},{128,64},{192,128},{0,192},{65,1},{129,65},{193,129},{1,193... | collective-permute-start | bytes 294920 | tf_op jit(solution)/shard_map/ppermute | solution.py:33
  18.2 19.2 %copy-start.36 = (s32[1024]{0:T(1024)}, s32[1024]{0:T(1024)S(1)}, u32[]{:S(2)}) copy-start(s32[1024]{0:T(1024)S(1)} %pad_clamp_fusion) | copy-start | bytes 12292
  23.8 13.4 %collective-permute-start.2 = (bf16[4,1,2,8,1536]{4,3,2,1,0:T(8,128)(2,1)S(1)}, bf16[4,1,2,8,1536]{4,3,2,1,0:T(8,128)(2,1)S(1)}, u32[]{:S(2)}, u32[]{:S(2)}) collective-permute-start(bf16[4,1,2,8,1536]{4,3,2,1,0:T(8,128)(2,1)S(1)} %get-tuple-element.1375), channel_id=1, source_target_pairs={{0,8},{8,16},{16,24},{24,32},{32,40},{40,48},{48,56},{56,0},{1,9},... | collective-permute-start | bytes 589832 | tf_op jit(solution)/shard_map/ppermute | solution.py:30
  25.2 11.9 %collective-permute-start.3 = (bf16[4,1,2,8,1536]{4,3,2,1,0:T(8,128)(2,1)S(1)}, bf16[4,1,2,8,1536]{4,3,2,1,0:T(8,128)(2,1)S(1)}, u32[]{:S(2)}, u32[]{:S(2)}) collective-permute-start(bf16[4,1,2,8,1536]{4,3,2,1,0:T(8,128)(2,1)S(1)} %get-tuple-element.1374), channel_id=1, source_target_pairs={{8,0},{16,8},{24,16},{32,24},{40,32},{48,40},{56,48},{0,56},{9,1},... | collective-permute-start | bytes 589832 | tf_op jit(solution)/shard_map/ppermute | solution.py:33
  37.3 17.2 %collective-permute-start.4 = (bf16[4,4,1,8,1536]{4,3,2,1,0:T(8,128)(2,1)S(1)}, bf16[4,4,1,8,1536]{4,3,2,1,0:T(8,128)(2,1)S(1)}, u32[]{:S(2)}, u32[]{:S(2)}) collective-permute-start(bf16[4,4,1,8,1536]{4,3,2,1,0:T(8,128)(2,1)S(1)} %get-tuple-element.1367), channel_id=1, source_target_pairs={{0,1},{1,2},{2,3},{3,4},{4,5},{5,6},{6,7},{7,0},{8,9},{9,10},{10,1... | collective-permute-start | bytes 1179656 | tf_op jit(solution)/shard_map/ppermute | solution.py:30
  44.3 11.3 %collective-permute-start.5 = (bf16[4,4,1,8,1536]{4,3,2,1,0:T(8,128)(2,1)S(1)}, bf16[4,4,1,8,1536]{4,3,2,1,0:T(8,128)(2,1)S(1)}, u32[]{:S(2)}, u32[]{:S(2)}) collective-permute-start(bf16[4,4,1,8,1536]{4,3,2,1,0:T(8,128)(2,1)S(1)} %get-tuple-element.1366), channel_id=1, source_target_pairs={{1,0},{2,1},{3,2},{4,3},{5,4},{6,5},{7,6},{0,7},{9,8},{10,9},{11,1... | collective-permute-start | bytes 1179656 | tf_op jit(solution)/shard_map/ppermute | solution.py:33
  75.4 10.0 %copy-start.11 = (f32[32,32,1,96]{3,2,1,0:T(1,128)S(1)}, f32[32,32,1,96]{3,2,1,0:T(1,128)}, u32[]{:S(2)}) copy-start(f32[32,32,1,96]{3,2,1,0:T(1,128)} %get-tuple-element.1763) | copy-start | bytes 1179652 | tf_op jit(solution)/shard_map/while
  117.1 10.0 %copy-start.11 = (f32[32,32,1,96]{3,2,1,0:T(1,128)S(1)}, f32[32,32,1,96]{3,2,1,0:T(1,128)}, u32[]{:S(2)}) copy-start(f32[32,32,1,96]{3,2,1,0:T(1,128)} %get-tuple-element.1763) | copy-start | bytes 1179652 | tf_op jit(solution)/shard_map/while
  158.8 10.0 %copy-start.11 = (f32[32,32,1,96]{3,2,1,0:T(1,128)S(1)}, f32[32,32,1,96]{3,2,1,0:T(1,128)}, u32[]{:S(2)}) copy-start(f32[32,32,1,96]{3,2,1,0:T(1,128)} %get-tuple-element.1763) | copy-start | bytes 1179652 | tf_op jit(solution)/shard_map/while
  200.4 10.0 %copy-start.11 = (f32[32,32,1,96]{3,2,1,0:T(1,128)S(1)}, f32[32,32,1,96]{3,2,1,0:T(1,128)}, u32[]{:S(2)}) copy-start(f32[32,32,1,96]{3,2,1,0:T(1,128)} %get-tuple-element.1763) | copy-start | bytes 1179652 | tf_op jit(solution)/shard_map/while
  225.1 5.2 collective-permute-start.6
  225.2 5.1 collective-permute-start.7
  230.3 16.2 %collective-permute-start.8 = (bf16[4,1,2,8,1536]{4,3,2,1,0:T(8,128)(2,1)S(1)}, bf16[4,1,2,8,1536]{4,3,2,1,0:T(8,128)(2,1)S(1)}, u32[]{:S(2)}, u32[]{:S(2)}) collective-permute-start(bf16[4,1,2,8,1536]{4,3,2,1,0:T(8,128)(2,1)S(1)} %get-tuple-element.1373), channel_id=1, source_target_pairs={{0,8},{8,16},{16,24},{24,32},{32,40},{40,48},{48,56},{56,0},{1,9},... | collective-permute-start | bytes 589832 | tf_op jit(solution)/shard_map/ppermute | solution.py:30
  230.4 16.1 %collective-permute-start.9 = (bf16[4,1,2,8,1536]{4,3,2,1,0:T(8,128)(2,1)S(1)}, bf16[4,1,2,8,1536]{4,3,2,1,0:T(8,128)(2,1)S(1)}, u32[]{:S(2)}, u32[]{:S(2)}) collective-permute-start(bf16[4,1,2,8,1536]{4,3,2,1,0:T(8,128)(2,1)S(1)} %get-tuple-element.1372), channel_id=1, source_target_pairs={{8,0},{16,8},{24,16},{32,24},{40,32},{48,40},{56,48},{0,56},{9,1},... | collective-permute-start | bytes 589832 | tf_op jit(solution)/shard_map/ppermute | solution.py:33
  246.7 7.1 collective-permute-start.10
  248.6 11.8 %collective-permute-start.11 = (bf16[4,4,1,8,1536]{4,3,2,1,0:T(8,128)(2,1)S(1)}, bf16[4,4,1,8,1536]{4,3,2,1,0:T(8,128)(2,1)S(1)}, u32[]{:S(2)}, u32[]{:S(2)}) collective-permute-start(bf16[4,4,1,8,1536]{4,3,2,1,0:T(8,128)(2,1)S(1)} %get-tuple-element.1364), channel_id=1, source_target_pairs={{1,0},{2,1},{3,2},{4,3},{5,4},{6,5},{7,6},{0,7},{9,8},{10,9},{11,1... | collective-permute-start | bytes 1179656 | tf_op jit(solution)/shard_map/ppermute | solution.py:33
  281.6 10.0 %copy-start.12 = (f32[32,32,1,96]{3,2,1,0:T(1,128)S(1)}, f32[32,32,1,96]{3,2,1,0:T(1,128)}, u32[]{:S(2)}) copy-start(f32[32,32,1,96]{3,2,1,0:T(1,128)} %get-tuple-element.1801) | copy-start | bytes 1179652 | tf_op jit(solution)/shard_map/while
  324.5 10.0 %copy-start.12 = (f32[32,32,1,96]{3,2,1,0:T(1,128)S(1)}, f32[32,32,1,96]{3,2,1,0:T(1,128)}, u32[]{:S(2)}) copy-start(f32[32,32,1,96]{3,2,1,0:T(1,128)} %get-tuple-element.1801) | copy-start | bytes 1179652 | tf_op jit(solution)/shard_map/while
  367.4 10.0 %copy-start.12 = (f32[32,32,1,96]{3,2,1,0:T(1,128)S(1)}, f32[32,32,1,96]{3,2,1,0:T(1,128)}, u32[]{:S(2)}) copy-start(f32[32,32,1,96]{3,2,1,0:T(1,128)} %get-tuple-element.1801) | copy-start | bytes 1179652 | tf_op jit(solution)/shard_map/while
  410.4 10.0 %copy-start.12 = (f32[32,32,1,96]{3,2,1,0:T(1,128)S(1)}, f32[32,32,1,96]{3,2,1,0:T(1,128)}, u32[]{:S(2)}) copy-start(f32[32,32,1,96]{3,2,1,0:T(1,128)} %get-tuple-element.1801) | copy-start | bytes 1179652 | tf_op jit(solution)/shard_map/while
  435.0 5.6 collective-permute-start.12
  435.4 5.2 collective-permute-start.13
  440.6 29.0 %copy-start.24 = (bf16[64,384]{1,0:T(8,128)(2,1)S(1)}, bf16[64,384]{1,0:T(8,128)(2,1)}, u32[]{:S(2)}) copy-start(bf16[64,384]{1,0:T(8,128)(2,1)} %get-tuple-element.1970) | copy-start | bytes 147460
  440.7 14.5 %collective-permute-start.14 = (bf16[4,1,2,8,1536]{4,3,2,1,0:T(8,128)(2,1)S(1)}, bf16[4,1,2,8,1536]{4,3,2,1,0:T(8,128)(2,1)S(1)}, u32[]{:S(2)}, u32[]{:S(2)}) collective-permute-start(bf16[4,1,2,8,1536]{4,3,2,1,0:T(8,128)(2,1)S(1)} %get-tuple-element.1371), channel_id=1, source_target_pairs={{0,8},{8,16},{16,24},{24,32},{32,40},{40,48},{48,56},{56,0},{1,9},... | collective-permute-start | bytes 589832 | tf_op jit(solution)/shard_map/ppermute | solution.py:30
  440.8 14.4 %collective-permute-start.15 = (bf16[4,1,2,8,1536]{4,3,2,1,0:T(8,128)(2,1)S(1)}, bf16[4,1,2,8,1536]{4,3,2,1,0:T(8,128)(2,1)S(1)}, u32[]{:S(2)}, u32[]{:S(2)}) collective-permute-start(bf16[4,1,2,8,1536]{4,3,2,1,0:T(8,128)(2,1)S(1)} %get-tuple-element.1370), channel_id=1, source_target_pairs={{8,0},{16,8},{24,16},{32,24},{40,32},{48,40},{56,48},{0,56},{9,1},... | collective-permute-start | bytes 589832 | tf_op jit(solution)/shard_map/ppermute | solution.py:33
  455.3 8.1 collective-permute-start.16
  457.4 11.4 %collective-permute-start.17 = (bf16[4,4,1,8,1536]{4,3,2,1,0:T(8,128)(2,1)S(1)}, bf16[4,4,1,8,1536]{4,3,2,1,0:T(8,128)(2,1)S(1)}, u32[]{:S(2)}, u32[]{:S(2)}) collective-permute-start(bf16[4,4,1,8,1536]{4,3,2,1,0:T(8,128)(2,1)S(1)} %get-tuple-element.1362), channel_id=1, source_target_pairs={{1,0},{2,1},{3,2},{4,3},{5,4},{6,5},{7,6},{0,7},{9,8},{10,9},{11,1... | collective-permute-start | bytes 1179656 | tf_op jit(solution)/shard_map/ppermute | solution.py:33
  490.0 10.0 %copy-start.13 = (f32[32,32,1,96]{3,2,1,0:T(1,128)S(1)}, f32[32,32,1,96]{3,2,1,0:T(1,128)}, u32[]{:S(2)}) copy-start(f32[32,32,1,96]{3,2,1,0:T(1,128)} %get-tuple-element.1839) | copy-start | bytes 1179652 | tf_op jit(solution)/shard_map/while
  532.9 10.0 %copy-start.13 = (f32[32,32,1,96]{3,2,1,0:T(1,128)S(1)}, f32[32,32,1,96]{3,2,1,0:T(1,128)}, u32[]{:S(2)}) copy-start(f32[32,32,1,96]{3,2,1,0:T(1,128)} %get-tuple-element.1839) | copy-start | bytes 1179652 | tf_op jit(solution)/shard_map/while
  575.9 10.0 %copy-start.13 = (f32[32,32,1,96]{3,2,1,0:T(1,128)S(1)}, f32[32,32,1,96]{3,2,1,0:T(1,128)}, u32[]{:S(2)}) copy-start(f32[32,32,1,96]{3,2,1,0:T(1,128)} %get-tuple-element.1839) | copy-start | bytes 1179652 | tf_op jit(solution)/shard_map/while
  618.8 10.0 %copy-start.13 = (f32[32,32,1,96]{3,2,1,0:T(1,128)S(1)}, f32[32,32,1,96]{3,2,1,0:T(1,128)}, u32[]{:S(2)}) copy-start(f32[32,32,1,96]{3,2,1,0:T(1,128)} %get-tuple-element.1839) | copy-start | bytes 1179652 | tf_op jit(solution)/shard_map/while
  643.4 23.3 %copy-start.46 = (s32[32]{0:T(128)S(1)}, s32[32]{0:T(128)}, u32[]{:S(2)}) copy-start(s32[32]{0:T(128)} %param.54) | copy-start | bytes 388
  643.5 24.5 %copy-start.20 = (bf16[4,32,1536]{2,1,0:T(8,128)(2,1)S(1)}, bf16[4,32,1536]{2,1,0:T(8,128)(2,1)}, u32[]{:S(2)}) copy-start(bf16[4,32,1536]{2,1,0:T(8,128)(2,1)} %get-tuple-element.944) | copy-start | bytes 1179652
  643.5 5.7 collective-permute-start.18
  644.9 4.4 collective-permute-start.19
  649.3 14.7 %collective-permute-start.20 = (bf16[4,1,2,8,1536]{4,3,1,0,2:T(8,128)(2,1)S(1)}, bf16[4,1,2,8,1536]{4,3,1,0,2:T(8,128)(2,1)S(1)}, u32[]{:S(2)}, u32[]{:S(2)}) collective-permute-start(bf16[4,1,2,8,1536]{4,3,1,0,2:T(8,128)(2,1)S(1)} %get-tuple-element.1369), channel_id=1, source_target_pairs={{0,8},{8,16},{16,24},{24,32},{32,40},{40,48},{48,56},{56,0},{1,9},... | collective-permute-start | bytes 589832 | tf_op jit(solution)/shard_map/ppermute | solution.py:30
  649.4 14.6 %collective-permute-start.21 = (bf16[4,1,2,8,1536]{4,3,1,0,2:T(8,128)(2,1)S(1)}, bf16[4,1,2,8,1536]{4,3,1,0,2:T(8,128)(2,1)S(1)}, u32[]{:S(2)}, u32[]{:S(2)}) collective-permute-start(bf16[4,1,2,8,1536]{4,3,1,0,2:T(8,128)(2,1)S(1)} %get-tuple-element.1368), channel_id=1, source_target_pairs={{8,0},{16,8},{24,16},{32,24},{40,32},{48,40},{56,48},{0,56},{9,1},... | collective-permute-start | bytes 589832 | tf_op jit(solution)/shard_map/ppermute | solution.py:33
  665.1 6.4 collective-permute-start.22
  666.0 11.7 %collective-permute-start.23 = (bf16[4,4,1,8,1536]{4,3,1,0,2:T(8,128)(2,1)}, bf16[4,4,1,8,1536]{4,3,1,0,2:T(8,128)(2,1)}, u32[]{:S(2)}, u32[]{:S(2)}) collective-permute-start(bf16[4,4,1,8,1536]{4,3,1,0,2:T(8,128)(2,1)} %get-tuple-element.1360), channel_id=1, source_target_pairs={{1,0},{2,1},{3,2},{4,3},{5,4},{6,5},{7,6},{0,7},{9,8},{10,9},{11,1... | collective-permute-start | bytes 1179656 | tf_op jit(solution)/shard_map/ppermute | solution.py:33
  682.5 73.6 %copy-start.44 = (bf16[64,64]{1,0:T(8,128)(2,1)S(1)}, bf16[64,64]{1,0:T(8,128)(2,1)}, u32[]{:S(2)}) copy-start(bf16[64,64]{1,0:T(8,128)(2,1)} %param.49) | copy-start | bytes 24580
  682.5 73.6 %copy-start.45 = (bf16[8,64]{1,0:T(8,128)(2,1)S(1)}, bf16[8,64]{1,0:T(8,128)(2,1)}, u32[]{:S(2)}) copy-start(bf16[8,64]{1,0:T(8,128)(2,1)} %param.48) | copy-start | bytes 3076
  (106 other events, 586.6 us)
Sparse Core Ops, SparseCore 0:
  684.2 71.8 all-reduce.1
where the time goes:
time: 836 us; the launch traced here: 824 us
  local copies, waits for them, and re-layouts  345 us (41%)
  other arithmetic  162 us (19%)
  waiting for transfers between devices  142 us (17%)
  matrix products  97.7 us (12%)
  starting transfers between devices  57.3 us (7%)
  between operations  15.8 us (2%)
    reshape x12, local copies, waits for them, and re-layouts, update_one_block(): jnp.take(table_rows, index_part, axis=0)  93.8 us
    dot_general x48, other arithmetic, degree_messages(): jnp.einsum('krmc,krc->rmc', segment, weight_here, preferred_element_type=...  83.1 us
    psum x1, waiting for transfers between devices, spread(): return lax.psum(block, axis)  71.6 us
    gather x12, local copies, waits for them, and re-layouts, update_one_block(): jnp.take(table_rows, index_part, axis=0)  67.3 us
    ppermute x12, waiting for transfers between devices, with_halo(): lax.ppermute(lax.slice_in_dim(block, block.shape[dim] - width, None, axis...  53 us
    select_n x12, other arithmetic, update_one_block(): jnp.take(table_rows, index_part, axis=0)  47 us
    slice x12, local copies, waits for them, and re-layouts, degree_messages(): weight_here = radial4[:, :, degree, :]  41.3 us
    ppermute x12, starting transfers between devices, with_halo(): lax.ppermute(lax.slice_in_dim(block, 0, width, axis=dim), axis, backward)  39.7 us
  transfers between devices with their start and end apart: 25, of which 17 were waited for; matrix products, arithmetic and copies ran while one was open for 2% of the time, Pallas kernels for 0%

commit v1 on v0

v1 whole, which is shorter than its diff:
```python
import functools
import math

import jax
import jax.numpy as jnp
import numpy as np
from jax import lax
from jax.experimental import pallas as pl
from jax.experimental.pallas import tpu as pltpu
from jax.sharding import PartitionSpec as P

C = 96
COMPS = 16
WIDTH = C * COMPS
RH = 64
NB = 8
K = 32
LAYERS = 3
ATOMS = 128
FACE = 32
GHOSTS = 192
TABLE = 320
HALF = 64
CUTOFF = 4.0
DEGREE = (0, 1, 1, 1, 2, 2, 2, 2, 2, 3, 3, 3, 3, 3, 3, 3)
STARTS = (0, 1, 4, 9)
WIDTHS = (1, 3, 5, 7)
STEP = 2
PAIRS = K // (2 * STEP)
WIDE = 4
STEPS = K // WIDE
ENV_ROW = 16
BASIS_ROW = 24
GEO_ROWS = 32

VMEM_LIMIT = 24 * 1024 * 1024

f32 = jnp.float32
bf16 = jnp.bfloat16


def dot(a, b):
    return lax.dot_general(a, b, (((1,), (0,)), ((), ())), preferred_element_type=f32)


def dot_tn(a, b):
    return lax.dot_general(a, b, (((0,), (0,)), ((), ())), preferred_element_type=f32)


def dot_nt(a, b):
    return lax.dot_general(a, b, (((1,), (1,)), ((), ())), preferred_element_type=f32)


def sigmoid(u):
    return 0.5 * jnp.tanh(0.5 * u) + 0.5


def silu(u):
    half = 0.5 * u
    return half * jnp.tanh(half) + half


def harmonics(vx, vy, vz):
    x = vx * 0.5
    y = vy * 0.5
    z = vz * 0.5
    q = x * x + y * y + z * z
    zz = 5.0 * z * z - q
    return [
        jnp.ones_like(x),
        math.sqrt(3.0) * x,
        math.sqrt(3.0) * y,
        math.sqrt(3.0) * z,
        math.sqrt(15.0) * x * y,
        math.sqrt(15.0) * y * z,
        math.sqrt(5.0) / 2.0 * (3.0 * z * z - q),
        math.sqrt(15.0) * x * z,
        math.sqrt(15.0) / 2.0 * (x * x - y * y),
        math.sqrt(35.0 / 8.0) * y * (3.0 * x * x - y * y),
        math.sqrt(105.0) * x * y * z,
        math.sqrt(21.0 / 8.0) * y * zz,
        math.sqrt(7.0) / 2.0 * z * (5.0 * z * z - 3.0 * q),
        math.sqrt(21.0 / 8.0) * x * zz,
        math.sqrt(105.0) / 2.0 * z * (x * x - y * y),
        math.sqrt(35.0 / 8.0) * x * (x * x - 3.0 * y * y),
    ]


def params(semantics=None):
    return pltpu.CompilerParams(vmem_limit_bytes=VMEM_LIMIT, dimension_semantics=semantics)


def whole(*shape):
    return pl.BlockSpec(shape, lambda i: (0,) * len(shape))


def layer_block(t, *shape):
    return pl.BlockSpec((None,) + shape, lambda i: (t,) + (0,) * len(shape))


def slots(*shape):
    return pl.BlockSpec((WIDE,) + shape, lambda i: (i,) + (0,) * len(shape))


def pick_kernel(lists_ref, rows_ref, sel_ref, *out_refs):
    lists = jnp.concatenate(
        [lists_ref[i, j, k : k + 1, :] for i in (0, 1) for j in (0, 1) for k in (0, 1)], axis=0
    )
    entry = lax.broadcasted_iota(jnp.int32, (8, GHOSTS), 0)
    lane = lax.broadcasted_iota(jnp.int32, (8, GHOSTS), 1)
    spread = dot(lists.astype(f32).astype(bf16), (entry == lane % 8).astype(f32).astype(bf16))
    face, quarter = lane // FACE, (lane // 8) % 4
    side = 1 - face % 2
    high, low = quarter // 2, quarter % 2
    octant = jnp.where(
        face < 2, 4 * side + quarter, jnp.where(face < 4, 4 * high + 2 * side + low, 2 * quarter + side)
    )
    chosen = jnp.sum(jnp.where(entry == octant, spread, 0.0), axis=0, keepdims=True)
    atom = lax.broadcasted_iota(jnp.int32, (ATOMS, GHOSTS), 0)
    turned_sel = (atom == chosen.astype(jnp.int32)).astype(f32)
    sel = turned_sel.T.astype(bf16)
    sel_ref[...] = sel
    picked = dot(sel, rows_ref[...]).astype(bf16)
    for number, out_ref in enumerate(out_refs):
        out_ref[...] = picked[number * FACE : (number + 1) * FACE]


def pick(lists, rows):
    return pl.pallas_call(
        pick_kernel,
        grid=(1,),
        in_specs=[whole(2, 2, 2, 8), whole(ATOMS, WIDTH)],
        out_specs=[whole(GHOSTS, ATOMS)] + [whole(FACE, WIDTH)] * 6,
        out_shape=[jax.ShapeDtypeStruct((GHOSTS, ATOMS), bf16)]
        + [jax.ShapeDtypeStruct((FACE, WIDTH), bf16)] * 6,
        compiler_params=params(),
        name="pick",
    )(lists, rows)


def geometry_into(vec_ref, count_ref, geo_ref):
    sharpness = ((NB - 1) / CUTOFF) ** 2
    centers = lax.broadcasted_iota(jnp.int32, (NB, ATOMS), 0).astype(f32) * (CUTOFF / (NB - 1))

    def one_slot(k, carry):
        vx = vec_ref[0, pl.ds(k, 1), :]
        vy = vec_ref[1, pl.ds(k, 1), :]
        vz = vec_ref[2, pl.ds(k, 1), :]
        square = vx * vx + vy * vy + vz * vz
        shape = 1.0 - square / (CUTOFF * CUTOFF)
        valid = (k < count_ref[...]).astype(f32)
        envelope = shape * shape * valid * (K ** (-0.5))
        radius = jnp.sqrt(square)
        offset = radius - centers
        for m, value in enumerate(harmonics(vx, vy, vz)):
            geo_ref[k, m : m + 1, :] = value
        geo_ref[k, ENV_ROW:BASIS_ROW, :] = jnp.broadcast_to(envelope, (8, ATOMS))
        geo_ref[k, BASIS_ROW:GEO_ROWS, :] = jnp.exp(-sharpness * offset * offset)
        return carry

    lax.fori_loop(0, K, one_slot, 0, unroll=4)


def prepare_kernel(rows_ref, avec_ref, acount_ref, pvec_ref, pcount_ref, turned_ref, ageo_ref, pgeo_ref):
    turned_ref[...] = rows_ref[...].astype(f32).T.astype(bf16)
    geometry_into(avec_ref, acount_ref, ageo_ref)
    geometry_into(pvec_ref, pcount_ref, pgeo_ref)


def prepare(rows, avec, acount, pvec, pcount):
    geo = jax.ShapeDtypeStruct((K, GEO_ROWS, ATOMS), f32)
    return pl.pallas_call(
        prepare_kernel,
        grid=(1,),
        in_specs=[
            whole(ATOMS, WIDTH),
            whole(3, K, ATOMS),
            whole(1, ATOMS),
            whole(3, K, ATOMS),
            whole(1, ATOMS),
        ],
        out_specs=[whole(WIDTH, ATOMS), whole(K, GEO_ROWS, ATOMS), whole(K, GEO_ROWS, ATOMS)],
        out_shape=[jax.ShapeDtypeStruct((WIDTH, ATOMS), bf16), geo, geo],
        compiler_params=params(),
        cost_estimate=pl.CostEstimate(flops=10_000_000, bytes_accessed=3_000_000, transcendentals=100_000),
        name="prepare",
    )(rows, avec, acount, pvec, pcount)


def hidden_kernel(species_ref, geo_ref, win_ref, wemb_ref, wmid_ref, out_ref):
    ids = lax.broadcasted_iota(jnp.int32, (wemb_ref.shape[1], ATOMS), 0)
    emb = dot(wemb_ref[...], (ids == species_ref[...]).astype(f32).astype(bf16))
    for k in range(0, K, 8):
        basis = jnp.concatenate([geo_ref[k + s, BASIS_ROW:GEO_ROWS, :] for s in range(8)], axis=1)
        hidden = dot_tn(win_ref[...], basis.astype(bf16)) + jnp.concatenate([emb] * 8, axis=1)
        hidden = silu(hidden).astype(bf16)
        hidden = silu(dot_tn(wmid_ref[...], hidden)).astype(bf16)
        for s in range(8):
            out_ref[k + s] = hidden[:, s * ATOMS : (s + 1) * ATOMS]


def hidden_units(t, species, geo, radial_in, species_emb, radial_mid):
    return pl.pallas_call(
        hidden_kernel,
        grid=(1,),
        in_specs=[
            whole(1, ATOMS),
            whole(K, GEO_ROWS, ATOMS),
            layer_block(t, NB, RH),
            layer_block(t, RH, species_emb.shape[2]),
            layer_block(t, RH, RH),
        ],
        out_specs=whole(K, RH, ATOMS),
        out_shape=jax.ShapeDtypeStruct((K, RH, ATOMS), bf16),
        compiler_params=params(),
        cost_estimate=pl.CostEstimate(
            flops=2 * 4096 * 256 * RH * 2, bytes_accessed=2_000_000, transcendentals=600_000
        ),
        name="hidden_units",
    )(species, geo, radial_in, species_emb, radial_mid)


def layer_kernel(last, *refs):
    (idx_ref, geo_ref, hidden_ref, turned_ref, sel_ref, wout_ref, mix_ref, gate_ref, proj_ref) = refs[:9]
    ghost_refs = refs[9:15]
    out_refs = refs[15:-5]
    table_ref, acc_ref, even_ref, odd_ref, rad_ref = refs[-5:]

    table_ref[:, :ATOMS] = turned_ref[...]
    rows = jnp.concatenate([ref[...] for ref in ghost_refs], axis=0)
    table_ref[:, ATOMS:] = rows.astype(f32).T.astype(bf16)

    def front(first, got_ref, slot):
        hidden = jnp.concatenate([hidden_ref[first + s] for s in range(STEP)], axis=1)
        envelope = jnp.concatenate(
            [geo_ref[first + s, ENV_ROW : ENV_ROW + 1, :] for s in range(STEP)], axis=1
        )
        rad_ref[slot] = dot_tn(wout_ref[...], hidden) * envelope
        ids = lax.broadcasted_iota(jnp.int32, (TABLE, ATOMS), 0)
        hot = jnp.concatenate(
            [
                (ids == idx_ref[pl.ds(first + s, 1), :]).astype(f32).astype(bf16)
                for s in range(STEP)
            ],
            axis=1,
        )
        got_ref[...] = dot(table_ref[...], hot)

    def back(first, got_ref, slot, keep):
        for tile in range(0, C, 8):
            scalar = []
            weight = []
            for s in range(STEP):
                lanes = slice(s * ATOMS, (s + 1) * ATOMS)
                scalar.append(got_ref[tile : tile + 8, lanes])
                weight.append(
                    [rad_ref[slot, l * C + tile : l * C + tile + 8, lanes] for l in range(4)]
                )
            for m in range(COMPS):
                at = m * C + tile
                total = acc_ref[at : at + 8, :]
                for s in range(STEP):
                    if m == 0:
                        value = scalar[s]
                    else:
                        value = got_ref[at : at + 8, s * ATOMS : (s + 1) * ATOMS]
                        value = value + geo_ref[first + s, m : m + 1, :] * scalar[s]
                    total = total + weight[s][DEGREE[m]] * value
                acc_ref[at : at + 8, :] = total if keep is None else jnp.where(keep, total, 0.0)

    def two_steps(i, carry):
        first = i * (2 * STEP)
        front(first, even_ref, 0)
        back(jnp.maximum(first - STEP, 0), odd_ref, 1, i > 0)
        front(first + STEP, odd_ref, 1)
        back(first, even_ref, 0, None)
        return carry

    lax.fori_loop(0, PAIRS, two_steps, 0)
    back(K - STEP, odd_ref, 1, None)

    message = [acc_ref[m * C : (m + 1) * C, :].astype(bf16) for m in range(COMPS)]
    gate = sigmoid(dot_tn(gate_ref[...], message[0]))
    updated = []
    for degree in range(4):
        start, width = STARTS[degree], WIDTHS[degree]
        mixed = dot_tn(mix_ref[degree], jnp.concatenate(message[start : start + width], axis=1))
        for j in range(width):
            m = start + j
            part = mixed[:, j * ATOMS : (j + 1) * ATOMS]
            before = turned_ref[m * C : (m + 1) * C, :].astype(f32)
            change = silu(part) if degree == 0 else gate * part
            updated.append((before + change).astype(bf16))
    new = jnp.concatenate(updated, axis=0)
    sel = sel_ref[...]
    if not last:
        out_refs[0][...] = new
        picked = dot_nt(sel, new).astype(bf16)
        for face in range(6):
            out_refs[1 + face][...] = picked[face * FACE : (face + 1) * FACE]
    else:
        ones = (
            lax.broadcasted_iota(jnp.int32, (ATOMS, ATOMS), 0)
            == lax.broadcasted_iota(jnp.int32, (ATOMS, ATOMS), 1)
        ).astype(f32).astype(bf16)
        out_refs[0][...] = dot_nt(ones, new).astype(bf16)
        keys = jnp.concatenate(
            [dot(proj_ref[DEGREE[m]], updated[m]) for m in range(COMPS)], axis=0
        ).astype(bf16)
        rows = dot_nt(jnp.concatenate([sel, ones], axis=0), keys).astype(bf16)
        for face in range(6):
            out_refs[1 + face][...] = rows[face * FACE : (face + 1) * FACE]
        out_refs[7][...] = rows[GHOSTS : GHOSTS + HALF]
        out_refs[8][...] = rows[GHOSTS + HALF :]


def layer(t, idx, geo, hidden, turned, sel, ghosts, weights):
    last = t == LAYERS - 1
    if last:
        shapes = [(ATOMS, WIDTH)] + [(FACE, COMPS * RH)] * 6 + [(HALF, COMPS * RH)] * 2
    else:
        shapes = [(WIDTH, ATOMS)] + [(FACE, WIDTH)] * 6
    lanes = STEP * ATOMS
    return pl.pallas_call(
        functools.partial(layer_kernel, last),
        grid=(1,),
        in_specs=[
            whole(K, ATOMS),
            whole(K, GEO_ROWS, ATOMS),
            whole(K, RH, ATOMS),
            whole(WIDTH, ATOMS),
            whole(GHOSTS, ATOMS),
            layer_block(t, RH, 4 * C),
            layer_block(t, 4, C, C),
            layer_block(t, C, C),
            whole(4, RH, C),
        ]
        + [whole(FACE, WIDTH)] * 6,
        out_specs=[whole(*shape) for shape in shapes],
        out_shape=[jax.ShapeDtypeStruct(shape, bf16) for shape in shapes],
        scratch_shapes=[
            pltpu.VMEM((WIDTH, TABLE), bf16),
            pltpu.VMEM((WIDTH, ATOMS), f32),
            pltpu.VMEM((WIDTH, lanes), f32),
            pltpu.VMEM((WIDTH, lanes), f32),
            pltpu.VMEM((2, 4 * C, lanes), f32),
        ],
        compiler_params=params(),
        cost_estimate=pl.CostEstimate(
            flops=2 * 4096 * 512 * WIDTH, bytes_accessed=3_000_000, transcendentals=600_000
        ),
        name="layer",
    )(idx, geo, hidden, turned, sel, *weights, *ghosts)


def probe_weights_kernel(geo_ref, win_ref, wmid_ref, out_ref):
    basis = jnp.concatenate([geo_ref[s, BASIS_ROW:GEO_ROWS, :] for s in range(WIDE)], axis=1)
    hidden = silu(dot_tn(win_ref[...], basis.astype(bf16))).astype(bf16)
    hidden = silu(dot_tn(wmid_ref[...], hidden)).astype(bf16).astype(f32)
    for s in range(WIDE):
        scaled = hidden[:, s * ATOMS : (s + 1) * ATOMS] * geo_ref[s, ENV_ROW : ENV_ROW + 1, :]
        for m in range(COMPS):
            value = scaled if m == 0 else scaled * geo_ref[s, m : m + 1, :]
            out_ref[s, m * RH : (m + 1) * RH, :] = value.astype(bf16)


def probe_weights(geo, probe_in, probe_mid):
    return pl.pallas_call(
        probe_weights_kernel,
        grid=(STEPS,),
        in_specs=[slots(GEO_ROWS, ATOMS), whole(NB, RH), whole(RH, RH)],
        out_specs=slots(COMPS * RH, ATOMS),
        out_shape=jax.ShapeDtypeStruct((K, COMPS * RH, ATOMS), bf16),
        compiler_params=params(("arbitrary",)),
        cost_estimate=pl.CostEstimate(
            flops=2 * 4096 * 256 * WIDTH, bytes_accessed=9_000_000, transcendentals=600_000
        ),
        name="probe_weights",
    )(geo, probe_in, probe_mid)


def readout_kernel(place_ref, idx_ref, weight_ref, near_ref, far_ref, out_ref, keys_ref, acc_ref):
    step = pl.program_id(0)

    @pl.when(step == 0)
    def _():
        chip, core, root_chip, root_core = [place_ref[j] for j in range(4)]
        both = jnp.where(core == root_core, 1, 0)

        def fetch(at, rows, offset, other):
            start = pl.multiple_of(lax.rem(chip - root_chip - offset + 8, 4) * HALF, HALF)
            same = both if other == 0 else 1 - both

            @pl.when(same == 1)
            def _():
                keys_ref[at : at + rows, :] = near_ref[pl.ds(start, rows), :]

            @pl.when(same == 0)
            def _():
                keys_ref[at : at + rows, :] = far_ref[pl.ds(start, rows), :]

        fetch(0, HALF, 0, 0)
        fetch(HALF, HALF, 0, 1)
        for face, (offset, other) in enumerate(HOLDERS):
            fetch(ATOMS + face * FACE, FACE, offset, other)
        acc_ref[...] = jnp.zeros_like(acc_ref)

    weight = jnp.concatenate([weight_ref[s] for s in range(WIDE)], axis=1)
    product = dot(keys_ref[...], weight)
    rows = lax.broadcasted_iota(jnp.int32, (TABLE, ATOMS), 0)
    total = acc_ref[...]
    for s in range(WIDE):
        chosen = rows == idx_ref[pl.ds(step * WIDE + s, 1), :]
        part = jnp.where(chosen, product[:, s * ATOMS : (s + 1) * ATOMS], 0.0)
        total = total + jnp.sum(part.reshape(TABLE // 8, 8, ATOMS), axis=0)
    acc_ref[...] = total

    @pl.when(step == STEPS - 1)
    def _():
        out_ref[...] = jnp.sum(acc_ref[...], axis=0, keepdims=True)


def readout(place, idx, weight, near, far):
    return pl.pallas_call(
        readout_kernel,
        grid_spec=pltpu.PrefetchScalarGridSpec(
            num_scalar_prefetch=1,
            grid=(STEPS,),
            in_specs=[
                pl.BlockSpec((K, ATOMS), lambda i, place: (0, 0)),
                pl.BlockSpec((WIDE, COMPS * RH, ATOMS), lambda i, place: (i, 0, 0)),
                pl.BlockSpec((4 * HALF, COMPS * RH), lambda i, place: (0, 0)),
                pl.BlockSpec((4 * HALF, COMPS * RH), lambda i, place: (0, 0)),
            ],
            out_specs=pl.BlockSpec((1, ATOMS), lambda i, place: (0, 0)),
            scratch_shapes=[pltpu.VMEM((TABLE, COMPS * RH), bf16), pltpu.VMEM((8, ATOMS), f32)],
        ),
        out_shape=jax.ShapeDtypeStruct((1, ATOMS), f32),
        compiler_params=params(("arbitrary",)),
        name="readout",
    )(place, idx, weight, near, far)


DIRECTIONS = (("gx", 1), ("gx", -1), ("gy", 1), ("gy", -1), ("gz", 1), ("gz", -1))
HOLDERS = ((1, 0), (3, 0), (2, 0), (2, 1), (3, 1), (1, 1))
SENT_FIRST = (2, 3, 0, 1, 4, 5)


def shift(block, axis, by):
    count = lax.axis_size(axis)
    return lax.ppermute(block, axis, [(i, (i + by) % count) for i in range(count)])


def exchange(faces):
    landed = [None] * 6
    for face in SENT_FIRST:
        axis, by = DIRECTIONS[face]
        landed[face] = shift(faces[face], axis, by)
    return landed


def holder(place, offset, other):
    return (place // 2 + offset) % 4 * 2 + (place % 2 + other) % 2


def to_holder(block, axis, by, offset, other):
    outer, inner = lax.axis_size(axis), lax.axis_size("gz")
    if axis == "gz":
        pairs = [(i, holder((i + by) % inner, offset, other)) for i in range(inner)]
        return lax.ppermute(block, axis, pairs)
    pairs = [
        (i * inner + j, (i + by) % outer * inner + holder(j, offset, other))
        for i in range(outer)
        for j in range(inner)
    ]
    return lax.ppermute(block, (axis, "gz"), pairs)


def column_keys(faces, own_low, own_high, chip, core, root_chip, root_core, probe_weight):
    landed = [None] * 6
    for face in SENT_FIRST:
        landed[face] = to_holder(faces[face], *DIRECTIONS[face], *HOLDERS[face])
    other_half = to_holder(own_high, "gz", 0, 0, 1)
    offset = (chip - root_chip + 4) % 4
    other = (core - root_core + 2) % 2
    at_root = (offset == 0) & (other == 0)
    low = jnp.where(at_root, own_low[:FACE], other_half[:FACE])
    for face in range(6):
        here = (offset == HOLDERS[face][0]) & (other == HOLDERS[face][1])
        low = jnp.where(here, landed[face], low)
    high = jnp.where(at_root, own_low[FACE:], other_half[FACE:])
    mine = jnp.concatenate([low, high], axis=0)
    moved = [
        lax.ppermute(mine, "gz", [(i, (i + 2 * by) % 8) for i in range(8)]) for by in (1, 2, 3)
    ]
    *moved, probe_weight = lax.optimization_barrier((*moved, probe_weight))
    near = jnp.concatenate([mine] + moved, axis=0)
    far = lax.ppermute(near, "gz", [(i, i + 1 - 2 * (i % 2)) for i in range(8)])
    return near, far, probe_weight


def local(
    features,
    species,
    octant_lists,
    neighbour_index,
    neighbour_count,
    edge_vectors,
    radial_in,
    species_emb,
    radial_mid,
    radial_out,
    mix_weight,
    gate_weight,
    probe_in,
    probe_mid,
    probe_proj,
    probe_vectors,
    probe_index,
    probe_count,
    slab_index,
):
    column = lax.axis_index("gx") * lax.axis_size("gy") + lax.axis_index("gy")
    root = lax.dynamic_index_in_dim(slab_index, column, 0, keepdims=False)
    mine = lax.axis_index("gz")
    chip, core, root_chip, root_core = mine // 2, mine % 2, root // 2, root % 2

    sel, *faces = pick(octant_lists, features)
    ghosts = exchange(faces)
    turned, geo, probe_geo = prepare(
        features,
        edge_vectors,
        neighbour_count.reshape(1, ATOMS),
        probe_vectors,
        probe_count.reshape(1, ATOMS),
    )
    species_row = species.reshape(1, ATOMS)
    weights = (radial_out, mix_weight, gate_weight, jnp.swapaxes(probe_proj, 1, 2))
    emb_turned = jnp.swapaxes(species_emb, 1, 2)
    for t in range(LAYERS):
        hidden = hidden_units(t, species_row, geo, radial_in, emb_turned, radial_mid)
        outs = layer(t, neighbour_index, geo, hidden, turned, sel, ghosts, weights)
        if t < LAYERS - 1:
            turned = outs[0]
            ghosts = exchange(outs[1:])
    near, far, probe_weight = column_keys(
        outs[1:7], outs[7], outs[8], chip, core, root_chip, root_core,
        probe_weights(probe_geo, probe_in, probe_mid),
    )
    place = jnp.stack([chip, core, root_chip, root_core])
    density = readout(place, probe_index, probe_weight, near, far)
    return (outs[0], density.reshape(ATOMS))


def solution(mesh):
    in_specs = (
        P(("gx", "gy", "gz"), None),
        P(("gx", "gy", "gz")),
        P(None, None, None, ("gx", "gy", "gz")),
        P(None, ("gx", "gy", "gz")),
        P(("gx", "gy", "gz")),
        P(None, None, ("gx", "gy", "gz")),
        P(),
        P(),
        P(),
        P(),
        P(),
        P(),
        P(),
        P(),
        P(),
        P(None, None, ("gx", "gy", "gz")),
        P(None, ("gx", "gy", "gz")),
        P(("gx", "gy", "gz")),
        P(),
    )
    out_specs = (P(("gx", "gy", "gz"), None), P(("gx", "gy", "gz")))
    return jax.shard_map(local, mesh=mesh, in_specs=in_specs, out_specs=out_specs, check_vma=False)
```

time: 836 us -> 142 us (0.17); the launches traced: 824 us -> 142 us
  local copies, waits for them, and re-layouts: 345 us -> 12.5 us
  other arithmetic: 162 us -> 0.19 us
  waiting for transfers between devices: 142 us -> 11.2 us
  matrix products: 97.7 us -> 0 us
  Pallas kernels: 0 us -> 47.4 us
  between operations: 15.8 us -> 3.66 us
  starting transfers between devices: 57.3 us -> 66.8 us
    reshape x33 -> x0, local copies, waits for them, and re-layouts: 126 us -> none  [the longest x12 93.8 us: update_one_block(): jnp.take(table_rows, index_part, axis=0)]
    gather x28 -> x0, local copies, waits for them, and re-layouts: 112 us -> none  [the longest x12 67.3 us: update_one_block(): jnp.take(table_rows, index_part, axis=0)]
    dot_general x105 -> x0, matrix products: 97.7 us -> none  [the longest x12 29.7 us: update_one_block(): jnp.einsum('krg,go->kro', hidden_two, radial_out, preferred_element_type=...]
    dot_general x48 -> x0, other arithmetic: 83.1 us -> none  [degree_messages(): jnp.einsum('krmc,krc->rmc', segment, weight_here, preferred_element_type=...]
    psum x1 -> x0, waiting for transfers between devices: 71.6 us -> none  [spread(): return lax.psum(block, axis)]
    slice x93 -> x0, local copies, waits for them, and re-layouts: 70 us -> none  [the longest x12 41.3 us: degree_messages(): weight_here = radial4[:, :, degree, :]]
    ppermute x24 -> x29, waiting for transfers between devices: 70.4 us -> 11.2 us  [the longest x18 3.79 us: shift(): lax.ppermute(block, axis, [(i, (i + by) % count) for i in range(count)])]
    pallas_call x0 -> x10, Pallas kernels: none -> 47.4 us  [the longest x3 33.3 us: layer(): pl.pallas_call(functools.partial(layer_kernel, last), grid=(1,), in_specs...]
  transfers between devices with their start and end apart: 25 -> 29, of which waited for: 17 -> 7; matrix products, arithmetic and copies ran while one was open for 2% -> 0% of each run, Pallas kernels for 0% -> 6%
where the time goes in v1:
time: 142 us
  starting transfers between devices  66.8 us (47%)
  Pallas kernels  47.4 us (33%)
  local copies, waits for them, and re-layouts  12.5 us (9%)
  waiting for transfers between devices  11.2 us (8%)
  between operations  3.66 us (3%)
    ppermute x18, starting transfers between devices, shift(): lax.ppermute(block, axis, [(i, (i + by) % count) for i in range(count)])  45.3 us
    pallas_call x3, Pallas kernels, layer(): pl.pallas_call(functools.partial(layer_kernel, last), grid=(1,), in_specs...  33.3 us
    unnamed x50, local copies, waits for them, and re-layouts  11.9 us
    ppermute x3, starting transfers between devices, to_holder(): return lax.ppermute(block, axis, pairs)  7.5 us
    ppermute x4, starting transfers between devices, to_holder(): return lax.ppermute(block, (axis, 'gz'), pairs)  6.41 us
    pallas_call x1, Pallas kernels, readout(): pl.pallas_call(readout_kernel, grid_spec=pltpu.PrefetchScalarGridSpec(num...  5.43 us
    pallas_call x1, Pallas kernels, probe_weights(): pl.pallas_call(probe_weights_kernel, grid=(STEPS,), in_specs=[slots(GEO_R...  4.12 us
    ppermute x1, starting transfers between devices, column_keys(): far = lax.ppermute(near, 'gz', [(i, i + 1 - 2 * (i % 2)) for i in range(8)])  4.02 us
  transfers between devices with their start and end apart: 29, of which 7 were waited for; matrix products, arithmetic and copies ran while one was open for 0% of the time, Pallas kernels for 6%

profile of v1, /device:TPU:1, one launch (start us, length us, event | category | flops | bytes accessed | tf_op | source)
XLA Modules:
  0.0 141.7 jit_solution(15277493726769249840)
XLA Ops:
  0.6 1.0 copy-done
  2.8 2.1 %collective-permute-start = (bf16[32,1536]{1,0:T(8,128)(2,1)S(1)}, bf16[32,1536]{1,0:T(8,128)(2,1)S(1)}, u32[]{:S(2)}, u32[]{:S(2)}) collective-permute-start(bf16[32,1536]{1,0:T(8,128)(2,1)S(1)} %get-tuple-element.42), channel_id=1, source_target_pairs={{0,64},{64,128},{128,192},{192,0},{1,65},{65,129},{129,193},{193,1... | collective-permute-start | bytes 294920 | tf_op jit(solution)/shard_map/ppermute | solution.py:451
  4.9 1.4 collective-permute-start.1
  6.3 1.4 collective-permute-start.2
  7.7 8.1 %collective-permute-start.3 = (bf16[32,1536]{1,0:T(8,128)(2,1)S(1)}, bf16[32,1536]{1,0:T(8,128)(2,1)S(1)}, u32[]{:S(2)}, u32[]{:S(2)}) collective-permute-start(bf16[32,1536]{1,0:T(8,128)(2,1)S(1)} %get-tuple-element.45), channel_id=1, source_target_pairs={{0,56},{8,0},{16,8},{24,16},{32,24},{40,32},{48,40},{56,48},{1,57}... | collective-permute-start | bytes 294920 | tf_op jit(solution)/shard_map/ppermute | solution.py:451
  15.7 2.1 %collective-permute-start.4 = (bf16[32,1536]{1,0:T(8,128)(2,1)S(1)}, bf16[32,1536]{1,0:T(8,128)(2,1)S(1)}, u32[]{:S(2)}, u32[]{:S(2)}) collective-permute-start(bf16[32,1536]{1,0:T(8,128)(2,1)S(1)} %get-tuple-element.46), channel_id=1, source_target_pairs={{0,1},{1,2},{2,3},{3,4},{4,5},{5,6},{6,7},{7,0},{8,9},{9,10},{10,1... | collective-permute-start | bytes 294920 | tf_op jit(solution)/shard_map/ppermute | solution.py:451
  17.9 0.8 copy-done.4
  18.7 0.8 copy-done.5
  20.8 1.1 prepare.1
  21.9 0.8 copy-done.1
  22.7 0.8 copy-done.2
  23.5 0.7 copy-done.3
  24.9 1.0 hidden_units.5.refs_2_
  25.9 1.0 copy-done.12
  26.9 0.9 copy-done.14
  27.8 0.9 copy-done.16
  28.7 0.8 copy-done.18
  29.5 0.7 copy-done.20
  30.3 10.9 %layer.3 = (bf16[1536,128]{1,0:T(8,128)(2,1)S(1)}, bf16[32,1536]{1,0:T(8,128)(2,1)S(1)}, bf16[32,1536]{1,0:T(8,128)(2,1)S(1)}, bf16[32,1536]{1,0:T(8,128)(2,1)S(...) custom-call(s32[32,128]{1,0:T(8,128)S(1)} %copy-done.20, ...), custom_call_target="tpu_custom_call" | custom-call | flops 6442450944 | bytes 3000000 | tf_op jit(solution)/shard_map/layer/pallas_call | solution.py:324
  41.2 2.7 %collective-permute-start.7 = (bf16[32,1536]{1,0:T(8,128)(2,1)S(1)}, bf16[32,1536]{1,0:T(8,128)(2,1)S(1)}, u32[]{:S(2)}, u32[]{:S(2)}) collective-permute-start(bf16[32,1536]{1,0:T(8,128)(2,1)S(1)} %get-tuple-element.50), channel_id=1, source_target_pairs={{0,192},{64,0},{128,64},{192,128},{1,193},{65,1},{129,65},{193,129... | collective-permute-start | bytes 294920 | tf_op jit(solution)/shard_map/ppermute | solution.py:451
  43.9 7.5 %collective-permute-start.9 = (bf16[32,1536]{1,0:T(8,128)(2,1)S(1)}, bf16[32,1536]{1,0:T(8,128)(2,1)S(1)}, u32[]{:S(2)}, u32[]{:S(2)}) collective-permute-start(bf16[32,1536]{1,0:T(8,128)(2,1)S(1)} %get-tuple-element.52), channel_id=1, source_target_pairs={{0,56},{8,0},{16,8},{24,16},{32,24},{40,32},{48,40},{56,48},{1,57}... | collective-permute-start | bytes 294920 | tf_op jit(solution)/shard_map/ppermute | solution.py:451
  51.4 2.9 %collective-permute-start.10 = (bf16[32,1536]{1,0:T(8,128)(2,1)S(1)}, bf16[32,1536]{1,0:T(8,128)(2,1)S(1)}, u32[]{:S(2)}, u32[]{:S(2)}) collective-permute-start(bf16[32,1536]{1,0:T(8,128)(2,1)S(1)} %get-tuple-element.53), channel_id=1, source_target_pairs={{0,1},{1,2},{2,3},{3,4},{4,5},{5,6},{6,7},{7,0},{8,9},{9,10},{10,1... | collective-permute-start | bytes 294920 | tf_op jit(solution)/shard_map/ppermute | solution.py:451
  54.3 1.3 collective-permute-start.11
  55.6 1.0 hidden_units.4.refs_2_
  56.6 2.4 %collective-permute-done.11.refs_14_ = bf16[32,1536]{1,0:T(8,128)(2,1)S(1)} collective-permute-done((bf16[32,1536]{1,0:T(8,128)(2,1)S(1)}, bf16[32,1536]{1,0:T(8,128)(2,1)S(1)}, u32[]{:S(2)}, u32[]{:S(2)}) %collective-permute-start.11) | collective-permute-done | bytes 98336 | tf_op jit(solution)/shard_map/ppermute | solution.py:451
  59.0 10.9 %layer.4 = (bf16[1536,128]{1,0:T(8,128)(2,1)S(1)}, bf16[32,1536]{1,0:T(8,128)(2,1)S(1)}, bf16[32,1536]{1,0:T(8,128)(2,1)S(1)}, bf16[32,1536]{1,0:T(8,128)(2,1)S(...) custom-call(s32[32,128]{1,0:T(8,128)S(1)} %copy-done.20, ...), custom_call_target="tpu_custom_call" | custom-call | flops 6442450944 | bytes 3000000 | tf_op jit(solution)/shard_map/layer/pallas_call | solution.py:324
  70.0 2.7 %collective-permute-start.13 = (bf16[32,1536]{1,0:T(8,128)(2,1)S(1)}, bf16[32,1536]{1,0:T(8,128)(2,1)S(1)}, u32[]{:S(2)}, u32[]{:S(2)}) collective-permute-start(bf16[32,1536]{1,0:T(8,128)(2,1)S(1)} %get-tuple-element.57), channel_id=1, source_target_pairs={{0,192},{64,0},{128,64},{192,128},{1,193},{65,1},{129,65},{193,129... | collective-permute-start | bytes 294920 | tf_op jit(solution)/shard_map/ppermute | solution.py:451
  72.7 7.5 %collective-permute-start.15 = (bf16[32,1536]{1,0:T(8,128)(2,1)S(1)}, bf16[32,1536]{1,0:T(8,128)(2,1)S(1)}, u32[]{:S(2)}, u32[]{:S(2)}) collective-permute-start(bf16[32,1536]{1,0:T(8,128)(2,1)S(1)} %get-tuple-element.59), channel_id=1, source_target_pairs={{0,56},{8,0},{16,8},{24,16},{32,24},{40,32},{48,40},{56,48},{1,57}... | collective-permute-start | bytes 294920 | tf_op jit(solution)/shard_map/ppermute | solution.py:451
  80.2 0.9 collective-permute-start.16
  81.1 4.6 %collective-permute-start.17 = (bf16[32,1536]{1,0:T(8,128)(2,1)S(1)}, bf16[32,1536]{1,0:T(8,128)(2,1)S(1)}, u32[]{:S(2)}, u32[]{:S(2)}) collective-permute-start(bf16[32,1536]{1,0:T(8,128)(2,1)S(1)} %get-tuple-element.61), channel_id=1, source_target_pairs={{0,7},{1,0},{2,1},{3,2},{4,3},{5,4},{6,5},{7,6},{8,15},{9,8},{10,9... | collective-permute-start | bytes 294920 | tf_op jit(solution)/shard_map/ppermute | solution.py:451
  85.7 1.0 hidden_units.3.refs_2_
  86.8 1.4 collective-permute-done.17.refs_14_
  88.2 11.6 %layer.5 = (bf16[128,1536]{1,0:T(8,128)(2,1)}, bf16[32,1024]{1,0:T(8,128)(2,1)S(1)}, bf16[32,1024]{1,0:T(8,128)(2,1)S(1)}, bf16[32,1024]{1,0:T(8,128)(2,1)S(1)},...) custom-call(s32[32,128]{1,0:T(8,128)S(1)} %copy-done.20, ...), custom_call_target="tpu_custom_call" | custom-call | flops 6442450944 | bytes 3000000 | tf_op jit(solution)/shard_map/layer/pallas_call | solution.py:324
  99.7 5.6 %collective-permute-start.18 = (bf16[32,1024]{1,0:T(8,128)(2,1)S(1)}, bf16[32,1024]{1,0:T(8,128)(2,1)S(1)}, u32[]{:S(2)}, u32[]{:S(2)}) collective-permute-start(bf16[32,1024]{1,0:T(8,128)(2,1)S(1)} %get-tuple-element.63), channel_id=1, source_target_pairs={{0,0},{1,3},{2,2},{3,5},{4,4},{5,7},{6,6},{7,1},{8,8},{9,11},{10,1... | collective-permute-start | bytes 196616 | tf_op jit(solution)/shard_map/ppermute | solution.py:470
  106.0 1.3 collective-permute-start.24
  107.2 4.0 %collective-permute-start.20 = (bf16[32,1024]{1,0:T(8,128)(2,1)S(1)}, bf16[32,1024]{1,0:T(8,128)(2,1)S(1)}, u32[]{:S(2)}, u32[]{:S(2)}) collective-permute-start(bf16[32,1024]{1,0:T(8,128)(2,1)S(1)} %get-tuple-element.65), channel_id=1, source_target_pairs={{0,61},{1,60},{2,63},{3,62},{4,57},{5,56},{6,59},{7,58},{8,5},{9,4... | collective-permute-start | bytes 196616 | tf_op jit(solution)/shard_map/ppermute | solution.py:476
  111.3 0.9 collective-permute-start.22
  112.2 1.4 %collective-permute-start.23 = (bf16[32,1024]{1,0:T(8,128)(2,1)S(1)}, bf16[32,1024]{1,0:T(8,128)(2,1)S(1)}, u32[]{:S(2)}, u32[]{:S(2)}) collective-permute-start(bf16[32,1024]{1,0:T(8,128)(2,1)S(1)} %get-tuple-element.68), channel_id=1, source_target_pairs={{0,66},{1,67},{2,68},{3,69},{4,70},{5,71},{6,64},{7,65},{64,130},{... | collective-permute-start | bytes 196616 | tf_op jit(solution)/shard_map/ppermute | solution.py:476
  116.9 2.2 %collective-permute-done.21 = bf16[32,1024]{1,0:T(8,128)(2,1)S(1)} collective-permute-done((bf16[32,1024]{1,0:T(8,128)(2,1)S(1)}, bf16[32,1024]{1,0:T(8,128)(2,1)S(1)}, u32[]{:S(2)}, u32[]{:S(2)}) %collective-permute-start.21) | collective-permute-done | bytes 65568 | tf_op jit(solution)/shard_map/ppermute | solution.py:476
  119.7 0.9 collective-permute-start.27
  120.6 1.2 collective-permute-start.26
  121.8 1.4 collective-permute-start.25
  123.2 4.1 %probe_weights.1.weight_ref = bf16[32,1024,128]{2,1,0:T(8,128)(2,1)S(1)} custom-call(f32[32,32,128]{2,1,0:T(8,128)S(1)} %get-tuple-element.71.geo_ref, bf16[8,64]{1,0:T(8,128)(2,1)S(1)} %copy-done.22, bf16[64,64]{1,0:T(8,128)(2,1)S(1)} %copy-done.21), custom_call_target="tpu_custom_call" | custom-call | flops 3221225472 | bytes 9000000 | tf_op jit(solution)/shard_map/probe_weights/pallas_call | solution.py:368
  127.3 0.8 collective-permute-done.26
  128.2 2.5 %collective-permute-done.25 = bf16[64,1024]{1,0:T(8,128)(2,1)S(1)} collective-permute-done((bf16[64,1024]{1,0:T(8,128)(2,1)S(1)}, bf16[64,1024]{1,0:T(8,128)(2,1)S(1)}, u32[]{:S(2)}, u32[]{:S(2)}) %collective-permute-start.25) | collective-permute-done | bytes 131104 | tf_op jit(solution)/shard_map/ppermute | solution.py:494
  130.7 4.0 %collective-permute-start.28 = (bf16[256,1024]{1,0:T(8,128)(2,1)S(1)}, bf16[256,1024]{1,0:T(8,128)(2,1)S(1)}, u32[]{:S(2)}, u32[]{:S(2)}) collective-permute-start(bf16[256,1024]{1,0:T(8,128)(2,1)S(1)} %constant_dynamic-update-slice_fusion.near_ref), channel_id=1, source_target_pairs={{0,1},{1,0},{2,3},{3,2},{4,5},{5,4},{6,7},{7,6},{8,9},{9,8},{10,11... | collective-permute-start | bytes 1572872 | tf_op jit(solution)/shard_map/ppermute | solution.py:498
  134.8 1.5 %collective-permute-done.28.far_ref = bf16[256,1024]{1,0:T(8,128)(2,1)S(1)} collective-permute-done((bf16[256,1024]{1,0:T(8,128)(2,1)S(1)}, bf16[256,1024]{1,0:T(8,128)(2,1)S(1)}, u32[]{:S(2)}, u32[]{:S(2)}) %collective-permute-start.28) | collective-permute-done | bytes 524320 | tf_op jit(solution)/shard_map/ppermute | solution.py:498
  136.3 5.4 %readout.1 = f32[1,128]{1,0:T(1,128)} custom-call(s32[4]{0:T(128)S(1)} %pad_add_fusion.place_ref, s32[32,128]{1,0:T(8,128)S(1)} %copy-done.6, bf16[32,1024,128]{2,1,0:T(8,128)(2,1)S(1)} %probe_weights.1.weight_ref, bf16[256,1024]{1,0:T(8,128)(2,1)S(1)} %constant_dynamic-update-slice_fusion.near_ref, bf16[256,1024]{1,0:T(8,128)(2,1)S(1)} %collective-permute-done.28.far_ref), custom_call_target="tpu_custom_call" | custom-call | tf_op jit(solution)/shard_map/readout/pallas_call | solution.py:424
  (76 shorter events, 5.3 us)
Async XLA Ops:
  0.6 1.0 copy-start
  2.8 15.1 %collective-permute-start = (bf16[32,1536]{1,0:T(8,128)(2,1)S(1)}, bf16[32,1536]{1,0:T(8,128)(2,1)S(1)}, u32[]{:S(2)}, u32[]{:S(2)}) collective-permute-start(bf16[32,1536]{1,0:T(8,128)(2,1)S(1)} %get-tuple-element.42), channel_id=1, source_target_pairs={{0,64},{64,128},{128,192},{192,0},{1,65},{65,129},{129,193},{193,1... | collective-permute-start | bytes 294920 | tf_op jit(solution)/shard_map/ppermute | solution.py:451
  4.9 21.0 %collective-permute-start.1 = (bf16[32,1536]{1,0:T(8,128)(2,1)S(1)}, bf16[32,1536]{1,0:T(8,128)(2,1)S(1)}, u32[]{:S(2)}, u32[]{:S(2)}) collective-permute-start(bf16[32,1536]{1,0:T(8,128)(2,1)S(1)} %get-tuple-element.43), channel_id=1, source_target_pairs={{0,192},{64,0},{128,64},{192,128},{1,193},{65,1},{129,65},{193,129... | collective-permute-start | bytes 294920 | tf_op jit(solution)/shard_map/ppermute | solution.py:451
  6.3 19.6 %collective-permute-start.2 = (bf16[32,1536]{1,0:T(8,128)(2,1)S(1)}, bf16[32,1536]{1,0:T(8,128)(2,1)S(1)}, u32[]{:S(2)}, u32[]{:S(2)}) collective-permute-start(bf16[32,1536]{1,0:T(8,128)(2,1)S(1)} %get-tuple-element.44), channel_id=1, source_target_pairs={{0,8},{8,16},{16,24},{24,32},{32,40},{40,48},{48,56},{56,0},{1,9},... | collective-permute-start | bytes 294920 | tf_op jit(solution)/shard_map/ppermute | solution.py:451
  7.7 18.2 %collective-permute-start.3 = (bf16[32,1536]{1,0:T(8,128)(2,1)S(1)}, bf16[32,1536]{1,0:T(8,128)(2,1)S(1)}, u32[]{:S(2)}, u32[]{:S(2)}) collective-permute-start(bf16[32,1536]{1,0:T(8,128)(2,1)S(1)} %get-tuple-element.45), channel_id=1, source_target_pairs={{0,56},{8,0},{16,8},{24,16},{32,24},{40,32},{48,40},{56,48},{1,57}... | collective-permute-start | bytes 294920 | tf_op jit(solution)/shard_map/ppermute | solution.py:451
  15.7 10.2 %collective-permute-start.4 = (bf16[32,1536]{1,0:T(8,128)(2,1)S(1)}, bf16[32,1536]{1,0:T(8,128)(2,1)S(1)}, u32[]{:S(2)}, u32[]{:S(2)}) collective-permute-start(bf16[32,1536]{1,0:T(8,128)(2,1)S(1)} %get-tuple-element.46), channel_id=1, source_target_pairs={{0,1},{1,2},{2,3},{3,4},{4,5},{5,6},{6,7},{7,0},{8,9},{9,10},{10,1... | collective-permute-start | bytes 294920 | tf_op jit(solution)/shard_map/ppermute | solution.py:451
  17.9 8.0 %collective-permute-start.5 = (bf16[32,1536]{1,0:T(8,128)(2,1)S(1)}, bf16[32,1536]{1,0:T(8,128)(2,1)S(1)}, u32[]{:S(2)}, u32[]{:S(2)}) collective-permute-start(bf16[32,1536]{1,0:T(8,128)(2,1)S(1)} %get-tuple-element.47), channel_id=1, source_target_pairs={{0,7},{1,0},{2,1},{3,2},{4,3},{5,4},{6,5},{7,6},{8,15},{9,8},{10,9... | collective-permute-start | bytes 294920 | tf_op jit(solution)/shard_map/ppermute | solution.py:451
  17.9 0.8 copy-start.4
  18.7 0.8 copy-start.5
  21.9 0.8 copy-start.1
  22.7 0.8 copy-start.2
  25.9 1.0 copy-start.12
  26.9 0.9 copy-start.14
  27.8 0.9 copy-start.16
  28.7 0.8 copy-start.18
  29.5 0.7 copy-start.20
  30.3 25.3 %copy-start.8 = (s32[128]{0:T(128)S(1)}, s32[128]{0:T(128)}, u32[]{:S(2)}) copy-start(s32[128]{0:T(128)} %param.20) | copy-start | bytes 1540
  30.3 28.8 %copy-start.13 = (bf16[3,4,96,96]{3,2,1,0:T(8,128)(2,1)S(1)}, bf16[3,4,96,96]{3,2,1,0:T(8,128)(2,1)}, u32[]{:S(2)}) copy-start(bf16[3,4,96,96]{3,2,1,0:T(8,128)(2,1)} %refs_6_.5) | copy-start | bytes 663556
  30.3 28.8 %copy-start.15 = (bf16[3,64,384]{2,1,0:T(8,128)(2,1)S(1)}, bf16[3,64,384]{2,1,0:T(8,128)(2,1)}, u32[]{:S(2)}) copy-start(bf16[3,64,384]{2,1,0:T(8,128)(2,1)} %refs_5_.5) | copy-start | bytes 442372
  30.3 28.8 %copy-start.17 = (bf16[3,96,96]{2,1,0:T(8,128)(2,1)S(1)}, bf16[3,96,96]{2,1,0:T(8,128)(2,1)}, u32[]{:S(2)}) copy-start(bf16[3,96,96]{2,1,0:T(8,128)(2,1)} %refs_7_.5) | copy-start | bytes 165892
  30.3 28.8 %copy-start.19 = (bf16[4,96,64]{1,2,0:T(8,128)(2,1)S(1)}, bf16[4,96,64]{1,2,0:T(8,128)(2,1)}, u32[]{:S(2)}) copy-start(bf16[4,96,64]{1,2,0:T(8,128)(2,1)} %param.33) | copy-start | bytes 147460
  41.2 13.1 %collective-permute-start.6 = (bf16[32,1536]{1,0:T(8,128)(2,1)S(1)}, bf16[32,1536]{1,0:T(8,128)(2,1)S(1)}, u32[]{:S(2)}, u32[]{:S(2)}) collective-permute-start(bf16[32,1536]{1,0:T(8,128)(2,1)S(1)} %get-tuple-element.49), channel_id=1, source_target_pairs={{0,64},{64,128},{128,192},{192,0},{1,65},{65,129},{129,193},{193,1... | collective-permute-start | bytes 294920 | tf_op jit(solution)/shard_map/ppermute | solution.py:451
  41.2 15.3 %collective-permute-start.7 = (bf16[32,1536]{1,0:T(8,128)(2,1)S(1)}, bf16[32,1536]{1,0:T(8,128)(2,1)S(1)}, u32[]{:S(2)}, u32[]{:S(2)}) collective-permute-start(bf16[32,1536]{1,0:T(8,128)(2,1)S(1)} %get-tuple-element.50), channel_id=1, source_target_pairs={{0,192},{64,0},{128,64},{192,128},{1,193},{65,1},{129,65},{193,129... | collective-permute-start | bytes 294920 | tf_op jit(solution)/shard_map/ppermute | solution.py:451
  43.9 12.7 %collective-permute-start.8 = (bf16[32,1536]{1,0:T(8,128)(2,1)S(1)}, bf16[32,1536]{1,0:T(8,128)(2,1)S(1)}, u32[]{:S(2)}, u32[]{:S(2)}) collective-permute-start(bf16[32,1536]{1,0:T(8,128)(2,1)S(1)} %get-tuple-element.51), channel_id=1, source_target_pairs={{0,8},{8,16},{16,24},{24,32},{32,40},{40,48},{48,56},{56,0},{1,9},... | collective-permute-start | bytes 294920 | tf_op jit(solution)/shard_map/ppermute | solution.py:451
  43.9 12.7 %collective-permute-start.9 = (bf16[32,1536]{1,0:T(8,128)(2,1)S(1)}, bf16[32,1536]{1,0:T(8,128)(2,1)S(1)}, u32[]{:S(2)}, u32[]{:S(2)}) collective-permute-start(bf16[32,1536]{1,0:T(8,128)(2,1)S(1)} %get-tuple-element.52), channel_id=1, source_target_pairs={{0,56},{8,0},{16,8},{24,16},{32,24},{40,32},{48,40},{56,48},{1,57}... | collective-permute-start | bytes 294920 | tf_op jit(solution)/shard_map/ppermute | solution.py:451
  51.4 5.2 %collective-permute-start.10 = (bf16[32,1536]{1,0:T(8,128)(2,1)S(1)}, bf16[32,1536]{1,0:T(8,128)(2,1)S(1)}, u32[]{:S(2)}, u32[]{:S(2)}) collective-permute-start(bf16[32,1536]{1,0:T(8,128)(2,1)S(1)} %get-tuple-element.53), channel_id=1, source_target_pairs={{0,1},{1,2},{2,3},{3,4},{4,5},{5,6},{6,7},{7,0},{8,9},{9,10},{10,1... | collective-permute-start | bytes 294920 | tf_op jit(solution)/shard_map/ppermute | solution.py:451
  54.3 4.8 %collective-permute-start.11 = (bf16[32,1536]{1,0:T(8,128)(2,1)S(1)}, bf16[32,1536]{1,0:T(8,128)(2,1)S(1)}, u32[]{:S(2)}, u32[]{:S(2)}) collective-permute-start(bf16[32,1536]{1,0:T(8,128)(2,1)S(1)} %get-tuple-element.54), channel_id=1, source_target_pairs={{0,7},{1,0},{2,1},{3,2},{4,3},{5,4},{6,5},{7,6},{8,15},{9,8},{10,9... | collective-permute-start | bytes 294920 | tf_op jit(solution)/shard_map/ppermute | solution.py:451
  69.9 11.2 %collective-permute-start.12 = (bf16[32,1536]{1,0:T(8,128)(2,1)S(1)}, bf16[32,1536]{1,0:T(8,128)(2,1)S(1)}, u32[]{:S(2)}, u32[]{:S(2)}) collective-permute-start(bf16[32,1536]{1,0:T(8,128)(2,1)S(1)} %get-tuple-element.56), channel_id=1, source_target_pairs={{0,64},{64,128},{128,192},{192,0},{1,65},{65,129},{129,193},{193,1... | collective-permute-start | bytes 294920 | tf_op jit(solution)/shard_map/ppermute | solution.py:451
  70.0 16.7 %collective-permute-start.13 = (bf16[32,1536]{1,0:T(8,128)(2,1)S(1)}, bf16[32,1536]{1,0:T(8,128)(2,1)S(1)}, u32[]{:S(2)}, u32[]{:S(2)}) collective-permute-start(bf16[32,1536]{1,0:T(8,128)(2,1)S(1)} %get-tuple-element.57), channel_id=1, source_target_pairs={{0,192},{64,0},{128,64},{192,128},{1,193},{65,1},{129,65},{193,129... | collective-permute-start | bytes 294920 | tf_op jit(solution)/shard_map/ppermute | solution.py:451
  72.7 14.1 %collective-permute-start.14 = (bf16[32,1536]{1,0:T(8,128)(2,1)S(1)}, bf16[32,1536]{1,0:T(8,128)(2,1)S(1)}, u32[]{:S(2)}, u32[]{:S(2)}) collective-permute-start(bf16[32,1536]{1,0:T(8,128)(2,1)S(1)} %get-tuple-element.58), channel_id=1, source_target_pairs={{0,8},{8,16},{16,24},{24,32},{32,40},{40,48},{48,56},{56,0},{1,9},... | collective-permute-start | bytes 294920 | tf_op jit(solution)/shard_map/ppermute | solution.py:451
  72.7 14.1 %collective-permute-start.15 = (bf16[32,1536]{1,0:T(8,128)(2,1)S(1)}, bf16[32,1536]{1,0:T(8,128)(2,1)S(1)}, u32[]{:S(2)}, u32[]{:S(2)}) collective-permute-start(bf16[32,1536]{1,0:T(8,128)(2,1)S(1)} %get-tuple-element.59), channel_id=1, source_target_pairs={{0,56},{8,0},{16,8},{24,16},{32,24},{40,32},{48,40},{56,48},{1,57}... | collective-permute-start | bytes 294920 | tf_op jit(solution)/shard_map/ppermute | solution.py:451
  80.2 6.6 %collective-permute-start.16 = (bf16[32,1536]{1,0:T(8,128)(2,1)S(1)}, bf16[32,1536]{1,0:T(8,128)(2,1)S(1)}, u32[]{:S(2)}, u32[]{:S(2)}) collective-permute-start(bf16[32,1536]{1,0:T(8,128)(2,1)S(1)} %get-tuple-element.60), channel_id=1, source_target_pairs={{0,1},{1,2},{2,3},{3,4},{4,5},{5,6},{6,7},{7,0},{8,9},{9,10},{10,1... | collective-permute-start | bytes 294920 | tf_op jit(solution)/shard_map/ppermute | solution.py:451
  81.1 7.0 %collective-permute-start.17 = (bf16[32,1536]{1,0:T(8,128)(2,1)S(1)}, bf16[32,1536]{1,0:T(8,128)(2,1)S(1)}, u32[]{:S(2)}, u32[]{:S(2)}) collective-permute-start(bf16[32,1536]{1,0:T(8,128)(2,1)S(1)} %get-tuple-element.61), channel_id=1, source_target_pairs={{0,7},{1,0},{2,1},{3,2},{4,3},{5,4},{6,5},{7,6},{8,15},{9,8},{10,9... | collective-permute-start | bytes 294920 | tf_op jit(solution)/shard_map/ppermute | solution.py:451
  88.1 25.5 %copy-start.23 = (s32[32]{0:T(128)S(1)}, s32[32]{0:T(128)}, u32[]{:S(2)}) copy-start(s32[32]{0:T(128)} %param.37) | copy-start | bytes 388
  88.1 35.1 %copy-start.21 = (bf16[64,64]{1,0:T(8,128)(2,1)S(1)}, bf16[64,64]{1,0:T(8,128)(2,1)}, u32[]{:S(2)}) copy-start(bf16[64,64]{1,0:T(8,128)(2,1)} %wmid_ref.7) | copy-start | bytes 24580
  88.2 35.1 %copy-start.22 = (bf16[8,64]{1,0:T(8,128)(2,1)S(1)}, bf16[8,64]{1,0:T(8,128)(2,1)}, u32[]{:S(2)}) copy-start(bf16[8,64]{1,0:T(8,128)(2,1)} %win_ref.7) | copy-start | bytes 3076
  99.7 36.6 %copy-start.6 = (s32[32,128]{1,0:T(8,128)S(1)}, s32[32,128]{1,0:T(8,128)}, u32[]{:S(2)}) copy-start(s32[32,128]{1,0:T(8,128)} %idx_ref.1) | copy-start | bytes 49156
  99.7 11.6 %collective-permute-start.18 = (bf16[32,1024]{1,0:T(8,128)(2,1)S(1)}, bf16[32,1024]{1,0:T(8,128)(2,1)S(1)}, u32[]{:S(2)}, u32[]{:S(2)}) collective-permute-start(bf16[32,1024]{1,0:T(8,128)(2,1)S(1)} %get-tuple-element.63), channel_id=1, source_target_pairs={{0,0},{1,3},{2,2},{3,5},{4,4},{5,7},{6,6},{7,1},{8,8},{9,11},{10,1... | collective-permute-start | bytes 196616 | tf_op jit(solution)/shard_map/ppermute | solution.py:470
  105.3 6.9 %collective-permute-start.19 = (bf16[32,1024]{1,0:T(8,128)(2,1)S(1)}, bf16[32,1024]{1,0:T(8,128)(2,1)S(1)}, u32[]{:S(2)}, u32[]{:S(2)}) collective-permute-start(bf16[32,1024]{1,0:T(8,128)(2,1)S(1)} %get-tuple-element.64), channel_id=1, source_target_pairs={{0,6},{1,1},{2,0},{3,3},{4,2},{5,5},{6,4},{7,7},{8,14},{9,9},{10,8... | collective-permute-start | bytes 196616 | tf_op jit(solution)/shard_map/ppermute | solution.py:470
  106.0 13.6 %collective-permute-start.24 = (bf16[64,1024]{1,0:T(8,128)(2,1)S(1)}, bf16[64,1024]{1,0:T(8,128)(2,1)S(1)}, u32[]{:S(2)}, u32[]{:S(2)}) collective-permute-start(bf16[64,1024]{1,0:T(8,128)(2,1)S(1)} %get-tuple-element.70), channel_id=1, source_target_pairs={{0,1},{1,0},{2,3},{3,2},{4,5},{5,4},{6,7},{7,6},{8,9},{9,8},{10,11... | collective-permute-start | bytes 393224 | tf_op jit(solution)/shard_map/ppermute | solution.py:470
  107.2 9.7 %collective-permute-start.20 = (bf16[32,1024]{1,0:T(8,128)(2,1)S(1)}, bf16[32,1024]{1,0:T(8,128)(2,1)S(1)}, u32[]{:S(2)}, u32[]{:S(2)}) collective-permute-start(bf16[32,1024]{1,0:T(8,128)(2,1)S(1)} %get-tuple-element.65), channel_id=1, source_target_pairs={{0,61},{1,60},{2,63},{3,62},{4,57},{5,56},{6,59},{7,58},{8,5},{9,4... | collective-permute-start | bytes 196616 | tf_op jit(solution)/shard_map/ppermute | solution.py:476
  111.3 7.9 %collective-permute-start.21 = (bf16[32,1024]{1,0:T(8,128)(2,1)S(1)}, bf16[32,1024]{1,0:T(8,128)(2,1)S(1)}, u32[]{:S(2)}, u32[]{:S(2)}) collective-permute-start(bf16[32,1024]{1,0:T(8,128)(2,1)S(1)} %get-tuple-element.66), channel_id=1, source_target_pairs={{0,12},{1,13},{2,14},{3,15},{4,8},{5,9},{6,10},{7,11},{8,20},{9,21... | collective-permute-start | bytes 196616 | tf_op jit(solution)/shard_map/ppermute | solution.py:476
  111.3 7.9 %collective-permute-start.22 = (bf16[32,1024]{1,0:T(8,128)(2,1)S(1)}, bf16[32,1024]{1,0:T(8,128)(2,1)S(1)}, u32[]{:S(2)}, u32[]{:S(2)}) collective-permute-start(bf16[32,1024]{1,0:T(8,128)(2,1)S(1)} %get-tuple-element.67), channel_id=1, source_target_pairs={{0,198},{1,199},{2,192},{3,193},{4,194},{5,195},{6,196},{7,197},{6... | collective-permute-start | bytes 196616 | tf_op jit(solution)/shard_map/ppermute | solution.py:476
  112.2 7.3 %collective-permute-start.23 = (bf16[32,1024]{1,0:T(8,128)(2,1)S(1)}, bf16[32,1024]{1,0:T(8,128)(2,1)S(1)}, u32[]{:S(2)}, u32[]{:S(2)}) collective-permute-start(bf16[32,1024]{1,0:T(8,128)(2,1)S(1)} %get-tuple-element.68), channel_id=1, source_target_pairs={{0,66},{1,67},{2,68},{3,69},{4,70},{5,71},{6,64},{7,65},{64,130},{... | collective-permute-start | bytes 196616 | tf_op jit(solution)/shard_map/ppermute | solution.py:476
  119.7 7.7 %collective-permute-start.27 = (bf16[64,1024]{1,0:T(8,128)(2,1)S(1)}, bf16[64,1024]{1,0:T(8,128)(2,1)S(1)}, u32[]{:S(2)}, u32[]{:S(2)}) collective-permute-start(bf16[64,1024]{1,0:T(8,128)(2,1)S(1)} %pad_maximum_fusion), channel_id=1, source_target_pairs={{0,6},{1,7},{2,0},{3,1},{4,2},{5,3},{6,4},{7,5},{8,14},{9,15},{10,... | collective-permute-start | bytes 393224 | tf_op jit(solution)/shard_map/ppermute | solution.py:494
  120.6 7.6 %collective-permute-start.26 = (bf16[64,1024]{1,0:T(8,128)(2,1)S(1)}, bf16[64,1024]{1,0:T(8,128)(2,1)S(1)}, u32[]{:S(2)}, u32[]{:S(2)}) collective-permute-start(bf16[64,1024]{1,0:T(8,128)(2,1)S(1)} %pad_maximum_fusion), channel_id=1, source_target_pairs={{0,4},{1,5},{2,6},{3,7},{4,0},{5,1},{6,2},{7,3},{8,12},{9,13},{10,... | collective-permute-start | bytes 393224 | tf_op jit(solution)/shard_map/ppermute | solution.py:494
  121.8 8.8 %collective-permute-start.25 = (bf16[64,1024]{1,0:T(8,128)(2,1)S(1)}, bf16[64,1024]{1,0:T(8,128)(2,1)S(1)}, u32[]{:S(2)}, u32[]{:S(2)}) collective-permute-start(bf16[64,1024]{1,0:T(8,128)(2,1)S(1)} %pad_maximum_fusion), channel_id=1, source_target_pairs={{0,2},{1,3},{2,4},{3,5},{4,6},{5,7},{6,0},{7,1},{8,10},{9,11},{10,... | collective-permute-start | bytes 393224 | tf_op jit(solution)/shard_map/ppermute | solution.py:494
  130.7 5.6 %collective-permute-start.28 = (bf16[256,1024]{1,0:T(8,128)(2,1)S(1)}, bf16[256,1024]{1,0:T(8,128)(2,1)S(1)}, u32[]{:S(2)}, u32[]{:S(2)}) collective-permute-start(bf16[256,1024]{1,0:T(8,128)(2,1)S(1)} %constant_dynamic-update-slice_fusion.near_ref), channel_id=1, source_target_pairs={{0,1},{1,0},{2,3},{3,2},{4,5},{5,4},{6,7},{7,6},{8,9},{9,8},{10,11... | collective-permute-start | bytes 1572872 | tf_op jit(solution)/shard_map/ppermute | solution.py:498
  (5 other events, 3.3 us)

commit v2 on v1

v2 whole, which is shorter than its diff:
```python
import functools
import math

import jax
import jax.numpy as jnp
import numpy as np
from jax import lax
from jax.experimental import pallas as pl
from jax.experimental.pallas import tpu as pltpu
from jax.sharding import PartitionSpec as P

C = 96
COMPS = 16
WIDTH = C * COMPS
RH = 64
NB = 8
SPECIES = 89
K = 32
LAYERS = 3
ATOMS = 128
FACE = 32
GHOSTS = 192
TABLE = 320
PADDED = 384
HALF = 64
CUTOFF = 4.0
DEGREE = (0, 1, 1, 1, 2, 2, 2, 2, 2, 3, 3, 3, 3, 3, 3, 3)
STARTS = (0, 1, 4, 9)
WIDTHS = (1, 3, 5, 7)
STEP = 2
PAIRS = K // (2 * STEP)
PARTS = 3
WIDE = 16
STEPS = K // WIDE
ENV_ROW = 16
BASIS_ROW = 24
GEO_ROWS = 32

VMEM_LIMIT = 24 * 1024 * 1024
VMEM_MOST = 62 * 1024 * 1024

f32 = jnp.float32
bf16 = jnp.bfloat16
f8 = jnp.float8_e4m3fn


def dot(a, b):
    return lax.dot_general(a, b, (((1,), (0,)), ((), ())), preferred_element_type=f32)


def dot_tn(a, b):
    return lax.dot_general(a, b, (((0,), (0,)), ((), ())), preferred_element_type=f32)


def dot_nt(a, b):
    return lax.dot_general(a, b, (((1,), (1,)), ((), ())), preferred_element_type=f32)


def sigmoid(u):
    return 0.5 * jnp.tanh(0.5 * u) + 0.5


def silu(u):
    half = 0.5 * u
    return half * jnp.tanh(half) + half


def power_scale(largest):
    scale = jnp.ones_like(largest)
    inverse = jnp.ones_like(largest)
    for j in (64, 32, 16, 8, 4, 2, 1):
        up = largest * inverse > 224.0 * 2.0**j
        scale = jnp.where(up, scale * 2.0**j, scale)
        inverse = jnp.where(up, inverse * 2.0**-j, inverse)
    for j in (32, 16, 8, 4, 2, 1):
        down = largest * inverse * 2.0**j <= 448.0
        scale = jnp.where(down, scale * 2.0**-j, scale)
        inverse = jnp.where(down, inverse * 2.0**j, inverse)
    return scale, inverse


def harmonics(vx, vy, vz):
    x = vx * 0.5
    y = vy * 0.5
    z = vz * 0.5
    q = x * x + y * y + z * z
    zz = 5.0 * z * z - q
    return [
        jnp.ones_like(x),
        math.sqrt(3.0) * x,
        math.sqrt(3.0) * y,
        math.sqrt(3.0) * z,
        math.sqrt(15.0) * x * y,
        math.sqrt(15.0) * y * z,
        math.sqrt(5.0) / 2.0 * (3.0 * z * z - q),
        math.sqrt(15.0) * x * z,
        math.sqrt(15.0) / 2.0 * (x * x - y * y),
        math.sqrt(35.0 / 8.0) * y * (3.0 * x * x - y * y),
        math.sqrt(105.0) * x * y * z,
        math.sqrt(21.0 / 8.0) * y * zz,
        math.sqrt(7.0) / 2.0 * z * (5.0 * z * z - 3.0 * q),
        math.sqrt(21.0 / 8.0) * x * zz,
        math.sqrt(105.0) / 2.0 * z * (x * x - y * y),
        math.sqrt(35.0 / 8.0) * x * (x * x - 3.0 * y * y),
    ]


def params(semantics=None, limit=VMEM_LIMIT):
    return pltpu.CompilerParams(vmem_limit_bytes=limit, dimension_semantics=semantics)


def whole(*shape):
    return pl.BlockSpec(shape, lambda i: (0,) * len(shape))


def slots(*shape):
    return pl.BlockSpec((WIDE,) + shape, lambda i: (i,) + (0,) * len(shape))


def in_vmem(count):
    return [pl.BlockSpec(memory_space=pltpu.VMEM)] * count


def in_hbm(count):
    return [pl.BlockSpec(memory_space=pltpu.HBM)] * count


def like(array):
    return jax.ShapeDtypeStruct(array.shape, array.dtype)


AXES = ("gx", "gy", "gz")
BLOCKS = 6
SENT = (3, 5, 2, 0, 1, 4)


def partner(index, count, turn):
    return (index + 1) % count if index % 2 == turn else (index - 1) % count


def parity(axis_number):
    return lax.axis_index(AXES[axis_number]) % 2


def pick_kernel(lists_hbm, rows_hbm, sel_ref, *refs):
    out_refs = refs[:BLOCKS]
    lists_ref, rows_ref, sems = refs[BLOCKS:]
    rows_copy = pltpu.make_async_copy(rows_hbm, rows_ref, sems.at[0])
    rows_copy.start()
    lists_copy = pltpu.make_async_copy(lists_hbm, lists_ref, sems.at[1])
    lists_copy.start()
    lists_copy.wait()
    lists = jnp.concatenate(
        [lists_ref[i, j, k : k + 1, :] for i in (0, 1) for j in (0, 1) for k in (0, 1)], axis=0
    )
    entry = lax.broadcasted_iota(jnp.int32, (8, GHOSTS), 0)
    lane = lax.broadcasted_iota(jnp.int32, (8, GHOSTS), 1)
    spread = dot(lists.astype(f32).astype(bf16), (entry == lane % 8).astype(f32).astype(bf16))
    block, quarter = lane // FACE, (lane // 8) % 4
    odd = jnp.where(block < 2, parity(0), jnp.where(block < 4, parity(1), parity(2)))
    side = jnp.where(block % 2 == odd, 1, 0)
    high, low = quarter // 2, quarter % 2
    octant = jnp.where(
        block < 2, 4 * side + quarter, jnp.where(block < 4, 4 * high + 2 * side + low, 2 * quarter + side)
    )
    chosen = jnp.sum(jnp.where(entry == octant, spread, 0.0), axis=0, keepdims=True)
    atom = lax.broadcasted_iota(jnp.int32, (ATOMS, GHOSTS), 0)
    turned_sel = (atom == chosen.astype(jnp.int32)).astype(f32)
    sel = turned_sel.T.astype(bf16)
    sel_ref[...] = sel
    rows_copy.wait()
    picked = dot(sel, rows_ref[...]).astype(bf16)
    for number, out_ref in enumerate(out_refs):
        out_ref[...] = picked[number * FACE : (number + 1) * FACE]


def pick(lists, rows):
    return pl.pallas_call(
        pick_kernel,
        grid=(1,),
        in_specs=in_hbm(2),
        out_specs=[whole(GHOSTS, ATOMS)] + [whole(FACE, WIDTH)] * BLOCKS,
        out_shape=[jax.ShapeDtypeStruct((GHOSTS, ATOMS), bf16)]
        + [jax.ShapeDtypeStruct((FACE, WIDTH), bf16)] * BLOCKS,
        scratch_shapes=[
            pltpu.VMEM(lists.shape, jnp.int32),
            pltpu.VMEM(rows.shape, bf16),
            pltpu.SemaphoreType.DMA((2,)),
        ],
        compiler_params=params(),
        name="pick",
    )(lists, rows)


def geometry_into(vec_ref, count_ref, geo_ref):
    sharpness = ((NB - 1) / CUTOFF) ** 2
    centers = lax.broadcasted_iota(jnp.int32, (NB, ATOMS), 0).astype(f32) * (CUTOFF / (NB - 1))

    def one_slot(k, carry):
        vx = vec_ref[0, pl.ds(k, 1), :]
        vy = vec_ref[1, pl.ds(k, 1), :]
        vz = vec_ref[2, pl.ds(k, 1), :]
        square = vx * vx + vy * vy + vz * vz
        shape = 1.0 - square / (CUTOFF * CUTOFF)
        valid = (k < count_ref[...]).astype(f32)
        envelope = shape * shape * valid * (K ** (-0.5))
        radius = jnp.sqrt(square)
        offset = radius - centers
        for m, value in enumerate(harmonics(vx, vy, vz)):
            geo_ref[k, m : m + 1, :] = value
        geo_ref[k, ENV_ROW:BASIS_ROW, :] = jnp.broadcast_to(envelope, (8, ATOMS))
        geo_ref[k, BASIS_ROW:GEO_ROWS, :] = jnp.exp(-sharpness * offset * offset)
        return carry

    lax.fori_loop(0, K, one_slot, 0, unroll=4)


PACK_OUT = 0
PACK_MIX = 192
PACK_GATE = 576
PACK_MID = 672
PACK_EMB = 736
PACK_IN = 800
PACK_LAYER = 816
PACK_PROJ = LAYERS * PACK_LAYER
PACK_PROBE_IN = PACK_PROJ + 256
PACK_PROBE_MID = PACK_PROBE_IN + 16
PACK_ROWS = PACK_PROBE_MID + 64
WEIGHTS = 9


def pack_weights(refs, pack_ref):
    win_ref, wemb_ref, wmid_ref, wout_ref, mix_ref, gate_ref, proj_ref, pin_ref, pmid_ref = refs

    def put(at, value):
        pack_ref[at : at + value.shape[0], : value.shape[1]] = value

    def padded(value):
        return jnp.concatenate([value, jnp.zeros_like(value)], axis=0)

    for t in range(LAYERS):
        base = t * PACK_LAYER
        for j in range(3):
            put(base + PACK_OUT + RH * j, wout_ref[t, :, 128 * j : 128 * (j + 1)])
        for degree in range(4):
            put(base + PACK_MIX + C * degree, mix_ref[t, degree])
        put(base + PACK_GATE, gate_ref[t])
        put(base + PACK_MID, wmid_ref[t])
        put(base + PACK_EMB, wemb_ref[t])
        put(base + PACK_IN, padded(win_ref[t]))
    for degree in range(4):
        put(PACK_PROJ + RH * degree, proj_ref[degree])
    put(PACK_PROBE_IN, padded(pin_ref[...]))
    put(PACK_PROBE_MID, pmid_ref[...])


def hidden_into(t, species_ref, geo_ref, pack_ref, out_ref):
    base = t * PACK_LAYER
    wemb = pack_ref[base + PACK_EMB : base + PACK_EMB + RH, :SPECIES]
    win = pack_ref[base + PACK_IN : base + PACK_IN + 16, :RH][:NB]
    wmid = pack_ref[base + PACK_MID : base + PACK_MID + RH, :RH]
    ids = lax.broadcasted_iota(jnp.int32, (SPECIES, ATOMS), 0)
    emb = dot(wemb, (ids == species_ref[...]).astype(f32).astype(bf16))
    for k in range(0, K, 8):
        basis = jnp.concatenate([geo_ref[k + s, BASIS_ROW:GEO_ROWS, :] for s in range(8)], axis=1)
        hidden = dot_tn(win, basis.astype(bf16)) + jnp.concatenate([emb] * 8, axis=1)
        hidden = silu(hidden).astype(bf16)
        hidden = silu(dot_tn(wmid, hidden)).astype(bf16)
        for s in range(8):
            out_ref[k + s] = hidden[:, s * ATOMS : (s + 1) * ATOMS]


def prepare_kernel(*refs):
    inputs = refs[: 7 + WEIGHTS]
    turned_ref, ageo_ref, pgeo_ref, index_ref, hidden_ref, pack_ref = refs[7 + WEIGHTS : 13 + WEIGHTS]
    *landed, sems = refs[13 + WEIGHTS :]
    copies = [
        pltpu.make_async_copy(source, target, sems.at[number])
        for number, (source, target) in enumerate(zip(inputs, landed))
    ]
    for copy in copies:
        copy.start()
    avec_ref, acount_ref, rows_ref, old_ref, pvec_ref, pcount_ref, species_ref = landed[:7]
    copies[0].wait()
    copies[1].wait()
    geometry_into(avec_ref, acount_ref, ageo_ref)
    copies[2].wait()
    turned_ref[...] = rows_ref[...].astype(f32).T.astype(bf16)
    copies[3].wait()
    index = old_ref[...]
    block = (index - ATOMS) // FACE
    odd = jnp.where(block < 2, parity(0), jnp.where(block < 4, parity(1), parity(2)))
    moved = jnp.where(block % 2 == 0, index + FACE, index - FACE)
    index_ref[...] = jnp.where((index >= ATOMS) & (odd == 0), moved, index)
    copies[4].wait()
    copies[5].wait()
    geometry_into(pvec_ref, pcount_ref, pgeo_ref)
    for copy in copies[6:]:
        copy.wait()
    pack_weights(landed[7:], pack_ref)
    hidden_into(0, species_ref, ageo_ref, pack_ref, hidden_ref)


def prepare(inputs):
    outs = [
        jax.ShapeDtypeStruct((WIDTH, ATOMS), bf16),
        jax.ShapeDtypeStruct((K, GEO_ROWS, ATOMS), f32),
        jax.ShapeDtypeStruct((K, GEO_ROWS, ATOMS), f32),
        jax.ShapeDtypeStruct((K, ATOMS), jnp.int32),
        jax.ShapeDtypeStruct((K, RH, ATOMS), bf16),
        jax.ShapeDtypeStruct((PACK_ROWS, 128), bf16),
    ]
    return pl.pallas_call(
        prepare_kernel,
        grid=(1,),
        in_specs=in_hbm(7 + WEIGHTS),
        out_specs=[whole(*out.shape) for out in outs],
        out_shape=outs,
        scratch_shapes=[pltpu.VMEM(array.shape, array.dtype) for array in inputs]
        + [pltpu.SemaphoreType.DMA((7 + WEIGHTS,))],
        compiler_params=params(limit=VMEM_MOST),
        cost_estimate=pl.CostEstimate(flops=10_000_000, bytes_accessed=9_000_000, transcendentals=100_000),
        name="prepare",
    )(*inputs)


def hidden_kernel(t, species_ref, geo_ref, pack_ref, out_ref):
    hidden_into(t, species_ref, geo_ref, pack_ref, out_ref)


def hidden_units(t, species, geo, pack):
    return pl.pallas_call(
        functools.partial(hidden_kernel, t),
        grid=(1,),
        in_specs=[whole(1, ATOMS), whole(K, GEO_ROWS, ATOMS), whole(PACK_ROWS, 128)],
        out_specs=whole(K, RH, ATOMS),
        out_shape=jax.ShapeDtypeStruct((K, RH, ATOMS), bf16),
        compiler_params=params(),
        cost_estimate=pl.CostEstimate(
            flops=2 * 4096 * 256 * RH * 2, bytes_accessed=2_000_000, transcendentals=600_000
        ),
        name="hidden_units",
    )(species, geo, pack)


def layer_kernel(t, *refs):
    last = t == LAYERS - 1
    base = t * PACK_LAYER
    idx_ref, geo_ref, hidden_ref, turned_ref, sel_ref, pack_ref = refs[:6]
    ghost_refs = refs[6:12]
    out_refs = refs[12:-5]
    wout = jnp.concatenate(
        [pack_ref[base + PACK_OUT + RH * j : base + PACK_OUT + RH * (j + 1), :] for j in range(3)],
        axis=1,
    )
    table_ref, acc_ref, even_ref, odd_ref, rad_ref = refs[-5:]

    own = turned_ref[...].astype(f32)
    ghosts = jnp.concatenate([ghost_refs[SENT.index(b)][...] for b in range(BLOCKS)], axis=0)
    ghosts = ghosts.astype(f32).T
    scale, inverse = power_scale(
        jnp.maximum(
            jnp.max(jnp.abs(own), axis=(0, 1), keepdims=True),
            jnp.max(jnp.abs(ghosts), axis=(0, 1), keepdims=True),
        )
    )
    for at, part in ((0, own), (ATOMS, ghosts)):
        lanes = part.shape[1]
        part = part * inverse
        high = part.astype(f8)
        table_ref[:, at : at + lanes] = high
        low = part - high.astype(f32)
        table_ref[:, PADDED + at : PADDED + at + lanes] = low.astype(f8)
    for at in (TABLE, PADDED + TABLE):
        table_ref[:, at : at + PADDED - TABLE] = jnp.zeros((WIDTH, PADDED - TABLE), f8)

    def front(first, slot):
        hidden = jnp.concatenate([hidden_ref[first + s] for s in range(STEP)], axis=1)
        envelope = jnp.concatenate(
            [geo_ref[first + s, ENV_ROW : ENV_ROW + 1, :] for s in range(STEP)], axis=1
        )
        rad_ref[slot] = dot_tn(wout, hidden) * (envelope * scale)
        ids = lax.broadcasted_iota(jnp.int32, (PADDED, ATOMS), 0)
        hot = jnp.concatenate(
            [(ids == idx_ref[pl.ds(first + s, 1), :]).astype(f32) for s in range(STEP)], axis=1
        )
        hot = hot.astype(f8)
        return jnp.concatenate([hot, hot], axis=0)

    def back(first, got_ref, slot, keep, tiles):
        for tile in tiles:
            scalar = []
            weight = []
            for s in range(STEP):
                lanes = slice(s * ATOMS, (s + 1) * ATOMS)
                scalar.append(got_ref[tile : tile + 8, lanes])
                weight.append(
                    [rad_ref[slot, l * C + tile : l * C + tile + 8, lanes] for l in range(4)]
                )
            for m in range(COMPS):
                at = m * C + tile
                total = acc_ref[at : at + 8, :]
                for s in range(STEP):
                    if m == 0:
                        value = scalar[s]
                    else:
                        value = got_ref[at : at + 8, s * ATOMS : (s + 1) * ATOMS]
                        value = value + geo_ref[first + s, m : m + 1, :] * scalar[s]
                    total = total + weight[s][DEGREE[m]] * value
                acc_ref[at : at + 8, :] = total if keep is None else jnp.where(keep, total, 0.0)

    def one_step(first, slot, behind, keep):
        got_ref, behind_ref = (even_ref, odd_ref) if slot == 0 else (odd_ref, even_ref)
        hot = front(first, slot)
        for part in range(PARTS):
            back(behind, behind_ref, 1 - slot, keep, range(part * C // PARTS, (part + 1) * C // PARTS, 8))
            rows = slice(part * WIDTH // PARTS, (part + 1) * WIDTH // PARTS)
            got_ref[rows, :] = dot(table_ref[rows, :], hot)

    def two_steps(i, carry):
        first = i * (2 * STEP)
        one_step(first, 0, jnp.maximum(first - STEP, 0), i > 0)
        one_step(first + STEP, 1, first, None)
        return carry

    lax.fori_loop(0, PAIRS, two_steps, 0)
    back(K - STEP, odd_ref, 1, None, range(0, C, 8))

    message = [acc_ref[m * C : (m + 1) * C, :].astype(bf16) for m in range(COMPS)]
    gate = sigmoid(dot_tn(pack_ref[base + PACK_GATE : base + PACK_GATE + C, :C], message[0]))
    updated = []
    for degree in range(4):
        start, width = STARTS[degree], WIDTHS[degree]
        at = base + PACK_MIX + C * degree
        mixed = dot_tn(pack_ref[at : at + C, :C], jnp.concatenate(message[start : start + width], axis=1))
        for j in range(width):
            m = start + j
            part = mixed[:, j * ATOMS : (j + 1) * ATOMS]
            before = turned_ref[m * C : (m + 1) * C, :].astype(f32)
            change = silu(part) if degree == 0 else gate * part
            updated.append((before + change).astype(bf16))
    new = jnp.concatenate(updated, axis=0)
    sel = sel_ref[...]
    if not last:
        out_refs[0][...] = new
        picked = dot_nt(sel, new).astype(bf16)
        for face in range(6):
            out_refs[1 + face][...] = picked[face * FACE : (face + 1) * FACE]
    else:
        ones = (
            lax.broadcasted_iota(jnp.int32, (ATOMS, ATOMS), 0)
            == lax.broadcasted_iota(jnp.int32, (ATOMS, ATOMS), 1)
        ).astype(f32).astype(bf16)
        out_refs[0][...] = dot_nt(ones, new).astype(bf16)
        keys = jnp.concatenate(
            [
                dot(pack_ref[PACK_PROJ + RH * l : PACK_PROJ + RH * (l + 1), :C], updated[m])
                for m, l in enumerate(DEGREE)
            ],
            axis=0,
        ).astype(bf16)
        rows = dot_nt(jnp.concatenate([sel, ones], axis=0), keys).astype(bf16)
        for face in range(6):
            out_refs[1 + face][...] = rows[face * FACE : (face + 1) * FACE]
        out_refs[7][...] = rows[GHOSTS : GHOSTS + HALF]
        out_refs[8][...] = rows[GHOSTS + HALF :]


def layer(t, idx, geo, hidden, turned, sel, ghosts, pack):
    last = t == LAYERS - 1
    if last:
        shapes = [(ATOMS, WIDTH)] + [(FACE, COMPS * RH)] * 6 + [(HALF, COMPS * RH)] * 2
    else:
        shapes = [(WIDTH, ATOMS)] + [(FACE, WIDTH)] * 6
    lanes = STEP * ATOMS
    return pl.pallas_call(
        functools.partial(layer_kernel, t),
        grid=(1,),
        in_specs=[
            whole(K, ATOMS),
            whole(K, GEO_ROWS, ATOMS),
            whole(K, RH, ATOMS),
            whole(WIDTH, ATOMS),
            whole(GHOSTS, ATOMS),
            whole(PACK_ROWS, 128),
        ]
        + [whole(FACE, WIDTH)] * BLOCKS,
        out_specs=[whole(*shape) for shape in shapes],
        out_shape=[jax.ShapeDtypeStruct(shape, bf16) for shape in shapes],
        scratch_shapes=[
            pltpu.VMEM((WIDTH, 2 * PADDED), f8),
            pltpu.VMEM((WIDTH, ATOMS), f32),
            pltpu.VMEM((WIDTH, lanes), f32),
            pltpu.VMEM((WIDTH, lanes), f32),
            pltpu.VMEM((2, 4 * C, lanes), f32),
        ],
        compiler_params=params(limit=VMEM_LIMIT),
        cost_estimate=pl.CostEstimate(
            flops=2 * 4096 * 512 * WIDTH, bytes_accessed=3_000_000, transcendentals=600_000
        ),
        name="layer",
    )(idx, geo, hidden, turned, sel, pack, *[ghosts[b] for b in SENT])


def probe_weights_kernel(geo_ref, pack_ref, out_ref):
    win = pack_ref[PACK_PROBE_IN : PACK_PROBE_IN + 16, :RH][:NB]
    wmid = pack_ref[PACK_PROBE_MID : PACK_PROBE_MID + RH, :RH]
    basis = jnp.concatenate([geo_ref[s, BASIS_ROW:GEO_ROWS, :] for s in range(WIDE)], axis=1)
    hidden = silu(dot_tn(win, basis.astype(bf16))).astype(bf16)
    hidden = silu(dot_tn(wmid, hidden)).astype(bf16).astype(f32)
    for s in range(WIDE):
        scaled = hidden[:, s * ATOMS : (s + 1) * ATOMS] * geo_ref[s, ENV_ROW : ENV_ROW + 1, :]
        for m in range(COMPS):
            value = scaled if m == 0 else scaled * geo_ref[s, m : m + 1, :]
            out_ref[s, m * RH : (m + 1) * RH, :] = value.astype(bf16)


def probe_weights(geo, pack):
    return pl.pallas_call(
        probe_weights_kernel,
        grid=(STEPS,),
        in_specs=[slots(GEO_ROWS, ATOMS), whole(PACK_ROWS, 128)],
        out_specs=slots(COMPS * RH, ATOMS),
        out_shape=jax.ShapeDtypeStruct((K, COMPS * RH, ATOMS), bf16),
        compiler_params=params(("arbitrary",)),
        cost_estimate=pl.CostEstimate(
            flops=2 * 4096 * 256 * WIDTH, bytes_accessed=9_000_000, transcendentals=600_000
        ),
        name="probe_weights",
    )(geo, pack)


HOLDERS = (2, 3, 4, 5, 5, 4)


def column_root(slab_ref):
    return slab_ref[lax.axis_index("gx") * lax.axis_size("gy") + lax.axis_index("gy")]


def collect_kernel(slab_ref, *refs):
    *block_refs, low_ref, high_ref, out_ref = refs
    code = lax.axis_index("gz") ^ column_root(slab_ref)

    @pl.when(code == 0)
    def _():
        out_ref[...] = low_ref[...]

    @pl.when(code == 1)
    def _():
        out_ref[...] = high_ref[...]

    for block, holder in enumerate(HOLDERS):
        at = FACE if block >= 4 else 0

        @pl.when(code == holder)
        def _(block=block, at=at):
            out_ref[at : at + FACE, :] = block_refs[SENT.index(block)][...]

    @pl.when((code == 2) | (code == 3))
    def _():
        out_ref[FACE:, :] = jnp.zeros((HALF - FACE, COMPS * RH), bf16)

    @pl.when(code > 5)
    def _():
        out_ref[...] = jnp.zeros_like(out_ref)


def collect(slab, blocks, low, high):
    return pl.pallas_call(
        collect_kernel,
        in_specs=[pl.BlockSpec(memory_space=pltpu.SMEM)] + in_vmem(BLOCKS + 2),
        out_specs=pl.BlockSpec(memory_space=pltpu.VMEM),
        out_shape=jax.ShapeDtypeStruct((HALF, COMPS * RH), bf16),
        compiler_params=params(),
        name="collect",
    )(slab, *[blocks[b] for b in SENT], low, high)


def readout_kernel(slab_ref, idx_ref, weight_ref, near_ref, far_ref, out_ref, keys_ref, acc_ref):
    step = pl.program_id(0)

    @pl.when(step == 0)
    def _():
        root = column_root(slab_ref)
        code = lax.axis_index("gz") ^ root

        def fetch(at, rows, holder, start):
            place = code ^ holder
            start = pl.multiple_of(place // 2 * HALF + start, FACE)

            @pl.when(place % 2 == 0)
            def _():
                keys_ref[pl.ds(at, rows), :] = near_ref[pl.ds(start, rows), :]

            @pl.when(place % 2 == 1)
            def _():
                keys_ref[pl.ds(at, rows), :] = far_ref[pl.ds(start, rows), :]

        fetch(0, HALF, 0, 0)
        fetch(HALF, HALF, 1, 0)
        for block, holder in enumerate(HOLDERS):
            odd = (parity(0), parity(1), root % 2)[block // 2]
            face = jnp.where(odd == block % 2, block // 2 * 2 + 1, block // 2 * 2)
            at = pl.multiple_of(ATOMS + face * FACE, FACE)
            fetch(at, FACE, holder, FACE if block >= 4 else 0)
        acc_ref[...] = jnp.zeros_like(acc_ref)

    weight = jnp.concatenate([weight_ref[s] for s in range(WIDE)], axis=1)
    product = dot(keys_ref[...], weight)
    rows = lax.broadcasted_iota(jnp.int32, (TABLE, ATOMS), 0)
    total = acc_ref[...]
    for s in range(WIDE):
        chosen = rows == idx_ref[pl.ds(step * WIDE + s, 1), :]
        part = jnp.where(chosen, product[:, s * ATOMS : (s + 1) * ATOMS], 0.0)
        total = total + jnp.sum(part.reshape(TABLE // 8, 8, ATOMS), axis=0)
    acc_ref[...] = total

    @pl.when(step == STEPS - 1)
    def _():
        out_ref[...] = jnp.sum(acc_ref[...], axis=0, keepdims=True)


def readout(slab, idx, weight, near, far):
    return pl.pallas_call(
        readout_kernel,
        grid=(STEPS,),
        in_specs=[
            pl.BlockSpec(memory_space=pltpu.SMEM),
            whole(K, ATOMS),
            slots(COMPS * RH, ATOMS),
            whole(4 * HALF, COMPS * RH),
            whole(4 * HALF, COMPS * RH),
        ],
        out_specs=whole(1, ATOMS),
        scratch_shapes=[pltpu.VMEM((TABLE, COMPS * RH), bf16), pltpu.VMEM((8, ATOMS), f32)],
        out_shape=jax.ShapeDtypeStruct((1, ATOMS), f32),
        compiler_params=params(("arbitrary",)),
        name="readout",
    )(slab, idx, weight, near, far)


def exchange(blocks):
    landed = [None] * BLOCKS
    for block in SENT:
        axis, turn = AXES[block // 2], block % 2
        count = lax.axis_size(axis)
        pairs = [(i, partner(i, count, turn)) for i in range(count)]
        landed[block] = lax.ppermute(blocks[block], axis, pairs)
    return landed


def along_column(block, code):
    return lax.ppermute(block, "gz", [(i, i ^ code) for i in range(lax.axis_size("gz"))])


def column_keys(slab, blocks, low, high, probe_weight):
    landed = [None] * BLOCKS
    inner = lax.axis_size("gz")
    for block in SENT:
        axis, turn, holder = AXES[block // 2], block % 2, HOLDERS[block]
        outer = lax.axis_size(axis)
        if axis == "gz":
            pairs = [(i, partner(i, inner, turn) ^ holder) for i in range(inner)]
            landed[block] = lax.ppermute(blocks[block], axis, pairs)
        else:
            pairs = [
                (i * inner + j, partner(i, outer, turn) * inner + (j ^ holder))
                for i in range(outer)
                for j in range(inner)
            ]
            landed[block] = lax.ppermute(blocks[block], (axis, "gz"), pairs)
    mine = collect(slab, landed, low, along_column(high, 1))
    moved = [along_column(mine, code) for code in (6, 4, 2)][::-1]
    *moved, probe_weight = lax.optimization_barrier((*moved, probe_weight))
    near = jnp.concatenate([mine] + moved, axis=0)
    return near, along_column(near, 1), probe_weight


def local(
    features,
    species,
    octant_lists,
    neighbour_index,
    neighbour_count,
    edge_vectors,
    radial_in,
    species_emb,
    radial_mid,
    radial_out,
    mix_weight,
    gate_weight,
    probe_in,
    probe_mid,
    probe_proj,
    probe_vectors,
    probe_index,
    probe_count,
    slab_index,
):
    sel, *blocks = pick(octant_lists, features)
    ghosts = exchange(blocks)
    species_row = species.reshape(1, ATOMS)
    turned, geo, probe_geo, index, hidden, pack = prepare(
        (
            edge_vectors,
            neighbour_count.reshape(1, ATOMS),
            features,
            neighbour_index,
            probe_vectors,
            probe_count.reshape(1, ATOMS),
            species_row,
            radial_in,
            jnp.swapaxes(species_emb, 1, 2),
            radial_mid,
            radial_out,
            mix_weight,
            gate_weight,
            jnp.swapaxes(probe_proj, 1, 2),
            probe_in,
            probe_mid,
        )
    )
    for t in range(LAYERS):
        if t > 0:
            hidden = hidden_units(t, species_row, geo, pack)
        outs = layer(t, index, geo, hidden, turned, sel, ghosts, pack)
        if t < LAYERS - 1:
            turned = outs[0]
            ghosts = exchange(outs[1:])
    near, far, probe_weight = column_keys(
        slab_index, outs[1:7], outs[7], outs[8], probe_weights(probe_geo, pack)
    )
    density = readout(slab_index, probe_index, probe_weight, near, far)
    return (outs[0], density.reshape(ATOMS))


def solution(mesh):
    in_specs = (
        P(("gx", "gy", "gz"), None),
        P(("gx", "gy", "gz")),
        P(None, None, None, ("gx", "gy", "gz")),
        P(None, ("gx", "gy", "gz")),
        P(("gx", "gy", "gz")),
        P(None, None, ("gx", "gy", "gz")),
        P(),
        P(),
        P(),
        P(),
        P(),
        P(),
        P(),
        P(),
        P(),
        P(None, None, ("gx", "gy", "gz")),
        P(None, ("gx", "gy", "gz")),
        P(("gx", "gy", "gz")),
        P(),
    )
    out_specs = (P(("gx", "gy", "gz"), None), P(("gx", "gy", "gz")))
    return jax.shard_map(local, mesh=mesh, in_specs=in_specs, out_specs=out_specs, check_vma=False)
```

time: 142 us -> 130 us (0.915)
  waiting for transfers between devices: 11.2 us -> 18.2 us
  starting transfers between devices: 66.8 us -> 59.9 us
  local copies, waits for them, and re-layouts: 12.5 us -> 6.6 us
  Pallas kernels: 47.4 us -> 43.9 us
  between operations: 3.66 us -> 0.81 us
    ppermute x29, waiting for transfers between devices: 11.2 us -> 18.2 us  [the longest x5 8.89 us: along_column(): lax.ppermute(block, 'gz', [(i, i ^ code) for i in range(lax.axis_size('gz...]
    ppermute x29, starting transfers between devices: 66.8 us -> 59.9 us  [the longest x18 40.4 us: exchange(): landed[block] = lax.ppermute(blocks[block], axis, pairs)]
    unnamed x50 -> x28, local copies, waits for them, and re-layouts: 11.9 us -> 6.6 us
    pallas_call x1, Pallas kernels: 4.12 us -> 2.19 us  [probe_weights(): pl.pallas_call(probe_weights_kernel, grid=(STEPS,), in_specs=[slots(GEO_R...]
    pallas_call x9, Pallas kernels: 43.3 us -> 41.7 us  [the longest x3 29.8 us: layer(): pl.pallas_call(functools.partial(layer_kernel, t), grid=(1,), in_specs=[w...]
  transfers between devices with their start and end apart: 29 -> 29, of which waited for: 7 -> 10; matrix products, arithmetic and copies ran while one was open for 0% -> 0% of each run, Pallas kernels for 6% -> 7%
where the time goes in v2:
time: 130 us
  starting transfers between devices  59.9 us (46%)
  Pallas kernels  43.9 us (34%)
  waiting for transfers between devices  18.2 us (14%)
  local copies, waits for them, and re-layouts  6.6 us (5%)
    ppermute x18, starting transfers between devices, exchange(): landed[block] = lax.ppermute(blocks[block], axis, pairs)  40.4 us
    pallas_call x3, Pallas kernels, layer(): pl.pallas_call(functools.partial(layer_kernel, t), grid=(1,), in_specs=[w...  29.8 us
    ppermute x4, starting transfers between devices, column_keys(): landed[block] = lax.ppermute(blocks[block], (axis, 'gz'), pairs)  14.4 us
    ppermute x5, waiting for transfers between devices, along_column(): lax.ppermute(block, 'gz', [(i, i ^ code) for i in range(lax.axis_size('gz...  8.89 us
    unnamed x28, local copies, waits for them, and re-layouts  6.6 us
    ppermute x5, starting transfers between devices, along_column(): lax.ppermute(block, 'gz', [(i, i ^ code) for i in range(lax.axis_size('gz...  4.6 us
    pallas_call x1, Pallas kernels, readout(): pl.pallas_call(readout_kernel, grid=(STEPS,), in_specs=[pl.BlockSpec(memo...  4.36 us
    pallas_call x1, Pallas kernels, prepare(): pl.pallas_call(prepare_kernel, grid=(1,), in_specs=in_hbm(7 + WEIGHTS), o...  4.21 us
  transfers between devices with their start and end apart: 29, of which 10 were waited for; matrix products, arithmetic and copies ran while one was open for 0% of the time, Pallas kernels for 7%

profile of v2, /device:TPU:1, one launch (start us, length us, event | category | flops | bytes accessed | tf_op | source)
XLA Modules:
  0.0 129.5 jit_solution(8869314948526696594)
XLA Ops:
  0.6 1.0 copy-done.4
  1.6 0.7 copy-done.7
  2.3 0.7 pick.1
  3.1 10.3 %collective-permute-start = (bf16[32,1536]{1,0:T(8,128)(2,1)S(1)}, bf16[32,1536]{1,0:T(8,128)(2,1)S(1)}, u32[]{:S(2)}, u32[]{:S(2)}) collective-permute-start(bf16[32,1536]{1,0:T(8,128)(2,1)S(1)} %get-tuple-element.48), channel_id=1, source_target_pairs={{0,56},{8,16},{16,8},{24,32},{32,24},{40,48},{48,40},{56,0},{1,57}... | collective-permute-start | bytes 294920 | tf_op jit(solution)/shard_map/ppermute | solution.py:648
  13.3 1.6 %collective-permute-start.1 = (bf16[32,1536]{1,0:T(8,128)(2,1)S(1)}, bf16[32,1536]{1,0:T(8,128)(2,1)S(1)}, u32[]{:S(2)}, u32[]{:S(2)}) collective-permute-start(bf16[32,1536]{1,0:T(8,128)(2,1)S(1)} %get-tuple-element.49), channel_id=1, source_target_pairs={{0,7},{1,2},{2,1},{3,4},{4,3},{5,6},{6,5},{7,0},{8,15},{9,10},{10,... | collective-permute-start | bytes 294920 | tf_op jit(solution)/shard_map/ppermute | solution.py:648
  14.9 1.2 collective-permute-start.3
  16.1 1.8 %collective-permute-start.4 = (bf16[32,1536]{1,0:T(8,128)(2,1)S(1)}, bf16[32,1536]{1,0:T(8,128)(2,1)S(1)}, u32[]{:S(2)}, u32[]{:S(2)}) collective-permute-start(bf16[32,1536]{1,0:T(8,128)(2,1)S(1)} %get-tuple-element.52), channel_id=1, source_target_pairs={{0,192},{64,128},{128,64},{192,0},{1,193},{65,129},{129,65},{193,1... | collective-permute-start | bytes 294920 | tf_op jit(solution)/shard_map/ppermute | solution.py:648
  17.9 1.0 collective-permute-start.5
  19.0 4.2 %prepare.1 = (bf16[1536,128]{1,0:T(8,128)(2,1)}, f32[32,32,128]{2,1,0:T(8,128)}, f32[32,32,128]{2,1,0:T(8,128)}, s32[32,128]{1,0:T(8,128)}, bf16[32,64,128]{2,1,0:T(8,128)(2,1)}, /*index=5*/bf16[2784,128]{1,0:T(8,128)(2,1)}) custom-call(f32[3,32,128]{2,1,0:T(8,128)} %refs_0_.1, s32[1,128]{1,0:T(1,128)} %bitcast.11, bf16[128,1536]{1,0:T(8,128)(2,1)} %rows_hbm.1, ...), custom_call_target="tpu_custom_call" | custom-call | flops 10000000 | bytes 9000000 | tf_op jit(solution)/shard_map/prepare/pallas_call | solution.py:313
  23.3 1.1 copy-done
  24.4 1.0 copy-done.2
  25.4 1.0 copy-done.10
  26.4 1.0 copy-done.11
  27.4 0.7 copy-done.12
  28.2 9.7 %layer.3 = (bf16[1536,128]{1,0:T(8,128)(2,1)S(1)}, bf16[32,1536]{1,0:T(8,128)(2,1)S(1)}, bf16[32,1536]{1,0:T(8,128)(2,1)S(1)}, bf16[32,1536]{1,0:T(8,128)(2,1)S(...) custom-call(s32[32,128]{1,0:T(8,128)S(1)} %copy-done.12, ...), custom_call_target="tpu_custom_call" | custom-call | flops 6442450944 | bytes 3000000 | tf_op jit(solution)/shard_map/layer/pallas_call | solution.py:476
  37.9 8.2 %collective-permute-start.6 = (bf16[32,1536]{1,0:T(8,128)(2,1)S(1)}, bf16[32,1536]{1,0:T(8,128)(2,1)S(1)}, u32[]{:S(2)}, u32[]{:S(2)}) collective-permute-start(bf16[32,1536]{1,0:T(8,128)(2,1)S(1)} %get-tuple-element.55), channel_id=1, source_target_pairs={{0,56},{8,16},{16,8},{24,32},{32,24},{40,48},{48,40},{56,0},{1,57}... | collective-permute-start | bytes 294920 | tf_op jit(solution)/shard_map/ppermute | solution.py:648
  46.1 1.4 %collective-permute-start.7 = (bf16[32,1536]{1,0:T(8,128)(2,1)S(1)}, bf16[32,1536]{1,0:T(8,128)(2,1)S(1)}, u32[]{:S(2)}, u32[]{:S(2)}) collective-permute-start(bf16[32,1536]{1,0:T(8,128)(2,1)S(1)} %get-tuple-element.56), channel_id=1, source_target_pairs={{0,7},{1,2},{2,1},{3,4},{4,3},{5,6},{6,5},{7,0},{8,15},{9,10},{10,... | collective-permute-start | bytes 294920 | tf_op jit(solution)/shard_map/ppermute | solution.py:648
  47.5 1.2 collective-permute-start.9
  48.7 1.8 %collective-permute-start.10 = (bf16[32,1536]{1,0:T(8,128)(2,1)S(1)}, bf16[32,1536]{1,0:T(8,128)(2,1)S(1)}, u32[]{:S(2)}, u32[]{:S(2)}) collective-permute-start(bf16[32,1536]{1,0:T(8,128)(2,1)S(1)} %get-tuple-element.59), channel_id=1, source_target_pairs={{0,192},{64,128},{128,64},{192,0},{1,193},{65,129},{129,65},{193,1... | collective-permute-start | bytes 294920 | tf_op jit(solution)/shard_map/ppermute | solution.py:648
  50.5 1.0 hidden_units.3.refs_2_
  51.5 2.2 %collective-permute-done.7.refs_7_ = bf16[32,1536]{1,0:T(8,128)(2,1)S(1)} collective-permute-done((bf16[32,1536]{1,0:T(8,128)(2,1)S(1)}, bf16[32,1536]{1,0:T(8,128)(2,1)S(1)}, u32[]{:S(2)}, u32[]{:S(2)}) %collective-permute-start.7) | collective-permute-done | bytes 98336 | tf_op jit(solution)/shard_map/ppermute | solution.py:648
  53.7 0.3 collective-permute-done.10.refs_10_
  54.1 9.7 %layer.4 = (bf16[1536,128]{1,0:T(8,128)(2,1)S(1)}, bf16[32,1536]{1,0:T(8,128)(2,1)S(1)}, bf16[32,1536]{1,0:T(8,128)(2,1)S(1)}, bf16[32,1536]{1,0:T(8,128)(2,1)S(...) custom-call(s32[32,128]{1,0:T(8,128)S(1)} %copy-done.13, ...), custom_call_target="tpu_custom_call" | custom-call | flops 6442450944 | bytes 3000000 | tf_op jit(solution)/shard_map/layer/pallas_call | solution.py:476
  63.8 5.3 %collective-permute-start.12 = (bf16[32,1536]{1,0:T(8,128)(2,1)S(1)}, bf16[32,1536]{1,0:T(8,128)(2,1)S(1)}, u32[]{:S(2)}, u32[]{:S(2)}) collective-permute-start(bf16[32,1536]{1,0:T(8,128)(2,1)S(1)} %get-tuple-element.62), channel_id=1, source_target_pairs={{0,56},{8,16},{16,8},{24,32},{32,24},{40,48},{48,40},{56,0},{1,57}... | collective-permute-start | bytes 294920 | tf_op jit(solution)/shard_map/ppermute | solution.py:648
  69.1 2.4 %collective-permute-start.13 = (bf16[32,1536]{1,0:T(8,128)(2,1)S(1)}, bf16[32,1536]{1,0:T(8,128)(2,1)S(1)}, u32[]{:S(2)}, u32[]{:S(2)}) collective-permute-start(bf16[32,1536]{1,0:T(8,128)(2,1)S(1)} %get-tuple-element.63), channel_id=1, source_target_pairs={{0,7},{1,2},{2,1},{3,4},{4,3},{5,6},{6,5},{7,0},{8,15},{9,10},{10,... | collective-permute-start | bytes 294920 | tf_op jit(solution)/shard_map/ppermute | solution.py:648
  71.6 1.2 collective-permute-start.15
  72.8 1.8 %collective-permute-start.16 = (bf16[32,1536]{1,0:T(8,128)(2,1)S(1)}, bf16[32,1536]{1,0:T(8,128)(2,1)S(1)}, u32[]{:S(2)}, u32[]{:S(2)}) collective-permute-start(bf16[32,1536]{1,0:T(8,128)(2,1)S(1)} %get-tuple-element.66), channel_id=1, source_target_pairs={{0,192},{64,128},{128,64},{192,0},{1,193},{65,129},{129,65},{193,1... | collective-permute-start | bytes 294920 | tf_op jit(solution)/shard_map/ppermute | solution.py:648
  74.6 1.0 collective-permute-start.17
  75.6 1.0 hidden_units.2.refs_2_
  76.7 0.7 collective-permute-done.13.refs_7_
  77.4 0.1 collective-permute-done.16.refs_10_
  77.5 10.4 %layer.5 = (bf16[128,1536]{1,0:T(8,128)(2,1)}, bf16[32,1024]{1,0:T(8,128)(2,1)S(1)}, bf16[32,1024]{1,0:T(8,128)(2,1)S(1)}, bf16[32,1024]{1,0:T(8,128)(2,1)S(1)},...) custom-call(s32[32,128]{1,0:T(8,128)S(1)} %copy-done.13, ...), custom_call_target="tpu_custom_call" | custom-call | flops 6442450944 | bytes 3000000 | tf_op jit(solution)/shard_map/layer/pallas_call | solution.py:476
  87.9 7.8 %collective-permute-start.18 = (bf16[32,1024]{1,0:T(8,128)(2,1)S(1)}, bf16[32,1024]{1,0:T(8,128)(2,1)S(1)}, u32[]{:S(2)}, u32[]{:S(2)}) collective-permute-start(bf16[32,1024]{1,0:T(8,128)(2,1)S(1)} %get-tuple-element.69), channel_id=1, source_target_pairs={{0,61},{1,60},{2,63},{3,62},{4,57},{5,56},{6,59},{7,58},{8,21},{9,... | collective-permute-start | bytes 196616 | tf_op jit(solution)/shard_map/ppermute | solution.py:671
  95.7 0.6 collective-permute-start.19
  96.3 2.5 %collective-permute-start.21 = (bf16[32,1024]{1,0:T(8,128)(2,1)S(1)}, bf16[32,1024]{1,0:T(8,128)(2,1)S(1)}, u32[]{:S(2)}, u32[]{:S(2)}) collective-permute-start(bf16[32,1024]{1,0:T(8,128)(2,1)S(1)} %get-tuple-element.72), channel_id=1, source_target_pairs={{0,66},{1,67},{2,64},{3,65},{4,70},{5,71},{6,68},{7,69},{64,2},{65... | collective-permute-start | bytes 196616 | tf_op jit(solution)/shard_map/ppermute | solution.py:671
  98.8 4.1 %collective-permute-start.22 = (bf16[32,1024]{1,0:T(8,128)(2,1)S(1)}, bf16[32,1024]{1,0:T(8,128)(2,1)S(1)}, u32[]{:S(2)}, u32[]{:S(2)}) collective-permute-start(bf16[32,1024]{1,0:T(8,128)(2,1)S(1)} %get-tuple-element.73), channel_id=1, source_target_pairs={{0,195},{1,194},{2,193},{3,192},{4,199},{5,198},{6,197},{7,196},{6... | collective-permute-start | bytes 196616 | tf_op jit(solution)/shard_map/ppermute | solution.py:671
  102.9 0.6 collective-permute-done.21.refs_3_
  103.5 2.5 %collective-permute-done.22.refs_4_ = bf16[32,1024]{1,0:T(8,128)(2,1)S(1)} collective-permute-done((bf16[32,1024]{1,0:T(8,128)(2,1)S(1)}, bf16[32,1024]{1,0:T(8,128)(2,1)S(1)}, u32[]{:S(2)}, u32[]{:S(2)}) %collective-permute-start.22) | collective-permute-done | bytes 65568 | tf_op jit(solution)/shard_map/ppermute | solution.py:671
  106.0 2.8 %collective-permute-done.23.refs_5_ = bf16[32,1024]{1,0:T(8,128)(2,1)S(1)} collective-permute-done((bf16[32,1024]{1,0:T(8,128)(2,1)S(1)}, bf16[32,1024]{1,0:T(8,128)(2,1)S(1)}, u32[]{:S(2)}, u32[]{:S(2)}) %collective-permute-start.23) | collective-permute-done | bytes 65568 | tf_op jit(solution)/shard_map/ppermute | solution.py:664
  108.8 0.6 collect.1
  109.4 1.9 %collective-permute-start.27 = (bf16[64,1024]{1,0:T(8,128)(2,1)S(1)}, bf16[64,1024]{1,0:T(8,128)(2,1)S(1)}, u32[]{:S(2)}, u32[]{:S(2)}) collective-permute-start(bf16[64,1024]{1,0:T(8,128)(2,1)S(1)} %collect.1), channel_id=1, source_target_pairs={{0,6},{1,7},{2,4},{3,5},{4,2},{5,3},{6,0},{7,1},{8,14},{9,15},{10,... | collective-permute-start | bytes 393224 | tf_op jit(solution)/shard_map/ppermute | solution.py:653
  111.3 1.7 %collective-permute-start.25 = (bf16[64,1024]{1,0:T(8,128)(2,1)S(1)}, bf16[64,1024]{1,0:T(8,128)(2,1)S(1)}, u32[]{:S(2)}, u32[]{:S(2)}) collective-permute-start(bf16[64,1024]{1,0:T(8,128)(2,1)S(1)} %collect.1), channel_id=1, source_target_pairs={{0,2},{1,3},{2,0},{3,1},{4,6},{5,7},{6,4},{7,5},{8,10},{9,11},{10,... | collective-permute-start | bytes 393224 | tf_op jit(solution)/shard_map/ppermute | solution.py:653
  113.1 2.2 %probe_weights.1.weight_ref = bf16[32,1024,128]{2,1,0:T(8,128)(2,1)S(1)} custom-call(f32[32,32,128]{2,1,0:T(8,128)S(1)} %copy-done.9, bf16[2784,128]{1,0:T(8,128)(2,1)S(1)} %copy-done.1), custom_call_target="tpu_custom_call" | custom-call | flops 3221225472 | bytes 9000000 | tf_op jit(solution)/shard_map/probe_weights/pallas_call | solution.py:519
  115.3 0.3 collective-permute-done.27
  115.6 7.1 %collective-permute-done.26 = bf16[64,1024]{1,0:T(8,128)(2,1)S(1)} collective-permute-done((bf16[64,1024]{1,0:T(8,128)(2,1)S(1)}, bf16[64,1024]{1,0:T(8,128)(2,1)S(1)}, u32[]{:S(2)}, u32[]{:S(2)}) %collective-permute-start.26) | collective-permute-done | bytes 131104 | tf_op jit(solution)/shard_map/ppermute | solution.py:653
  122.7 1.0 collective-permute-start.28
  123.6 1.5 %collective-permute-done.28.far_ref = bf16[256,1024]{1,0:T(8,128)(2,1)S(1)} collective-permute-done((bf16[256,1024]{1,0:T(8,128)(2,1)S(1)}, bf16[256,1024]{1,0:T(8,128)(2,1)S(1)}, u32[]{:S(2)}, u32[]{:S(2)}) %collective-permute-start.28) | collective-permute-done | bytes 524320 | tf_op jit(solution)/shard_map/ppermute | solution.py:653
  125.2 4.4 %readout.1 = f32[1,128]{1,0:T(1,128)} custom-call(s32[32]{0:T(128)S(1)} %copy-done.8, s32[32,128]{1,0:T(8,128)S(1)} %copy-done.5, bf16[32,1024,128]{2,1,0:T(8,128)(2,1)S(1)} %probe_weights.1.weight_ref, bf16[256,1024]{1,0:T(8,128)(2,1)S(1)} %pad_maximum_fusion.near_ref, bf16[256,1024]{1,0:T(8,128)(2,1)S(1)} %collective-permute-done.28.far_ref), custom_call_target="tpu_custom_call" | custom-call | tf_op jit(solution)/shard_map/readout/pallas_call | solution.py:624
  (49 shorter events, 0.1 us)
Async XLA Ops:
  0.6 1.0 copy-start.4
  1.6 0.7 copy-start.7
  3.1 14.9 %collective-permute-start = (bf16[32,1536]{1,0:T(8,128)(2,1)S(1)}, bf16[32,1536]{1,0:T(8,128)(2,1)S(1)}, u32[]{:S(2)}, u32[]{:S(2)}) collective-permute-start(bf16[32,1536]{1,0:T(8,128)(2,1)S(1)} %get-tuple-element.48), channel_id=1, source_target_pairs={{0,56},{8,16},{16,8},{24,32},{32,24},{40,48},{48,40},{56,0},{1,57}... | collective-permute-start | bytes 294920 | tf_op jit(solution)/shard_map/ppermute | solution.py:648
  13.3 9.9 %collective-permute-start.1 = (bf16[32,1536]{1,0:T(8,128)(2,1)S(1)}, bf16[32,1536]{1,0:T(8,128)(2,1)S(1)}, u32[]{:S(2)}, u32[]{:S(2)}) collective-permute-start(bf16[32,1536]{1,0:T(8,128)(2,1)S(1)} %get-tuple-element.49), channel_id=1, source_target_pairs={{0,7},{1,2},{2,1},{3,4},{4,3},{5,6},{6,5},{7,0},{8,15},{9,10},{10,... | collective-permute-start | bytes 294920 | tf_op jit(solution)/shard_map/ppermute | solution.py:648
  14.9 8.3 %collective-permute-start.2 = (bf16[32,1536]{1,0:T(8,128)(2,1)S(1)}, bf16[32,1536]{1,0:T(8,128)(2,1)S(1)}, u32[]{:S(2)}, u32[]{:S(2)}) collective-permute-start(bf16[32,1536]{1,0:T(8,128)(2,1)S(1)} %get-tuple-element.50), channel_id=1, source_target_pairs={{0,8},{8,0},{16,24},{24,16},{32,40},{40,32},{48,56},{56,48},{1,9},... | collective-permute-start | bytes 294920 | tf_op jit(solution)/shard_map/ppermute | solution.py:648
  14.9 8.3 %collective-permute-start.3 = (bf16[32,1536]{1,0:T(8,128)(2,1)S(1)}, bf16[32,1536]{1,0:T(8,128)(2,1)S(1)}, u32[]{:S(2)}, u32[]{:S(2)}) collective-permute-start(bf16[32,1536]{1,0:T(8,128)(2,1)S(1)} %get-tuple-element.51), channel_id=1, source_target_pairs={{0,64},{64,0},{128,192},{192,128},{1,65},{65,1},{129,193},{193,129... | collective-permute-start | bytes 294920 | tf_op jit(solution)/shard_map/ppermute | solution.py:648
  16.1 7.1 %collective-permute-start.4 = (bf16[32,1536]{1,0:T(8,128)(2,1)S(1)}, bf16[32,1536]{1,0:T(8,128)(2,1)S(1)}, u32[]{:S(2)}, u32[]{:S(2)}) collective-permute-start(bf16[32,1536]{1,0:T(8,128)(2,1)S(1)} %get-tuple-element.52), channel_id=1, source_target_pairs={{0,192},{64,128},{128,64},{192,0},{1,193},{65,129},{129,65},{193,1... | collective-permute-start | bytes 294920 | tf_op jit(solution)/shard_map/ppermute | solution.py:648
  17.9 5.3 %collective-permute-start.5 = (bf16[32,1536]{1,0:T(8,128)(2,1)S(1)}, bf16[32,1536]{1,0:T(8,128)(2,1)S(1)}, u32[]{:S(2)}, u32[]{:S(2)}) collective-permute-start(bf16[32,1536]{1,0:T(8,128)(2,1)S(1)} %get-tuple-element.53), channel_id=1, source_target_pairs={{0,1},{1,0},{2,3},{3,2},{4,5},{5,4},{6,7},{7,6},{8,9},{9,8},{10,11... | collective-permute-start | bytes 294920 | tf_op jit(solution)/shard_map/ppermute | solution.py:648
  23.2 1.1 copy-start
  24.4 1.0 copy-start.2
  25.4 1.0 copy-start.10
  26.4 1.0 copy-start.11
  27.4 0.7 copy-start.12
  28.1 22.3 %copy-start.1 = (bf16[2784,128]{1,0:T(8,128)(2,1)S(1)}, bf16[2784,128]{1,0:T(8,128)(2,1)}, u32[]{:S(2)}) copy-start(bf16[2784,128]{1,0:T(8,128)(2,1)} %get-tuple-element.44.pack_ref.refs_5_) | copy-start | bytes 2138116
  28.2 22.4 %copy-start.6 = (s32[128]{0:T(128)S(1)}, s32[128]{0:T(128)}, u32[]{:S(2)}) copy-start(s32[128]{0:T(128)} %param.20) | copy-start | bytes 1540
  28.2 26.0 %copy-start.3 = (f32[32,32,128]{2,1,0:T(8,128)S(1)}, f32[32,32,128]{2,1,0:T(8,128)}, u32[]{:S(2)}) copy-start(f32[32,32,128]{2,1,0:T(8,128)} %get-tuple-element.43.geo_ref.refs_1_) | copy-start | bytes 1572868
  28.2 26.0 %copy-start.13 = (s32[32,128]{1,0:T(8,128)S(1)}, s32[32,128]{1,0:T(8,128)}, u32[]{:S(2)}) copy-start(s32[32,128]{1,0:T(8,128)} %get-tuple-element.42.refs_0_) | copy-start | bytes 49156
  37.9 12.6 %collective-permute-start.6 = (bf16[32,1536]{1,0:T(8,128)(2,1)S(1)}, bf16[32,1536]{1,0:T(8,128)(2,1)S(1)}, u32[]{:S(2)}, u32[]{:S(2)}) collective-permute-start(bf16[32,1536]{1,0:T(8,128)(2,1)S(1)} %get-tuple-element.55), channel_id=1, source_target_pairs={{0,56},{8,16},{16,8},{24,32},{32,24},{40,48},{48,40},{56,0},{1,57}... | collective-permute-start | bytes 294920 | tf_op jit(solution)/shard_map/ppermute | solution.py:648
  46.1 7.7 %collective-permute-start.7 = (bf16[32,1536]{1,0:T(8,128)(2,1)S(1)}, bf16[32,1536]{1,0:T(8,128)(2,1)S(1)}, u32[]{:S(2)}, u32[]{:S(2)}) collective-permute-start(bf16[32,1536]{1,0:T(8,128)(2,1)S(1)} %get-tuple-element.56), channel_id=1, source_target_pairs={{0,7},{1,2},{2,1},{3,4},{4,3},{5,6},{6,5},{7,0},{8,15},{9,10},{10,... | collective-permute-start | bytes 294920 | tf_op jit(solution)/shard_map/ppermute | solution.py:648
  47.5 6.3 %collective-permute-start.8 = (bf16[32,1536]{1,0:T(8,128)(2,1)S(1)}, bf16[32,1536]{1,0:T(8,128)(2,1)S(1)}, u32[]{:S(2)}, u32[]{:S(2)}) collective-permute-start(bf16[32,1536]{1,0:T(8,128)(2,1)S(1)} %get-tuple-element.57), channel_id=1, source_target_pairs={{0,8},{8,0},{16,24},{24,16},{32,40},{40,32},{48,56},{56,48},{1,9},... | collective-permute-start | bytes 294920 | tf_op jit(solution)/shard_map/ppermute | solution.py:648
  47.5 6.3 %collective-permute-start.9 = (bf16[32,1536]{1,0:T(8,128)(2,1)S(1)}, bf16[32,1536]{1,0:T(8,128)(2,1)S(1)}, u32[]{:S(2)}, u32[]{:S(2)}) collective-permute-start(bf16[32,1536]{1,0:T(8,128)(2,1)S(1)} %get-tuple-element.58), channel_id=1, source_target_pairs={{0,64},{64,0},{128,192},{192,128},{1,65},{65,1},{129,193},{193,129... | collective-permute-start | bytes 294920 | tf_op jit(solution)/shard_map/ppermute | solution.py:648
  48.7 5.4 %collective-permute-start.10 = (bf16[32,1536]{1,0:T(8,128)(2,1)S(1)}, bf16[32,1536]{1,0:T(8,128)(2,1)S(1)}, u32[]{:S(2)}, u32[]{:S(2)}) collective-permute-start(bf16[32,1536]{1,0:T(8,128)(2,1)S(1)} %get-tuple-element.59), channel_id=1, source_target_pairs={{0,192},{64,128},{128,64},{192,0},{1,193},{65,129},{129,65},{193,1... | collective-permute-start | bytes 294920 | tf_op jit(solution)/shard_map/ppermute | solution.py:648
  50.5 3.6 %collective-permute-start.11 = (bf16[32,1536]{1,0:T(8,128)(2,1)S(1)}, bf16[32,1536]{1,0:T(8,128)(2,1)S(1)}, u32[]{:S(2)}, u32[]{:S(2)}) collective-permute-start(bf16[32,1536]{1,0:T(8,128)(2,1)S(1)} %get-tuple-element.60), channel_id=1, source_target_pairs={{0,1},{1,0},{2,3},{3,2},{4,5},{5,4},{6,7},{7,6},{8,9},{9,8},{10,11... | collective-permute-start | bytes 294920 | tf_op jit(solution)/shard_map/ppermute | solution.py:648
  63.8 10.8 %collective-permute-start.12 = (bf16[32,1536]{1,0:T(8,128)(2,1)S(1)}, bf16[32,1536]{1,0:T(8,128)(2,1)S(1)}, u32[]{:S(2)}, u32[]{:S(2)}) collective-permute-start(bf16[32,1536]{1,0:T(8,128)(2,1)S(1)} %get-tuple-element.62), channel_id=1, source_target_pairs={{0,56},{8,16},{16,8},{24,32},{32,24},{40,48},{48,40},{56,0},{1,57}... | collective-permute-start | bytes 294920 | tf_op jit(solution)/shard_map/ppermute | solution.py:648
  69.1 8.2 %collective-permute-start.13 = (bf16[32,1536]{1,0:T(8,128)(2,1)S(1)}, bf16[32,1536]{1,0:T(8,128)(2,1)S(1)}, u32[]{:S(2)}, u32[]{:S(2)}) collective-permute-start(bf16[32,1536]{1,0:T(8,128)(2,1)S(1)} %get-tuple-element.63), channel_id=1, source_target_pairs={{0,7},{1,2},{2,1},{3,4},{4,3},{5,6},{6,5},{7,0},{8,15},{9,10},{10,... | collective-permute-start | bytes 294920 | tf_op jit(solution)/shard_map/ppermute | solution.py:648
  71.5 5.8 %collective-permute-start.14 = (bf16[32,1536]{1,0:T(8,128)(2,1)S(1)}, bf16[32,1536]{1,0:T(8,128)(2,1)S(1)}, u32[]{:S(2)}, u32[]{:S(2)}) collective-permute-start(bf16[32,1536]{1,0:T(8,128)(2,1)S(1)} %get-tuple-element.64), channel_id=1, source_target_pairs={{0,8},{8,0},{16,24},{24,16},{32,40},{40,32},{48,56},{56,48},{1,9},... | collective-permute-start | bytes 294920 | tf_op jit(solution)/shard_map/ppermute | solution.py:648
  71.6 5.8 %collective-permute-start.15 = (bf16[32,1536]{1,0:T(8,128)(2,1)S(1)}, bf16[32,1536]{1,0:T(8,128)(2,1)S(1)}, u32[]{:S(2)}, u32[]{:S(2)}) collective-permute-start(bf16[32,1536]{1,0:T(8,128)(2,1)S(1)} %get-tuple-element.65), channel_id=1, source_target_pairs={{0,64},{64,0},{128,192},{192,128},{1,65},{65,1},{129,193},{193,129... | collective-permute-start | bytes 294920 | tf_op jit(solution)/shard_map/ppermute | solution.py:648
  72.8 4.7 %collective-permute-start.16 = (bf16[32,1536]{1,0:T(8,128)(2,1)S(1)}, bf16[32,1536]{1,0:T(8,128)(2,1)S(1)}, u32[]{:S(2)}, u32[]{:S(2)}) collective-permute-start(bf16[32,1536]{1,0:T(8,128)(2,1)S(1)} %get-tuple-element.66), channel_id=1, source_target_pairs={{0,192},{64,128},{128,64},{192,0},{1,193},{65,129},{129,65},{193,1... | collective-permute-start | bytes 294920 | tf_op jit(solution)/shard_map/ppermute | solution.py:648
  74.6 2.8 %collective-permute-start.17 = (bf16[32,1536]{1,0:T(8,128)(2,1)S(1)}, bf16[32,1536]{1,0:T(8,128)(2,1)S(1)}, u32[]{:S(2)}, u32[]{:S(2)}) collective-permute-start(bf16[32,1536]{1,0:T(8,128)(2,1)S(1)} %get-tuple-element.67), channel_id=1, source_target_pairs={{0,1},{1,0},{2,3},{3,2},{4,5},{5,4},{6,7},{7,6},{8,9},{9,8},{10,11... | collective-permute-start | bytes 294920 | tf_op jit(solution)/shard_map/ppermute | solution.py:648
  77.5 31.4 %copy-start.8 = (s32[32]{0:T(128)S(1)}, s32[32]{0:T(128)}, u32[]{:S(2)}) copy-start(s32[32]{0:T(128)} %slab_ref.3) | copy-start | bytes 388
  77.5 35.6 %copy-start.9 = (f32[32,32,128]{2,1,0:T(8,128)S(1)}, f32[32,32,128]{2,1,0:T(8,128)}, u32[]{:S(2)}) copy-start(f32[32,32,128]{2,1,0:T(8,128)} %get-tuple-element.77.geo_ref) | copy-start | bytes 1572868
  87.9 37.3 %copy-start.5 = (s32[32,128]{1,0:T(8,128)S(1)}, s32[32,128]{1,0:T(8,128)}, u32[]{:S(2)}) copy-start(s32[32,128]{1,0:T(8,128)} %idx_ref.1) | copy-start | bytes 49156
  87.9 10.9 %collective-permute-start.18 = (bf16[32,1024]{1,0:T(8,128)(2,1)S(1)}, bf16[32,1024]{1,0:T(8,128)(2,1)S(1)}, u32[]{:S(2)}, u32[]{:S(2)}) collective-permute-start(bf16[32,1024]{1,0:T(8,128)(2,1)S(1)} %get-tuple-element.69), channel_id=1, source_target_pairs={{0,61},{1,60},{2,63},{3,62},{4,57},{5,56},{6,59},{7,58},{8,21},{9,... | collective-permute-start | bytes 196616 | tf_op jit(solution)/shard_map/ppermute | solution.py:671
  95.7 7.2 %collective-permute-start.19 = (bf16[32,1024]{1,0:T(8,128)(2,1)S(1)}, bf16[32,1024]{1,0:T(8,128)(2,1)S(1)}, u32[]{:S(2)}, u32[]{:S(2)}) collective-permute-start(bf16[32,1024]{1,0:T(8,128)(2,1)S(1)} %get-tuple-element.70), channel_id=1, source_target_pairs={{0,3},{1,6},{2,5},{3,0},{4,7},{5,2},{6,1},{7,4},{8,11},{9,14},{10,... | collective-permute-start | bytes 196616 | tf_op jit(solution)/shard_map/ppermute | solution.py:664
  96.3 12.5 %collective-permute-start.24 = (bf16[64,1024]{1,0:T(8,128)(2,1)S(1)}, bf16[64,1024]{1,0:T(8,128)(2,1)S(1)}, u32[]{:S(2)}, u32[]{:S(2)}) collective-permute-start(bf16[64,1024]{1,0:T(8,128)(2,1)S(1)} %get-tuple-element.76), channel_id=1, source_target_pairs={{0,1},{1,0},{2,3},{3,2},{4,5},{5,4},{6,7},{7,6},{8,9},{9,8},{10,11... | collective-permute-start | bytes 393224 | tf_op jit(solution)/shard_map/ppermute | solution.py:653
  96.3 6.6 %collective-permute-start.20 = (bf16[32,1024]{1,0:T(8,128)(2,1)S(1)}, bf16[32,1024]{1,0:T(8,128)(2,1)S(1)}, u32[]{:S(2)}, u32[]{:S(2)}) collective-permute-start(bf16[32,1024]{1,0:T(8,128)(2,1)S(1)} %get-tuple-element.71), channel_id=1, source_target_pairs={{0,12},{1,13},{2,14},{3,15},{4,8},{5,9},{6,10},{7,11},{8,4},{9,5},... | collective-permute-start | bytes 196616 | tf_op jit(solution)/shard_map/ppermute | solution.py:671
  96.3 7.2 %collective-permute-start.21 = (bf16[32,1024]{1,0:T(8,128)(2,1)S(1)}, bf16[32,1024]{1,0:T(8,128)(2,1)S(1)}, u32[]{:S(2)}, u32[]{:S(2)}) collective-permute-start(bf16[32,1024]{1,0:T(8,128)(2,1)S(1)} %get-tuple-element.72), channel_id=1, source_target_pairs={{0,66},{1,67},{2,64},{3,65},{4,70},{5,71},{6,68},{7,69},{64,2},{65... | collective-permute-start | bytes 196616 | tf_op jit(solution)/shard_map/ppermute | solution.py:671
  98.8 7.3 %collective-permute-start.22 = (bf16[32,1024]{1,0:T(8,128)(2,1)S(1)}, bf16[32,1024]{1,0:T(8,128)(2,1)S(1)}, u32[]{:S(2)}, u32[]{:S(2)}) collective-permute-start(bf16[32,1024]{1,0:T(8,128)(2,1)S(1)} %get-tuple-element.73), channel_id=1, source_target_pairs={{0,195},{1,194},{2,193},{3,192},{4,199},{5,198},{6,197},{7,196},{6... | collective-permute-start | bytes 196616 | tf_op jit(solution)/shard_map/ppermute | solution.py:671
  102.9 6.0 %collective-permute-start.23 = (bf16[32,1024]{1,0:T(8,128)(2,1)S(1)}, bf16[32,1024]{1,0:T(8,128)(2,1)S(1)}, u32[]{:S(2)}, u32[]{:S(2)}) collective-permute-start(bf16[32,1024]{1,0:T(8,128)(2,1)S(1)} %get-tuple-element.74), channel_id=1, source_target_pairs={{0,4},{1,5},{2,6},{3,7},{4,0},{5,1},{6,2},{7,3},{8,12},{9,13},{10,... | collective-permute-start | bytes 196616 | tf_op jit(solution)/shard_map/ppermute | solution.py:664
  109.4 6.1 %collective-permute-start.27 = (bf16[64,1024]{1,0:T(8,128)(2,1)S(1)}, bf16[64,1024]{1,0:T(8,128)(2,1)S(1)}, u32[]{:S(2)}, u32[]{:S(2)}) collective-permute-start(bf16[64,1024]{1,0:T(8,128)(2,1)S(1)} %collect.1), channel_id=1, source_target_pairs={{0,6},{1,7},{2,4},{3,5},{4,2},{5,3},{6,0},{7,1},{8,14},{9,15},{10,... | collective-permute-start | bytes 393224 | tf_op jit(solution)/shard_map/ppermute | solution.py:653
  111.3 11.3 %collective-permute-start.26 = (bf16[64,1024]{1,0:T(8,128)(2,1)S(1)}, bf16[64,1024]{1,0:T(8,128)(2,1)S(1)}, u32[]{:S(2)}, u32[]{:S(2)}) collective-permute-start(bf16[64,1024]{1,0:T(8,128)(2,1)S(1)} %collect.1), channel_id=1, source_target_pairs={{0,4},{1,5},{2,6},{3,7},{4,0},{5,1},{6,2},{7,3},{8,12},{9,13},{10,... | collective-permute-start | bytes 393224 | tf_op jit(solution)/shard_map/ppermute | solution.py:653
  111.3 11.3 %collective-permute-start.25 = (bf16[64,1024]{1,0:T(8,128)(2,1)S(1)}, bf16[64,1024]{1,0:T(8,128)(2,1)S(1)}, u32[]{:S(2)}, u32[]{:S(2)}) collective-permute-start(bf16[64,1024]{1,0:T(8,128)(2,1)S(1)} %collect.1), channel_id=1, source_target_pairs={{0,2},{1,3},{2,0},{3,1},{4,6},{5,7},{6,4},{7,5},{8,10},{9,11},{10,... | collective-permute-start | bytes 393224 | tf_op jit(solution)/shard_map/ppermute | solution.py:653
  122.7 2.5 %collective-permute-start.28 = (bf16[256,1024]{1,0:T(8,128)(2,1)S(1)}, bf16[256,1024]{1,0:T(8,128)(2,1)S(1)}, u32[]{:S(2)}, u32[]{:S(2)}) collective-permute-start(bf16[256,1024]{1,0:T(8,128)(2,1)S(1)} %pad_maximum_fusion.near_ref), channel_id=1, source_target_pairs={{0,1},{1,0},{2,3},{3,2},{4,5},{5,4},{6,7},{7,6},{8,9},{9,8},{10,11... | collective-permute-start | bytes 1572872 | tf_op jit(solution)/shard_map/ppermute | solution.py:653

commit v3 on v2

--- a/solution.py
+++ b/solution.py
@@ -33,6 +33,7 @@
 WIDE = 16
 STEPS = K // WIDE
 ENV_ROW = 16
+INDEX_ROW = 17
 BASIS_ROW = 24
 GEO_ROWS = 32
 
@@ -187,12 +188,12 @@
             pltpu.VMEM(rows.shape, bf16),
             pltpu.SemaphoreType.DMA((2,)),
         ],
-        compiler_params=params(),
+        compiler_params=params(limit=VMEM_MOST),
         name="pick",
     )(lists, rows)
 
 
-def geometry_into(vec_ref, count_ref, geo_ref):
+def geometry_into(vec_ref, count_ref, geo_ref, index_ref=None):
     sharpness = ((NB - 1) / CUTOFF) ** 2
     centers = lax.broadcasted_iota(jnp.int32, (NB, ATOMS), 0).astype(f32) * (CUTOFF / (NB - 1))
 
@@ -209,56 +210,61 @@
         for m, value in enumerate(harmonics(vx, vy, vz)):
             geo_ref[k, m : m + 1, :] = value
         geo_ref[k, ENV_ROW:BASIS_ROW, :] = jnp.broadcast_to(envelope, (8, ATOMS))
+        if index_ref is not None:
+            geo_ref[k, INDEX_ROW : INDEX_ROW + 1, :] = index_ref[pl.ds(k, 1), :]
         geo_ref[k, BASIS_ROW:GEO_ROWS, :] = jnp.exp(-sharpness * offset * offset)
         return carry
 
     lax.fori_loop(0, K, one_slot, 0, unroll=4)
 
 
-PACK_OUT = 0
-PACK_MIX = 192
-PACK_GATE = 576
-PACK_MID = 672
-PACK_EMB = 736
-PACK_IN = 800
-PACK_LAYER = 816
-PACK_PROJ = LAYERS * PACK_LAYER
-PACK_PROBE_IN = PACK_PROJ + 256
-PACK_PROBE_MID = PACK_PROBE_IN + 16
-PACK_ROWS = PACK_PROBE_MID + 64
+OUT, MIX, GATE, MID, EMB, IN, LAYER_ROWS = 0, 192, 576, 672, 736, 800, 816
+FIRST_HIDDEN = WIDTH
+FIRST_LAYER = FIRST_HIDDEN + K * RH
+FIRST_SEL = FIRST_LAYER + LAYER_ROWS
+FIRST_ROWS = FIRST_SEL + GHOSTS
+LATER_PROJ = (LAYERS - 1) * LAYER_ROWS
+LATER_PROBE_IN = LATER_PROJ + 4 * RH
+LATER_PROBE_MID = LATER_PROBE_IN + 16
+LATER_SEL = LATER_PROBE_MID + RH
+LATER_ROWS = LATER_SEL + GHOSTS
 WEIGHTS = 9
 
 
-def pack_weights(refs, pack_ref):
+def weights_at(t):
+    return FIRST_LAYER if t == 0 else (t - 1) * LAYER_ROWS
+
+
+def pack_weights(refs, first_ref, later_ref):
     win_ref, wemb_ref, wmid_ref, wout_ref, mix_ref, gate_ref, proj_ref, pin_ref, pmid_ref = refs
 
-    def put(at, value):
+    def put(pack_ref, at, value):
         pack_ref[at : at + value.shape[0], : value.shape[1]] = value
 
     def padded(value):
         return jnp.concatenate([value, jnp.zeros_like(value)], axis=0)
 
     for t in range(LAYERS):
-        base = t * PACK_LAYER
+        pack_ref, base = first_ref if t == 0 else later_ref, weights_at(t)
         for j in range(3):
-            put(base + PACK_OUT + RH * j, wout_ref[t, :, 128 * j : 128 * (j + 1)])
+            put(pack_ref, base + OUT + RH * j, wout_ref[t, :, 128 * j : 128 * (j + 1)])
         for degree in range(4):
-            put(base + PACK_MIX + C * degree, mix_ref[t, degree])
-        put(base + PACK_GATE, gate_ref[t])
-        put(base + PACK_MID, wmid_ref[t])
-        put(base + PACK_EMB, wemb_ref[t])
-        put(base + PACK_IN, padded(win_ref[t]))
+            put(pack_ref, base + MIX + C * degree, mix_ref[t, degree])
+        put(pack_ref, base + GATE, gate_ref[t])
+        put(pack_ref, base + MID, wmid_ref[t])
+        put(pack_ref, base + EMB, wemb_ref[t])
+        put(pack_ref, base + IN, padded(win_ref[t]))
     for degree in range(4):
-        put(PACK_PROJ + RH * degree, proj_ref[degree])
-    put(PACK_PROBE_IN, padded(pin_ref[...]))
-    put(PACK_PROBE_MID, pmid_ref[...])
-
-
-def hidden_into(t, species_ref, geo_ref, pack_ref, out_ref):
-    base = t * PACK_LAYER
-    wemb = pack_ref[base + PACK_EMB : base + PACK_EMB + RH, :SPECIES]
-    win = pack_ref[base + PACK_IN : base + PACK_IN + 16, :RH][:NB]
-    wmid = pack_ref[base + PACK_MID : base + PACK_MID + RH, :RH]
+        put(later_ref, LATER_PROJ + RH * degree, proj_ref[degree])
+    put(later_ref, LATER_PROBE_IN, padded(pin_ref[...]))
+    put(later_ref, LATER_PROBE_MID, pmid_ref[...])
+
+
+def hidden_into(t, species_ref, geo_ref, pack_ref, put):
+    base = weights_at(t)
+    wemb = pack_ref[base + EMB : base + EMB + RH, :SPECIES]
+    win = pack_ref[base + IN : base + IN + 16, :RH][:NB]
+    wmid = pack_ref[base + MID : base + MID + RH, :RH]
     ids = lax.broadcasted_iota(jnp.int32, (SPECIES, ATOMS), 0)
     emb = dot(wemb, (ids == species_ref[...]).astype(f32).astype(bf16))
     for k in range(0, K, 8):
@@ -267,57 +273,60 @@
         hidden = silu(hidden).astype(bf16)
         hidden = silu(dot_tn(wmid, hidden)).astype(bf16)
         for s in range(8):
-            out_ref[k + s] = hidden[:, s * ATOMS : (s + 1) * ATOMS]
+            put(k + s, hidden[:, s * ATOMS : (s + 1) * ATOMS])
+
+
+INPUTS = 6 + WEIGHTS
 
 
 def prepare_kernel(*refs):
-    inputs = refs[: 7 + WEIGHTS]
-    turned_ref, ageo_ref, pgeo_ref, index_ref, hidden_ref, pack_ref = refs[7 + WEIGHTS : 13 + WEIGHTS]
-    *landed, sems = refs[13 + WEIGHTS :]
+    geo_ref, first_ref, later_ref = refs[INPUTS : INPUTS + 3]
+    *landed, index_ref, sems = refs[INPUTS + 3 :]
     copies = [
         pltpu.make_async_copy(source, target, sems.at[number])
-        for number, (source, target) in enumerate(zip(inputs, landed))
+        for number, (source, target) in enumerate(zip(refs[:INPUTS], landed))
     ]
     for copy in copies:
         copy.start()
-    avec_ref, acount_ref, rows_ref, old_ref, pvec_ref, pcount_ref, species_ref = landed[:7]
+    old_ref, vec_ref, count_ref, rows_ref, species_ref, sel_ref = landed[:6]
     copies[0].wait()
-    copies[1].wait()
-    geometry_into(avec_ref, acount_ref, ageo_ref)
-    copies[2].wait()
-    turned_ref[...] = rows_ref[...].astype(f32).T.astype(bf16)
-    copies[3].wait()
     index = old_ref[...]
     block = (index - ATOMS) // FACE
     odd = jnp.where(block < 2, parity(0), jnp.where(block < 4, parity(1), parity(2)))
     moved = jnp.where(block % 2 == 0, index + FACE, index - FACE)
-    index_ref[...] = jnp.where((index >= ATOMS) & (odd == 0), moved, index)
-    copies[4].wait()
-    copies[5].wait()
-    geometry_into(pvec_ref, pcount_ref, pgeo_ref)
-    for copy in copies[6:]:
+    index_ref[...] = jnp.where((index >= ATOMS) & (odd == 0), moved, index).astype(f32)
+    copies[1].wait()
+    copies[2].wait()
+    geometry_into(vec_ref, count_ref, geo_ref, index_ref)
+    copies[3].wait()
+    first_ref[:WIDTH, :] = rows_ref[...].astype(f32).T.astype(bf16)
+    for copy in copies[4:]:
         copy.wait()
-    pack_weights(landed[7:], pack_ref)
-    hidden_into(0, species_ref, ageo_ref, pack_ref, hidden_ref)
+    first_ref[FIRST_SEL:, :] = sel_ref[...]
+    later_ref[LATER_SEL:, :] = sel_ref[...]
+    pack_weights(landed[6:], first_ref, later_ref)
+
+    def put(k, hidden):
+        at = FIRST_HIDDEN + k * RH
+        first_ref[at : at + RH, :] = hidden
+
+    hidden_into(0, species_ref, geo_ref, first_ref, put)
 
 
 def prepare(inputs):
     outs = [
-        jax.ShapeDtypeStruct((WIDTH, ATOMS), bf16),
         jax.ShapeDtypeStruct((K, GEO_ROWS, ATOMS), f32),
-        jax.ShapeDtypeStruct((K, GEO_ROWS, ATOMS), f32),
-        jax.ShapeDtypeStruct((K, ATOMS), jnp.int32),
-        jax.ShapeDtypeStruct((K, RH, ATOMS), bf16),
-        jax.ShapeDtypeStruct((PACK_ROWS, 128), bf16),
+        jax.ShapeDtypeStruct((FIRST_ROWS, 128), bf16),
+        jax.ShapeDtypeStruct((LATER_ROWS, 128), bf16),
     ]
     return pl.pallas_call(
         prepare_kernel,
         grid=(1,),
-        in_specs=in_hbm(7 + WEIGHTS),
+        in_specs=in_hbm(INPUTS),
         out_specs=[whole(*out.shape) for out in outs],
         out_shape=outs,
         scratch_shapes=[pltpu.VMEM(array.shape, array.dtype) for array in inputs]
-        + [pltpu.SemaphoreType.DMA((7 + WEIGHTS,))],
+        + [pltpu.VMEM((K, ATOMS), f32), pltpu.SemaphoreType.DMA((INPUTS,))],
         compiler_params=params(limit=VMEM_MOST),
         cost_estimate=pl.CostEstimate(flops=10_000_000, bytes_accessed=9_000_000, transcendentals=100_000),
         name="prepare",
@@ -325,14 +334,17 @@
 
 
 def hidden_kernel(t, species_ref, geo_ref, pack_ref, out_ref):
-    hidden_into(t, species_ref, geo_ref, pack_ref, out_ref)
-
-
-def hidden_units(t, species, geo, pack):
+    def put(k, hidden):
+        out_ref[k] = hidden
+
+    hidden_into(t, species_ref, geo_ref, pack_ref, put)
+
+
+def hidden_units(t, species, geo, later):
     return pl.pallas_call(
         functools.partial(hidden_kernel, t),
         grid=(1,),
-        in_specs=[whole(1, ATOMS), whole(K, GEO_ROWS, ATOMS), whole(PACK_ROWS, 128)],
+        in_specs=[whole(1, ATOMS), whole(K, GEO_ROWS, ATOMS), whole(LATER_ROWS, 128)],
         out_specs=whole(K, RH, ATOMS),
         out_shape=jax.ShapeDtypeStruct((K, RH, ATOMS), bf16),
         compiler_params=params(),
@@ -340,22 +352,34 @@
             flops=2 * 4096 * 256 * RH * 2, bytes_accessed=2_000_000, transcendentals=600_000
         ),
         name="hidden_units",
-    )(species, geo, pack)
+    )(species, geo, later)
 
 
 def layer_kernel(t, *refs):
     last = t == LAYERS - 1
-    base = t * PACK_LAYER
-    idx_ref, geo_ref, hidden_ref, turned_ref, sel_ref, pack_ref = refs[:6]
-    ghost_refs = refs[6:12]
-    out_refs = refs[12:-5]
+    base = weights_at(t)
+    geo_ref, pack_ref, *refs = refs
+    ghost_refs, refs = refs[:BLOCKS], refs[BLOCKS:]
+    if t == 0:
+        turned_ref = pack_ref
+        sel = pack_ref[FIRST_SEL:FIRST_ROWS, :]
+
+        def hidden_of(k):
+            return pack_ref[pl.ds(pl.multiple_of(FIRST_HIDDEN + k * RH, RH), RH), :]
+
+    else:
+        turned_ref, hidden_ref, *refs = refs
+        sel = pack_ref[LATER_SEL:LATER_ROWS, :]
+
+        def hidden_of(k):
+            return hidden_ref[k]
+
+    out_refs = refs[:-5]
+    table_ref, acc_ref, even_ref, odd_ref, rad_ref = refs[-5:]
     wout = jnp.concatenate(
-        [pack_ref[base + PACK_OUT + RH * j : base + PACK_OUT + RH * (j + 1), :] for j in range(3)],
-        axis=1,
+        [pack_ref[base + OUT + RH * j : base + OUT + RH * (j + 1), :] for j in range(3)], axis=1
     )
-    table_ref, acc_ref, even_ref, odd_ref, rad_ref = refs[-5:]
-
-    own = turned_ref[...].astype(f32)
+    own = turned_ref[:WIDTH, :].astype(f32)
     ghosts = jnp.concatenate([ghost_refs[SENT.index(b)][...] for b in range(BLOCKS)], axis=0)
     ghosts = ghosts.astype(f32).T
     scale, inverse = power_scale(
@@ -375,14 +399,18 @@
         table_ref[:, at : at + PADDED - TABLE] = jnp.zeros((WIDTH, PADDED - TABLE), f8)
 
     def front(first, slot):
-        hidden = jnp.concatenate([hidden_ref[first + s] for s in range(STEP)], axis=1)
+        hidden = jnp.concatenate([hidden_of(first + s) for s in range(STEP)], axis=1)
         envelope = jnp.concatenate(
             [geo_ref[first + s, ENV_ROW : ENV_ROW + 1, :] for s in range(STEP)], axis=1
         )
         rad_ref[slot] = dot_tn(wout, hidden) * (envelope * scale)
-        ids = lax.broadcasted_iota(jnp.int32, (PADDED, ATOMS), 0)
+        ids = lax.broadcasted_iota(jnp.int32, (PADDED, ATOMS), 0).astype(f32)
         hot = jnp.concatenate(
-            [(ids == idx_ref[pl.ds(first + s, 1), :]).astype(f32) for s in range(STEP)], axis=1
+            [
+                (ids == geo_ref[first + s, INDEX_ROW : INDEX_ROW + 1, :]).astype(f32)
+                for s in range(STEP)
+            ],
+            axis=1,
         )
         hot = hot.astype(f8)
         return jnp.concatenate([hot, hot], axis=0)
@@ -427,11 +455,11 @@
     back(K - STEP, odd_ref, 1, None, range(0, C, 8))
 
     message = [acc_ref[m * C : (m + 1) * C, :].astype(bf16) for m in range(COMPS)]
-    gate = sigmoid(dot_tn(pack_ref[base + PACK_GATE : base + PACK_GATE + C, :C], message[0]))
+    gate = sigmoid(dot_tn(pack_ref[base + GATE : base + GATE + C, :C], message[0]))
     updated = []
     for degree in range(4):
         start, width = STARTS[degree], WIDTHS[degree]
-        at = base + PACK_MIX + C * degree
+        at = base + MIX + C * degree
         mixed = dot_tn(pack_ref[at : at + C, :C], jnp.concatenate(message[start : start + width], axis=1))
         for j in range(width):
             m = start + j
@@ -440,7 +468,6 @@
             change = silu(part) if degree == 0 else gate * part
             updated.append((before + change).astype(bf16))
     new = jnp.concatenate(updated, axis=0)
-    sel = sel_ref[...]
     if not last:
         out_refs[0][...] = new
         picked = dot_nt(sel, new).astype(bf16)
@@ -454,7 +481,7 @@
         out_refs[0][...] = dot_nt(ones, new).astype(bf16)
         keys = jnp.concatenate(
             [
-                dot(pack_ref[PACK_PROJ + RH * l : PACK_PROJ + RH * (l + 1), :C], updated[m])
+                dot(pack_ref[LATER_PROJ + RH * l : LATER_PROJ + RH * (l + 1), :C], updated[m])
                 for m, l in enumerate(DEGREE)
             ],
             axis=0,
@@ -466,7 +493,7 @@
         out_refs[8][...] = rows[GHOSTS + HALF :]
 
 
-def layer(t, idx, geo, hidden, turned, sel, ghosts, pack):
+def layer(t, geo, pack, ghosts, more):
     last = t == LAYERS - 1
     if last:
         shapes = [(ATOMS, WIDTH)] + [(FACE, COMPS * RH)] * 6 + [(HALF, COMPS * RH)] * 2
@@ -476,15 +503,9 @@
     return pl.pallas_call(
         functools.partial(layer_kernel, t),
         grid=(1,),
-        in_specs=[
-            whole(K, ATOMS),
-            whole(K, GEO_ROWS, ATOMS),
-            whole(K, RH, ATOMS),
-            whole(WIDTH, ATOMS),
-            whole(GHOSTS, ATOMS),
-            whole(PACK_ROWS, 128),
-        ]
-        + [whole(FACE, WIDTH)] * BLOCKS,
+        in_specs=[whole(K, GEO_ROWS, ATOMS), whole(*pack.shape)]
+        + [whole(FACE, WIDTH)] * BLOCKS
+        + [whole(*array.shape) for array in more],
         out_specs=[whole(*shape) for shape in shapes],
         out_shape=[jax.ShapeDtypeStruct(shape, bf16) for shape in shapes],
         scratch_shapes=[
@@ -499,35 +520,46 @@
             flops=2 * 4096 * 512 * WIDTH, bytes_accessed=3_000_000, transcendentals=600_000
         ),
         name="layer",
-    )(idx, geo, hidden, turned, sel, pack, *[ghosts[b] for b in SENT])
-
-
-def probe_weights_kernel(geo_ref, pack_ref, out_ref):
-    win = pack_ref[PACK_PROBE_IN : PACK_PROBE_IN + 16, :RH][:NB]
-    wmid = pack_ref[PACK_PROBE_MID : PACK_PROBE_MID + RH, :RH]
-    basis = jnp.concatenate([geo_ref[s, BASIS_ROW:GEO_ROWS, :] for s in range(WIDE)], axis=1)
+    )(geo, pack, *[ghosts[b] for b in SENT], *more)
+
+
+def probe_weights_kernel(vec_ref, count_ref, pack_ref, out_ref, geo_ref):
+    step = pl.program_id(0)
+
+    @pl.when(step == 0)
+    def _():
+        geometry_into(vec_ref, count_ref, geo_ref)
+
+    win = pack_ref[LATER_PROBE_IN : LATER_PROBE_IN + 16, :RH][:NB]
+    wmid = pack_ref[LATER_PROBE_MID : LATER_PROBE_MID + RH, :RH]
+    first = step * WIDE
+    basis = jnp.concatenate(
+        [geo_ref[first + s, BASIS_ROW:GEO_ROWS, :] for s in range(WIDE)], axis=1
+    )
     hidden = silu(dot_tn(win, basis.astype(bf16))).astype(bf16)
     hidden = silu(dot_tn(wmid, hidden)).astype(bf16).astype(f32)
     for s in range(WIDE):
-        scaled = hidden[:, s * ATOMS : (s + 1) * ATOMS] * geo_ref[s, ENV_ROW : ENV_ROW + 1, :]
+        scaled = hidden[:, s * ATOMS : (s + 1) * ATOMS]
+        scaled = scaled * geo_ref[first + s, ENV_ROW : ENV_ROW + 1, :]
         for m in range(COMPS):
-            value = scaled if m == 0 else scaled * geo_ref[s, m : m + 1, :]
+            value = scaled if m == 0 else scaled * geo_ref[first + s, m : m + 1, :]
             out_ref[s, m * RH : (m + 1) * RH, :] = value.astype(bf16)
 
 
-def probe_weights(geo, pack):
+def probe_weights(vectors, count, pack):
     return pl.pallas_call(
         probe_weights_kernel,
         grid=(STEPS,),
-        in_specs=[slots(GEO_ROWS, ATOMS), whole(PACK_ROWS, 128)],
+        in_specs=[whole(3, K, ATOMS), whole(1, ATOMS), whole(LATER_ROWS, 128)],
         out_specs=slots(COMPS * RH, ATOMS),
         out_shape=jax.ShapeDtypeStruct((K, COMPS * RH, ATOMS), bf16),
+        scratch_shapes=[pltpu.VMEM((K, GEO_ROWS, ATOMS), f32)],
         compiler_params=params(("arbitrary",)),
         cost_estimate=pl.CostEstimate(
             flops=2 * 4096 * 256 * WIDTH, bytes_accessed=9_000_000, transcendentals=600_000
         ),
         name="probe_weights",
-    )(geo, pack)
+    )(vectors, count, pack)
 
 
 HOLDERS = (2, 3, 4, 5, 5, 4)
@@ -700,15 +732,14 @@
     sel, *blocks = pick(octant_lists, features)
     ghosts = exchange(blocks)
     species_row = species.reshape(1, ATOMS)
-    turned, geo, probe_geo, index, hidden, pack = prepare(
+    geo, first, later = prepare(
         (
+            neighbour_index,
             edge_vectors,
             neighbour_count.reshape(1, ATOMS),
             features,
-            neighbour_index,
-            probe_vectors,
-            probe_count.reshape(1, ATOMS),
             species_row,
+            sel,
             radial_in,
             jnp.swapaxes(species_emb, 1, 2),
             radial_mid,
@@ -721,14 +752,19 @@
         )
     )
     for t in range(LAYERS):
-        if t > 0:
-            hidden = hidden_units(t, species_row, geo, pack)
-        outs = layer(t, index, geo, hidden, turned, sel, ghosts, pack)
+        if t == 0:
+            outs = layer(t, geo, first, ghosts, ())
+        else:
+            outs = layer(t, geo, later, ghosts, (turned, hidden_units(t, species_row, geo, later)))
         if t < LAYERS - 1:
             turned = outs[0]
             ghosts = exchange(outs[1:])
     near, far, probe_weight = column_keys(
-        slab_index, outs[1:7], outs[7], outs[8], probe_weights(probe_geo, pack)
+        slab_index,
+        outs[1:7],
+        outs[7],
+        outs[8],
+        probe_weights(probe_vectors, probe_count.reshape(1, ATOMS), later),
     )
     density = readout(slab_index, probe_index, probe_weight, near, far)
     return (outs[0], density.reshape(ATOMS))

time: 130 us -> 127 us (0.977)
  local copies, waits for them, and re-layouts: 6.6 us -> 2.33 us
  Pallas kernels: 43.9 us -> 46 us
    unnamed x28 -> x18, local copies, waits for them, and re-layouts: 6.6 us -> 2.33 us
    pallas_call x1, Pallas kernels: 0.73 us -> 2.17 us  [pick(): pl.pallas_call(pick_kernel, grid=(1,), in_specs=in_hbm(2), out_specs=[who...]
  transfers between devices with their start and end apart: 29 -> 29, of which waited for: 10 -> 9; matrix products, arithmetic and copies ran while one was open for 0% -> 0% of each run, Pallas kernels for 7% -> 7%
where the time goes in v3:
time: 127 us
  starting transfers between devices  59.8 us (47%)
  Pallas kernels  46 us (36%)
  waiting for transfers between devices  18.1 us (14%)
  local copies, waits for them, and re-layouts  2.33 us (2%)
    ppermute x18, starting transfers between devices, exchange(): landed[block] = lax.ppermute(blocks[block], axis, pairs)  40.5 us
    pallas_call x3, Pallas kernels, layer(): pl.pallas_call(functools.partial(layer_kernel, t), grid=(1,), in_specs=[w...  30.3 us
    ppermute x4, starting transfers between devices, column_keys(): landed[block] = lax.ppermute(blocks[block], (axis, 'gz'), pairs)  14 us
    ppermute x5, waiting for transfers between devices, along_column(): lax.ppermute(block, 'gz', [(i, i ^ code) for i in range(lax.axis_size('gz...  8.4 us
    ppermute x5, starting transfers between devices, along_column(): lax.ppermute(block, 'gz', [(i, i ^ code) for i in range(lax.axis_size('gz...  4.59 us
    pallas_call x1, Pallas kernels, readout(): pl.pallas_call(readout_kernel, grid=(STEPS,), in_specs=[pl.BlockSpec(memo...  4.36 us
    pallas_call x1, Pallas kernels, prepare(): pl.pallas_call(prepare_kernel, grid=(1,), in_specs=in_hbm(INPUTS), out_sp...  3.87 us
    ppermute x18, waiting for transfers between devices, exchange(): landed[block] = lax.ppermute(blocks[block], axis, pairs)  3.69 us
  transfers between devices with their start and end apart: 29, of which 9 were waited for; matrix products, arithmetic and copies ran while one was open for 0% of the time, Pallas kernels for 7%

profile of v3, /device:TPU:1, one launch (start us, length us, event | category | flops | bytes accessed | tf_op | source)
XLA Modules:
  0.0 127.0 jit_solution(4392950755511783374)
XLA Ops:
  0.6 2.2 %pick.1 = (bf16[192,128]{1,0:T(8,128)(2,1)}, bf16[32,1536]{1,0:T(8,128)(2,1)}, bf16[32,1536]{1,0:T(8,128)(2,1)}, bf16[32,1536]{1,0:T(8,128)(2,1)}, bf16[32,1536]...) custom-call(s32[2,2,2,8]{3,2,1,0:T(2,128)} %lists_hbm.1, bf16[128,1536]{1,0:T(8,128)(2,1)} %refs_3_.1), custom_call_target="tpu_custom_call" | custom-call | tf_op jit(solution)/shard_map/pick/pallas_call | solution.py:179
  2.8 10.3 %collective-permute-start = (bf16[32,1536]{1,0:T(8,128)(2,1)}, bf16[32,1536]{1,0:T(8,128)(2,1)S(1)}, u32[]{:S(2)}, u32[]{:S(2)}) collective-permute-start(bf16[32,1536]{1,0:T(8,128)(2,1)} %get-tuple-element.43), channel_id=1, source_target_pairs={{0,56},{8,16},{16,8},{24,32},{32,24},{40,48},{48,40},{56,0},{1,57}... | collective-permute-start | bytes 294920 | tf_op jit(solution)/shard_map/ppermute | solution.py:680
  13.1 1.6 %collective-permute-start.1 = (bf16[32,1536]{1,0:T(8,128)(2,1)}, bf16[32,1536]{1,0:T(8,128)(2,1)S(1)}, u32[]{:S(2)}, u32[]{:S(2)}) collective-permute-start(bf16[32,1536]{1,0:T(8,128)(2,1)} %get-tuple-element.44), channel_id=1, source_target_pairs={{0,7},{1,2},{2,1},{3,4},{4,3},{5,6},{6,5},{7,0},{8,15},{9,10},{10,... | collective-permute-start | bytes 294920 | tf_op jit(solution)/shard_map/ppermute | solution.py:680
  14.7 1.2 collective-permute-start.3
  15.9 1.8 %collective-permute-start.4 = (bf16[32,1536]{1,0:T(8,128)(2,1)}, bf16[32,1536]{1,0:T(8,128)(2,1)S(1)}, u32[]{:S(2)}, u32[]{:S(2)}) collective-permute-start(bf16[32,1536]{1,0:T(8,128)(2,1)} %get-tuple-element.47), channel_id=1, source_target_pairs={{0,192},{64,128},{128,64},{192,0},{1,193},{65,129},{129,65},{193,1... | collective-permute-start | bytes 294920 | tf_op jit(solution)/shard_map/ppermute | solution.py:680
  17.7 0.0 collective-permute-done.refs_2_
  17.7 1.3 %collective-permute-start.5 = (bf16[32,1536]{1,0:T(8,128)(2,1)}, bf16[32,1536]{1,0:T(8,128)(2,1)S(1)}, u32[]{:S(2)}, u32[]{:S(2)}) collective-permute-start(bf16[32,1536]{1,0:T(8,128)(2,1)} %get-tuple-element.48), channel_id=1, source_target_pairs={{0,1},{1,0},{2,3},{3,2},{4,5},{5,4},{6,7},{7,6},{8,9},{9,8},{10,11... | collective-permute-start | bytes 294920 | tf_op jit(solution)/shard_map/ppermute | solution.py:680
  19.0 3.9 %prepare.1 = (f32[32,32,128]{2,1,0:T(8,128)}, bf16[4592,128]{1,0:T(8,128)(2,1)}, bf16[2160,128]{1,0:T(8,128)(2,1)}) custom-call(s32[32,128]{1,0:T(8,128)} %refs_0_.1, f32[3,32,128]{2,1,0:T(8,128)} %refs_1_.1, s32[1,128]{1,0:T(1,128)} %bitcast.12, bf16[128,1536]{1,0:T(8,128)(2,1)} %refs_3_.1, s32[1,128]{1,0:T(1,128)} %bitcast.6, ...), custom_call_target="tpu_custom_call" | custom-call | flops 10000000 | bytes 9000000 | tf_op jit(solution)/shard_map/prepare/pallas_call | solution.py:322
  22.9 0.0 collective-permute-done.3.refs_5_
  22.9 0.0 collective-permute-done.4.refs_6_
  22.9 1.0 copy-done.1
  23.9 1.3 copy-done.6
  25.2 9.7 %layer.3 = (bf16[1536,128]{1,0:T(8,128)(2,1)S(1)}, bf16[32,1536]{1,0:T(8,128)(2,1)S(1)}, bf16[32,1536]{1,0:T(8,128)(2,1)S(1)}, bf16[32,1536]{1,0:T(8,128)(2,1)S(...) custom-call(f32[32,32,128]{2,1,0:T(8,128)S(1)} %copy-done.1, ...), custom_call_target="tpu_custom_call" | custom-call | flops 6442450944 | bytes 3000000 | tf_op jit(solution)/shard_map/layer/pallas_call | solution.py:503
  34.9 8.2 %collective-permute-start.6 = (bf16[32,1536]{1,0:T(8,128)(2,1)S(1)}, bf16[32,1536]{1,0:T(8,128)(2,1)S(1)}, u32[]{:S(2)}, u32[]{:S(2)}) collective-permute-start(bf16[32,1536]{1,0:T(8,128)(2,1)S(1)} %get-tuple-element.49), channel_id=1, source_target_pairs={{0,56},{8,16},{16,8},{24,32},{32,24},{40,48},{48,40},{56,0},{1,57}... | collective-permute-start | bytes 294920 | tf_op jit(solution)/shard_map/ppermute | solution.py:680
  43.1 1.4 %collective-permute-start.7 = (bf16[32,1536]{1,0:T(8,128)(2,1)S(1)}, bf16[32,1536]{1,0:T(8,128)(2,1)S(1)}, u32[]{:S(2)}, u32[]{:S(2)}) collective-permute-start(bf16[32,1536]{1,0:T(8,128)(2,1)S(1)} %get-tuple-element.50), channel_id=1, source_target_pairs={{0,7},{1,2},{2,1},{3,4},{4,3},{5,6},{6,5},{7,0},{8,15},{9,10},{10,... | collective-permute-start | bytes 294920 | tf_op jit(solution)/shard_map/ppermute | solution.py:680
  44.5 1.2 collective-permute-start.9
  45.7 1.8 %collective-permute-start.10 = (bf16[32,1536]{1,0:T(8,128)(2,1)S(1)}, bf16[32,1536]{1,0:T(8,128)(2,1)S(1)}, u32[]{:S(2)}, u32[]{:S(2)}) collective-permute-start(bf16[32,1536]{1,0:T(8,128)(2,1)S(1)} %get-tuple-element.53), channel_id=1, source_target_pairs={{0,192},{64,128},{128,64},{192,0},{1,193},{65,129},{129,65},{193,1... | collective-permute-start | bytes 294920 | tf_op jit(solution)/shard_map/ppermute | solution.py:680
  47.5 0.0 collective-permute-start.11
  47.6 1.0 hidden_units.2.refs_9_
  48.6 2.2 %collective-permute-done.7.refs_3_ = bf16[32,1536]{1,0:T(8,128)(2,1)S(1)} collective-permute-done((bf16[32,1536]{1,0:T(8,128)(2,1)S(1)}, bf16[32,1536]{1,0:T(8,128)(2,1)S(1)}, u32[]{:S(2)}, u32[]{:S(2)}) %collective-permute-start.7) | collective-permute-done | bytes 98336 | tf_op jit(solution)/shard_map/ppermute | solution.py:680
  50.8 0.3 collective-permute-done.10.refs_6_
  51.1 0.0 collective-permute-done.11.refs_7_
  51.1 9.9 %layer.4 = (bf16[1536,128]{1,0:T(8,128)(2,1)S(1)}, bf16[32,1536]{1,0:T(8,128)(2,1)S(1)}, bf16[32,1536]{1,0:T(8,128)(2,1)S(1)}, bf16[32,1536]{1,0:T(8,128)(2,1)S(...) custom-call(f32[32,32,128]{2,1,0:T(8,128)S(1)} %copy-done.2, ...), custom_call_target="tpu_custom_call" | custom-call | flops 6442450944 | bytes 3000000 | tf_op jit(solution)/shard_map/layer/pallas_call | solution.py:503
  61.1 5.1 %collective-permute-start.12 = (bf16[32,1536]{1,0:T(8,128)(2,1)S(1)}, bf16[32,1536]{1,0:T(8,128)(2,1)S(1)}, u32[]{:S(2)}, u32[]{:S(2)}) collective-permute-start(bf16[32,1536]{1,0:T(8,128)(2,1)S(1)} %get-tuple-element.56), channel_id=1, source_target_pairs={{0,56},{8,16},{16,8},{24,32},{32,24},{40,48},{48,40},{56,0},{1,57}... | collective-permute-start | bytes 294920 | tf_op jit(solution)/shard_map/ppermute | solution.py:680
  66.2 2.6 %collective-permute-start.13 = (bf16[32,1536]{1,0:T(8,128)(2,1)S(1)}, bf16[32,1536]{1,0:T(8,128)(2,1)S(1)}, u32[]{:S(2)}, u32[]{:S(2)}) collective-permute-start(bf16[32,1536]{1,0:T(8,128)(2,1)S(1)} %get-tuple-element.57), channel_id=1, source_target_pairs={{0,7},{1,2},{2,1},{3,4},{4,3},{5,6},{6,5},{7,0},{8,15},{9,10},{10,... | collective-permute-start | bytes 294920 | tf_op jit(solution)/shard_map/ppermute | solution.py:680
  68.8 1.5 %collective-permute-start.15 = (bf16[32,1536]{1,0:T(8,128)(2,1)S(1)}, bf16[32,1536]{1,0:T(8,128)(2,1)S(1)}, u32[]{:S(2)}, u32[]{:S(2)}) collective-permute-start(bf16[32,1536]{1,0:T(8,128)(2,1)S(1)} %get-tuple-element.59), channel_id=1, source_target_pairs={{0,64},{64,0},{128,192},{192,128},{1,65},{65,1},{129,193},{193,129... | collective-permute-start | bytes 294920 | tf_op jit(solution)/shard_map/ppermute | solution.py:680
  70.3 1.5 %collective-permute-start.16 = (bf16[32,1536]{1,0:T(8,128)(2,1)S(1)}, bf16[32,1536]{1,0:T(8,128)(2,1)S(1)}, u32[]{:S(2)}, u32[]{:S(2)}) collective-permute-start(bf16[32,1536]{1,0:T(8,128)(2,1)S(1)} %get-tuple-element.60), channel_id=1, source_target_pairs={{0,192},{64,128},{128,64},{192,0},{1,193},{65,129},{129,65},{193,1... | collective-permute-start | bytes 294920 | tf_op jit(solution)/shard_map/ppermute | solution.py:680
  71.9 1.0 collective-permute-start.17
  72.9 1.0 hidden_units.3.refs_9_
  73.9 0.7 collective-permute-done.13.refs_3_
  74.6 0.4 collective-permute-done.16.refs_6_
  75.0 10.7 %layer.5 = (bf16[128,1536]{1,0:T(8,128)(2,1)}, bf16[32,1024]{1,0:T(8,128)(2,1)S(1)}, bf16[32,1024]{1,0:T(8,128)(2,1)S(1)}, bf16[32,1024]{1,0:T(8,128)(2,1)S(1)},...) custom-call(f32[32,32,128]{2,1,0:T(8,128)S(1)} %copy-done.2, ...), custom_call_target="tpu_custom_call" | custom-call | flops 6442450944 | bytes 3000000 | tf_op jit(solution)/shard_map/layer/pallas_call | solution.py:503
  85.7 7.4 %collective-permute-start.18 = (bf16[32,1024]{1,0:T(8,128)(2,1)S(1)}, bf16[32,1024]{1,0:T(8,128)(2,1)S(1)}, u32[]{:S(2)}, u32[]{:S(2)}) collective-permute-start(bf16[32,1024]{1,0:T(8,128)(2,1)S(1)} %get-tuple-element.64), channel_id=1, source_target_pairs={{0,61},{1,60},{2,63},{3,62},{4,57},{5,56},{6,59},{7,58},{8,21},{9,... | collective-permute-start | bytes 196616 | tf_op jit(solution)/shard_map/ppermute | solution.py:703
  93.1 0.7 collective-permute-start.19
  93.8 0.0 collective-permute-start.20
  93.8 2.6 %collective-permute-start.21 = (bf16[32,1024]{1,0:T(8,128)(2,1)S(1)}, bf16[32,1024]{1,0:T(8,128)(2,1)S(1)}, u32[]{:S(2)}, u32[]{:S(2)}) collective-permute-start(bf16[32,1024]{1,0:T(8,128)(2,1)S(1)} %get-tuple-element.67), channel_id=1, source_target_pairs={{0,66},{1,67},{2,64},{3,65},{4,70},{5,71},{6,68},{7,69},{64,2},{65... | collective-permute-start | bytes 196616 | tf_op jit(solution)/shard_map/ppermute | solution.py:703
  96.4 4.0 %collective-permute-start.22 = (bf16[32,1024]{1,0:T(8,128)(2,1)S(1)}, bf16[32,1024]{1,0:T(8,128)(2,1)S(1)}, u32[]{:S(2)}, u32[]{:S(2)}) collective-permute-start(bf16[32,1024]{1,0:T(8,128)(2,1)S(1)} %get-tuple-element.68), channel_id=1, source_target_pairs={{0,195},{1,194},{2,193},{3,192},{4,199},{5,198},{6,197},{7,196},{6... | collective-permute-start | bytes 196616 | tf_op jit(solution)/shard_map/ppermute | solution.py:703
  100.4 0.6 collective-permute-done.21.refs_3_
  101.0 2.6 %collective-permute-done.22.refs_4_ = bf16[32,1024]{1,0:T(8,128)(2,1)S(1)} collective-permute-done((bf16[32,1024]{1,0:T(8,128)(2,1)S(1)}, bf16[32,1024]{1,0:T(8,128)(2,1)S(1)}, u32[]{:S(2)}, u32[]{:S(2)}) %collective-permute-start.22) | collective-permute-done | bytes 65568 | tf_op jit(solution)/shard_map/ppermute | solution.py:703
  103.6 2.8 %collective-permute-done.23.refs_5_ = bf16[32,1024]{1,0:T(8,128)(2,1)S(1)} collective-permute-done((bf16[32,1024]{1,0:T(8,128)(2,1)S(1)}, bf16[32,1024]{1,0:T(8,128)(2,1)S(1)}, u32[]{:S(2)}, u32[]{:S(2)}) %collective-permute-start.23) | collective-permute-done | bytes 65568 | tf_op jit(solution)/shard_map/ppermute | solution.py:696
  106.4 0.6 collect.1
  107.0 1.9 %collective-permute-start.27 = (bf16[64,1024]{1,0:T(8,128)(2,1)S(1)}, bf16[64,1024]{1,0:T(8,128)(2,1)S(1)}, u32[]{:S(2)}, u32[]{:S(2)}) collective-permute-start(bf16[64,1024]{1,0:T(8,128)(2,1)S(1)} %collect.1), channel_id=1, source_target_pairs={{0,6},{1,7},{2,4},{3,5},{4,2},{5,3},{6,0},{7,1},{8,14},{9,15},{10,... | collective-permute-start | bytes 393224 | tf_op jit(solution)/shard_map/ppermute | solution.py:685
  108.9 1.7 %collective-permute-start.25 = (bf16[64,1024]{1,0:T(8,128)(2,1)S(1)}, bf16[64,1024]{1,0:T(8,128)(2,1)S(1)}, u32[]{:S(2)}, u32[]{:S(2)}) collective-permute-start(bf16[64,1024]{1,0:T(8,128)(2,1)S(1)} %collect.1), channel_id=1, source_target_pairs={{0,2},{1,3},{2,0},{3,1},{4,6},{5,7},{6,4},{7,5},{8,10},{9,11},{10,... | collective-permute-start | bytes 393224 | tf_op jit(solution)/shard_map/ppermute | solution.py:685
  110.6 2.7 %probe_weights.1.weight_ref = bf16[32,1024,128]{2,1,0:T(8,128)(2,1)S(1)} custom-call(f32[3,32,128]{2,1,0:T(8,128)S(1)} %copy-done.7, s32[1,128]{1,0:T(1,128)S(1)} %bitcast.9, bf16[2160,128]{1,0:T(8,128)(2,1)S(1)} %copy-done), custom_call_target="tpu_custom_call" | custom-call | flops 3221225472 | bytes 9000000 | tf_op jit(solution)/shard_map/probe_weights/pallas_call | solution.py:550
  113.3 6.9 %collective-permute-done.26 = bf16[64,1024]{1,0:T(8,128)(2,1)S(1)} collective-permute-done((bf16[64,1024]{1,0:T(8,128)(2,1)S(1)}, bf16[64,1024]{1,0:T(8,128)(2,1)S(1)}, u32[]{:S(2)}, u32[]{:S(2)}) %collective-permute-start.26) | collective-permute-done | bytes 131104 | tf_op jit(solution)/shard_map/ppermute | solution.py:685
  120.2 1.0 collective-permute-start.28
  121.1 1.5 %collective-permute-done.28.far_ref = bf16[256,1024]{1,0:T(8,128)(2,1)S(1)} collective-permute-done((bf16[256,1024]{1,0:T(8,128)(2,1)S(1)}, bf16[256,1024]{1,0:T(8,128)(2,1)S(1)}, u32[]{:S(2)}, u32[]{:S(2)}) %collective-permute-start.28) | collective-permute-done | bytes 524320 | tf_op jit(solution)/shard_map/ppermute | solution.py:685
  122.7 4.4 %readout.1 = f32[1,128]{1,0:T(1,128)} custom-call(s32[32]{0:T(128)S(1)} %copy-done.5, s32[32,128]{1,0:T(8,128)S(1)} %copy-done.3, bf16[32,1024,128]{2,1,0:T(8,128)(2,1)S(1)} %probe_weights.1.weight_ref, bf16[256,1024]{1,0:T(8,128)(2,1)S(1)} %pad_maximum_fusion.near_ref, bf16[256,1024]{1,0:T(8,128)(2,1)S(1)} %collective-permute-done.28.far_ref), custom_call_target="tpu_custom_call" | custom-call | tf_op jit(solution)/shard_map/readout/pallas_call | solution.py:656
  (39 shorter events, 0.1 us)
Async XLA Ops:
  2.8 14.9 %collective-permute-start = (bf16[32,1536]{1,0:T(8,128)(2,1)}, bf16[32,1536]{1,0:T(8,128)(2,1)S(1)}, u32[]{:S(2)}, u32[]{:S(2)}) collective-permute-start(bf16[32,1536]{1,0:T(8,128)(2,1)} %get-tuple-element.43), channel_id=1, source_target_pairs={{0,56},{8,16},{16,8},{24,32},{32,24},{40,48},{48,40},{56,0},{1,57}... | collective-permute-start | bytes 294920 | tf_op jit(solution)/shard_map/ppermute | solution.py:680
  13.1 9.8 %collective-permute-start.1 = (bf16[32,1536]{1,0:T(8,128)(2,1)}, bf16[32,1536]{1,0:T(8,128)(2,1)S(1)}, u32[]{:S(2)}, u32[]{:S(2)}) collective-permute-start(bf16[32,1536]{1,0:T(8,128)(2,1)} %get-tuple-element.44), channel_id=1, source_target_pairs={{0,7},{1,2},{2,1},{3,4},{4,3},{5,6},{6,5},{7,0},{8,15},{9,10},{10,... | collective-permute-start | bytes 294920 | tf_op jit(solution)/shard_map/ppermute | solution.py:680
  14.7 8.2 %collective-permute-start.2 = (bf16[32,1536]{1,0:T(8,128)(2,1)}, bf16[32,1536]{1,0:T(8,128)(2,1)S(1)}, u32[]{:S(2)}, u32[]{:S(2)}) collective-permute-start(bf16[32,1536]{1,0:T(8,128)(2,1)} %get-tuple-element.45), channel_id=1, source_target_pairs={{0,8},{8,0},{16,24},{24,16},{32,40},{40,32},{48,56},{56,48},{1,9},... | collective-permute-start | bytes 294920 | tf_op jit(solution)/shard_map/ppermute | solution.py:680
  14.7 8.2 %collective-permute-start.3 = (bf16[32,1536]{1,0:T(8,128)(2,1)}, bf16[32,1536]{1,0:T(8,128)(2,1)S(1)}, u32[]{:S(2)}, u32[]{:S(2)}) collective-permute-start(bf16[32,1536]{1,0:T(8,128)(2,1)} %get-tuple-element.46), channel_id=1, source_target_pairs={{0,64},{64,0},{128,192},{192,128},{1,65},{65,1},{129,193},{193,129... | collective-permute-start | bytes 294920 | tf_op jit(solution)/shard_map/ppermute | solution.py:680
  15.9 7.0 %collective-permute-start.4 = (bf16[32,1536]{1,0:T(8,128)(2,1)}, bf16[32,1536]{1,0:T(8,128)(2,1)S(1)}, u32[]{:S(2)}, u32[]{:S(2)}) collective-permute-start(bf16[32,1536]{1,0:T(8,128)(2,1)} %get-tuple-element.47), channel_id=1, source_target_pairs={{0,192},{64,128},{128,64},{192,0},{1,193},{65,129},{129,65},{193,1... | collective-permute-start | bytes 294920 | tf_op jit(solution)/shard_map/ppermute | solution.py:680
  17.7 5.2 %collective-permute-start.5 = (bf16[32,1536]{1,0:T(8,128)(2,1)}, bf16[32,1536]{1,0:T(8,128)(2,1)S(1)}, u32[]{:S(2)}, u32[]{:S(2)}) collective-permute-start(bf16[32,1536]{1,0:T(8,128)(2,1)} %get-tuple-element.48), channel_id=1, source_target_pairs={{0,1},{1,0},{2,3},{3,2},{4,5},{5,4},{6,7},{7,6},{8,9},{9,8},{10,11... | collective-permute-start | bytes 294920 | tf_op jit(solution)/shard_map/ppermute | solution.py:680
  22.9 1.0 copy-start.1
  23.9 1.3 copy-start.6
  25.2 22.3 %copy-start = (bf16[2160,128]{1,0:T(8,128)(2,1)S(1)}, bf16[2160,128]{1,0:T(8,128)(2,1)}, u32[]{:S(2)}) copy-start(bf16[2160,128]{1,0:T(8,128)(2,1)} %get-tuple-element.41.pack_ref.refs_1_) | copy-start | bytes 1658884
  25.2 22.3 %copy-start.2 = (f32[32,32,128]{2,1,0:T(8,128)S(1)}, f32[32,32,128]{2,1,0:T(8,128)}, u32[]{:S(2)}) copy-start(f32[32,32,128]{2,1,0:T(8,128)} %get-tuple-element.40.refs_0_.geo_ref) | copy-start | bytes 1572868
  25.2 22.3 %copy-start.4 = (s32[128]{0:T(128)S(1)}, s32[128]{0:T(128)}, u32[]{:S(2)}) copy-start(s32[128]{0:T(128)} %param.20) | copy-start | bytes 1540
  34.9 12.6 %collective-permute-start.6 = (bf16[32,1536]{1,0:T(8,128)(2,1)S(1)}, bf16[32,1536]{1,0:T(8,128)(2,1)S(1)}, u32[]{:S(2)}, u32[]{:S(2)}) collective-permute-start(bf16[32,1536]{1,0:T(8,128)(2,1)S(1)} %get-tuple-element.49), channel_id=1, source_target_pairs={{0,56},{8,16},{16,8},{24,32},{32,24},{40,48},{48,40},{56,0},{1,57}... | collective-permute-start | bytes 294920 | tf_op jit(solution)/shard_map/ppermute | solution.py:680
  43.1 7.6 %collective-permute-start.7 = (bf16[32,1536]{1,0:T(8,128)(2,1)S(1)}, bf16[32,1536]{1,0:T(8,128)(2,1)S(1)}, u32[]{:S(2)}, u32[]{:S(2)}) collective-permute-start(bf16[32,1536]{1,0:T(8,128)(2,1)S(1)} %get-tuple-element.50), channel_id=1, source_target_pairs={{0,7},{1,2},{2,1},{3,4},{4,3},{5,6},{6,5},{7,0},{8,15},{9,10},{10,... | collective-permute-start | bytes 294920 | tf_op jit(solution)/shard_map/ppermute | solution.py:680
  44.5 6.3 %collective-permute-start.8 = (bf16[32,1536]{1,0:T(8,128)(2,1)S(1)}, bf16[32,1536]{1,0:T(8,128)(2,1)S(1)}, u32[]{:S(2)}, u32[]{:S(2)}) collective-permute-start(bf16[32,1536]{1,0:T(8,128)(2,1)S(1)} %get-tuple-element.51), channel_id=1, source_target_pairs={{0,8},{8,0},{16,24},{24,16},{32,40},{40,32},{48,56},{56,48},{1,9},... | collective-permute-start | bytes 294920 | tf_op jit(solution)/shard_map/ppermute | solution.py:680
  44.5 6.3 %collective-permute-start.9 = (bf16[32,1536]{1,0:T(8,128)(2,1)S(1)}, bf16[32,1536]{1,0:T(8,128)(2,1)S(1)}, u32[]{:S(2)}, u32[]{:S(2)}) collective-permute-start(bf16[32,1536]{1,0:T(8,128)(2,1)S(1)} %get-tuple-element.52), channel_id=1, source_target_pairs={{0,64},{64,0},{128,192},{192,128},{1,65},{65,1},{129,193},{193,129... | collective-permute-start | bytes 294920 | tf_op jit(solution)/shard_map/ppermute | solution.py:680
  45.7 5.4 %collective-permute-start.10 = (bf16[32,1536]{1,0:T(8,128)(2,1)S(1)}, bf16[32,1536]{1,0:T(8,128)(2,1)S(1)}, u32[]{:S(2)}, u32[]{:S(2)}) collective-permute-start(bf16[32,1536]{1,0:T(8,128)(2,1)S(1)} %get-tuple-element.53), channel_id=1, source_target_pairs={{0,192},{64,128},{128,64},{192,0},{1,193},{65,129},{129,65},{193,1... | collective-permute-start | bytes 294920 | tf_op jit(solution)/shard_map/ppermute | solution.py:680
  47.5 3.6 %collective-permute-start.11 = (bf16[32,1536]{1,0:T(8,128)(2,1)S(1)}, bf16[32,1536]{1,0:T(8,128)(2,1)S(1)}, u32[]{:S(2)}, u32[]{:S(2)}) collective-permute-start(bf16[32,1536]{1,0:T(8,128)(2,1)S(1)} %get-tuple-element.54), channel_id=1, source_target_pairs={{0,1},{1,0},{2,3},{3,2},{4,5},{5,4},{6,7},{7,6},{8,9},{9,8},{10,11... | collective-permute-start | bytes 294920 | tf_op jit(solution)/shard_map/ppermute | solution.py:680
  61.1 10.8 %collective-permute-start.12 = (bf16[32,1536]{1,0:T(8,128)(2,1)S(1)}, bf16[32,1536]{1,0:T(8,128)(2,1)S(1)}, u32[]{:S(2)}, u32[]{:S(2)}) collective-permute-start(bf16[32,1536]{1,0:T(8,128)(2,1)S(1)} %get-tuple-element.56), channel_id=1, source_target_pairs={{0,56},{8,16},{16,8},{24,32},{32,24},{40,48},{48,40},{56,0},{1,57}... | collective-permute-start | bytes 294920 | tf_op jit(solution)/shard_map/ppermute | solution.py:680
  66.2 8.4 %collective-permute-start.13 = (bf16[32,1536]{1,0:T(8,128)(2,1)S(1)}, bf16[32,1536]{1,0:T(8,128)(2,1)S(1)}, u32[]{:S(2)}, u32[]{:S(2)}) collective-permute-start(bf16[32,1536]{1,0:T(8,128)(2,1)S(1)} %get-tuple-element.57), channel_id=1, source_target_pairs={{0,7},{1,2},{2,1},{3,4},{4,3},{5,6},{6,5},{7,0},{8,15},{9,10},{10,... | collective-permute-start | bytes 294920 | tf_op jit(solution)/shard_map/ppermute | solution.py:680
  68.8 5.8 %collective-permute-start.14 = (bf16[32,1536]{1,0:T(8,128)(2,1)S(1)}, bf16[32,1536]{1,0:T(8,128)(2,1)S(1)}, u32[]{:S(2)}, u32[]{:S(2)}) collective-permute-start(bf16[32,1536]{1,0:T(8,128)(2,1)S(1)} %get-tuple-element.58), channel_id=1, source_target_pairs={{0,8},{8,0},{16,24},{24,16},{32,40},{40,32},{48,56},{56,48},{1,9},... | collective-permute-start | bytes 294920 | tf_op jit(solution)/shard_map/ppermute | solution.py:680
  68.8 5.8 %collective-permute-start.15 = (bf16[32,1536]{1,0:T(8,128)(2,1)S(1)}, bf16[32,1536]{1,0:T(8,128)(2,1)S(1)}, u32[]{:S(2)}, u32[]{:S(2)}) collective-permute-start(bf16[32,1536]{1,0:T(8,128)(2,1)S(1)} %get-tuple-element.59), channel_id=1, source_target_pairs={{0,64},{64,0},{128,192},{192,128},{1,65},{65,1},{129,193},{193,129... | collective-permute-start | bytes 294920 | tf_op jit(solution)/shard_map/ppermute | solution.py:680
  70.3 4.7 %collective-permute-start.16 = (bf16[32,1536]{1,0:T(8,128)(2,1)S(1)}, bf16[32,1536]{1,0:T(8,128)(2,1)S(1)}, u32[]{:S(2)}, u32[]{:S(2)}) collective-permute-start(bf16[32,1536]{1,0:T(8,128)(2,1)S(1)} %get-tuple-element.60), channel_id=1, source_target_pairs={{0,192},{64,128},{128,64},{192,0},{1,193},{65,129},{129,65},{193,1... | collective-permute-start | bytes 294920 | tf_op jit(solution)/shard_map/ppermute | solution.py:680
  71.9 3.1 %collective-permute-start.17 = (bf16[32,1536]{1,0:T(8,128)(2,1)S(1)}, bf16[32,1536]{1,0:T(8,128)(2,1)S(1)}, u32[]{:S(2)}, u32[]{:S(2)}) collective-permute-start(bf16[32,1536]{1,0:T(8,128)(2,1)S(1)} %get-tuple-element.61), channel_id=1, source_target_pairs={{0,1},{1,0},{2,3},{3,2},{4,5},{5,4},{6,7},{7,6},{8,9},{9,8},{10,11... | collective-permute-start | bytes 294920 | tf_op jit(solution)/shard_map/ppermute | solution.py:680
  75.0 31.3 %copy-start.5 = (s32[32]{0:T(128)S(1)}, s32[32]{0:T(128)}, u32[]{:S(2)}) copy-start(s32[32]{0:T(128)} %slab_ref.3) | copy-start | bytes 388
  75.0 35.6 %copy-start.7 = (f32[3,32,128]{2,1,0:T(8,128)S(1)}, f32[3,32,128]{2,1,0:T(8,128)}, u32[]{:S(2)}) copy-start(f32[3,32,128]{2,1,0:T(8,128)} %vec_ref.1) | copy-start | bytes 147460
  75.0 35.6 %copy-start.8 = (s32[128]{0:T(128)S(1)}, s32[128]{0:T(128)}, u32[]{:S(2)}) copy-start(s32[128]{0:T(128)} %param.36) | copy-start | bytes 1540
  85.7 37.0 %copy-start.3 = (s32[32,128]{1,0:T(8,128)S(1)}, s32[32,128]{1,0:T(8,128)}, u32[]{:S(2)}) copy-start(s32[32,128]{1,0:T(8,128)} %idx_ref.1) | copy-start | bytes 49156
  85.7 10.7 %collective-permute-start.18 = (bf16[32,1024]{1,0:T(8,128)(2,1)S(1)}, bf16[32,1024]{1,0:T(8,128)(2,1)S(1)}, u32[]{:S(2)}, u32[]{:S(2)}) collective-permute-start(bf16[32,1024]{1,0:T(8,128)(2,1)S(1)} %get-tuple-element.64), channel_id=1, source_target_pairs={{0,61},{1,60},{2,63},{3,62},{4,57},{5,56},{6,59},{7,58},{8,21},{9,... | collective-permute-start | bytes 196616 | tf_op jit(solution)/shard_map/ppermute | solution.py:703
  93.1 7.3 %collective-permute-start.19 = (bf16[32,1024]{1,0:T(8,128)(2,1)S(1)}, bf16[32,1024]{1,0:T(8,128)(2,1)S(1)}, u32[]{:S(2)}, u32[]{:S(2)}) collective-permute-start(bf16[32,1024]{1,0:T(8,128)(2,1)S(1)} %get-tuple-element.65), channel_id=1, source_target_pairs={{0,3},{1,6},{2,5},{3,0},{4,7},{5,2},{6,1},{7,4},{8,11},{9,14},{10,... | collective-permute-start | bytes 196616 | tf_op jit(solution)/shard_map/ppermute | solution.py:696
  93.8 12.6 %collective-permute-start.24 = (bf16[64,1024]{1,0:T(8,128)(2,1)S(1)}, bf16[64,1024]{1,0:T(8,128)(2,1)S(1)}, u32[]{:S(2)}, u32[]{:S(2)}) collective-permute-start(bf16[64,1024]{1,0:T(8,128)(2,1)S(1)} %get-tuple-element.71), channel_id=1, source_target_pairs={{0,1},{1,0},{2,3},{3,2},{4,5},{5,4},{6,7},{7,6},{8,9},{9,8},{10,11... | collective-permute-start | bytes 393224 | tf_op jit(solution)/shard_map/ppermute | solution.py:685
  93.8 6.6 %collective-permute-start.20 = (bf16[32,1024]{1,0:T(8,128)(2,1)S(1)}, bf16[32,1024]{1,0:T(8,128)(2,1)S(1)}, u32[]{:S(2)}, u32[]{:S(2)}) collective-permute-start(bf16[32,1024]{1,0:T(8,128)(2,1)S(1)} %get-tuple-element.66), channel_id=1, source_target_pairs={{0,12},{1,13},{2,14},{3,15},{4,8},{5,9},{6,10},{7,11},{8,4},{9,5},... | collective-permute-start | bytes 196616 | tf_op jit(solution)/shard_map/ppermute | solution.py:703
  93.8 7.2 %collective-permute-start.21 = (bf16[32,1024]{1,0:T(8,128)(2,1)S(1)}, bf16[32,1024]{1,0:T(8,128)(2,1)S(1)}, u32[]{:S(2)}, u32[]{:S(2)}) collective-permute-start(bf16[32,1024]{1,0:T(8,128)(2,1)S(1)} %get-tuple-element.67), channel_id=1, source_target_pairs={{0,66},{1,67},{2,64},{3,65},{4,70},{5,71},{6,68},{7,69},{64,2},{65... | collective-permute-start | bytes 196616 | tf_op jit(solution)/shard_map/ppermute | solution.py:703
  96.4 7.2 %collective-permute-start.22 = (bf16[32,1024]{1,0:T(8,128)(2,1)S(1)}, bf16[32,1024]{1,0:T(8,128)(2,1)S(1)}, u32[]{:S(2)}, u32[]{:S(2)}) collective-permute-start(bf16[32,1024]{1,0:T(8,128)(2,1)S(1)} %get-tuple-element.68), channel_id=1, source_target_pairs={{0,195},{1,194},{2,193},{3,192},{4,199},{5,198},{6,197},{7,196},{6... | collective-permute-start | bytes 196616 | tf_op jit(solution)/shard_map/ppermute | solution.py:703
  100.4 6.0 %collective-permute-start.23 = (bf16[32,1024]{1,0:T(8,128)(2,1)S(1)}, bf16[32,1024]{1,0:T(8,128)(2,1)S(1)}, u32[]{:S(2)}, u32[]{:S(2)}) collective-permute-start(bf16[32,1024]{1,0:T(8,128)(2,1)S(1)} %get-tuple-element.69), channel_id=1, source_target_pairs={{0,4},{1,5},{2,6},{3,7},{4,0},{5,1},{6,2},{7,3},{8,12},{9,13},{10,... | collective-permute-start | bytes 196616 | tf_op jit(solution)/shard_map/ppermute | solution.py:696
  107.0 6.3 %collective-permute-start.27 = (bf16[64,1024]{1,0:T(8,128)(2,1)S(1)}, bf16[64,1024]{1,0:T(8,128)(2,1)S(1)}, u32[]{:S(2)}, u32[]{:S(2)}) collective-permute-start(bf16[64,1024]{1,0:T(8,128)(2,1)S(1)} %collect.1), channel_id=1, source_target_pairs={{0,6},{1,7},{2,4},{3,5},{4,2},{5,3},{6,0},{7,1},{8,14},{9,15},{10,... | collective-permute-start | bytes 393224 | tf_op jit(solution)/shard_map/ppermute | solution.py:685
  108.9 11.3 %collective-permute-start.26 = (bf16[64,1024]{1,0:T(8,128)(2,1)S(1)}, bf16[64,1024]{1,0:T(8,128)(2,1)S(1)}, u32[]{:S(2)}, u32[]{:S(2)}) collective-permute-start(bf16[64,1024]{1,0:T(8,128)(2,1)S(1)} %collect.1), channel_id=1, source_target_pairs={{0,4},{1,5},{2,6},{3,7},{4,0},{5,1},{6,2},{7,3},{8,12},{9,13},{10,... | collective-permute-start | bytes 393224 | tf_op jit(solution)/shard_map/ppermute | solution.py:685
  108.9 11.3 %collective-permute-start.25 = (bf16[64,1024]{1,0:T(8,128)(2,1)S(1)}, bf16[64,1024]{1,0:T(8,128)(2,1)S(1)}, u32[]{:S(2)}, u32[]{:S(2)}) collective-permute-start(bf16[64,1024]{1,0:T(8,128)(2,1)S(1)} %collect.1), channel_id=1, source_target_pairs={{0,2},{1,3},{2,0},{3,1},{4,6},{5,7},{6,4},{7,5},{8,10},{9,11},{10,... | collective-permute-start | bytes 393224 | tf_op jit(solution)/shard_map/ppermute | solution.py:685
  120.2 2.5 %collective-permute-start.28 = (bf16[256,1024]{1,0:T(8,128)(2,1)S(1)}, bf16[256,1024]{1,0:T(8,128)(2,1)S(1)}, u32[]{:S(2)}, u32[]{:S(2)}) collective-permute-start(bf16[256,1024]{1,0:T(8,128)(2,1)S(1)} %pad_maximum_fusion.near_ref), channel_id=1, source_target_pairs={{0,1},{1,0},{2,3},{3,2},{4,5},{5,4},{6,7},{7,6},{8,9},{9,8},{10,11... | collective-permute-start | bytes 1572872 | tf_op jit(solution)/shard_map/ppermute | solution.py:685

commit v4 on v3

--- a/solution.py
+++ b/solution.py
@@ -22,7 +22,8 @@
 GHOSTS = 192
 TABLE = 320
 PADDED = 384
-HALF = 64
+PART = 48
+REST = 16
 CUTOFF = 4.0
 DEGREE = (0, 1, 1, 1, 2, 2, 2, 2, 2, 3, 3, 3, 3, 3, 3, 3)
 STARTS = (0, 1, 4, 9)
@@ -488,15 +489,19 @@
         ).astype(bf16)
         rows = dot_nt(jnp.concatenate([sel, ones], axis=0), keys).astype(bf16)
         for face in range(6):
-            out_refs[1 + face][...] = rows[face * FACE : (face + 1) * FACE]
-        out_refs[7][...] = rows[GHOSTS : GHOSTS + HALF]
-        out_refs[8][...] = rows[GHOSTS + HALF :]
+            out_refs[1 + face][:FACE, :] = rows[face * FACE : (face + 1) * FACE]
+        own = rows[GHOSTS:]
+        out_refs[5][FACE:, :] = own[2 * PART : 2 * PART + REST]
+        out_refs[7][...] = own[:PART]
+        out_refs[8][...] = own[PART : 2 * PART]
+        out_refs[9][...] = own[2 * PART + REST :]
 
 
 def layer(t, geo, pack, ghosts, more):
     last = t == LAYERS - 1
     if last:
-        shapes = [(ATOMS, WIDTH)] + [(FACE, COMPS * RH)] * 6 + [(HALF, COMPS * RH)] * 2
+        counts = (FACE, FACE, FACE, FACE, PART, FACE, PART, PART, REST)
+        shapes = [(ATOMS, WIDTH)] + [(count, COMPS * RH) for count in counts]
     else:
         shapes = [(WIDTH, ATOMS)] + [(FACE, WIDTH)] * 6
     lanes = STEP * ATOMS
@@ -562,7 +567,7 @@
     )(vectors, count, pack)
 
 
-HOLDERS = (2, 3, 4, 5, 5, 4)
+HOLDERS = (2, 3, 4, 5, 7, 6)
 
 
 def column_root(slab_ref):
@@ -570,7 +575,7 @@
 
 
 def collect_kernel(slab_ref, *refs):
-    *block_refs, low_ref, high_ref, out_ref = refs
+    *block_refs, low_ref, high_ref, rest_ref, out_ref = refs
     code = lax.axis_index("gz") ^ column_root(slab_ref)
 
     @pl.when(code == 0)
@@ -582,30 +587,27 @@
         out_ref[...] = high_ref[...]
 
     for block, holder in enumerate(HOLDERS):
-        at = FACE if block >= 4 else 0
 
         @pl.when(code == holder)
-        def _(block=block, at=at):
-            out_ref[at : at + FACE, :] = block_refs[SENT.index(block)][...]
-
-    @pl.when((code == 2) | (code == 3))
-    def _():
-        out_ref[FACE:, :] = jnp.zeros((HALF - FACE, COMPS * RH), bf16)
-
-    @pl.when(code > 5)
-    def _():
-        out_ref[...] = jnp.zeros_like(out_ref)
-
-
-def collect(slab, blocks, low, high):
+        def _(block=block, holder=holder):
+            out_ref[:FACE, :] = block_refs[SENT.index(block)][:FACE, :]
+            if holder == 6:
+                out_ref[FACE:, :] = block_refs[SENT.index(4)][FACE:, :]
+            elif holder == 2:
+                out_ref[FACE:, :] = rest_ref[...]
+            else:
+                out_ref[FACE:, :] = jnp.zeros((REST, COMPS * RH), bf16)
+
+
+def collect(slab, blocks, low, high, rest):
     return pl.pallas_call(
         collect_kernel,
-        in_specs=[pl.BlockSpec(memory_space=pltpu.SMEM)] + in_vmem(BLOCKS + 2),
+        in_specs=[pl.BlockSpec(memory_space=pltpu.SMEM)] + in_vmem(BLOCKS + 3),
         out_specs=pl.BlockSpec(memory_space=pltpu.VMEM),
-        out_shape=jax.ShapeDtypeStruct((HALF, COMPS * RH), bf16),
+        out_shape=jax.ShapeDtypeStruct((PART, COMPS * RH), bf16),
         compiler_params=params(),
         name="collect",
-    )(slab, *[blocks[b] for b in SENT], low, high)
+    )(slab, *[blocks[b] for b in SENT], low, high, rest)
 
 
 def readout_kernel(slab_ref, idx_ref, weight_ref, near_ref, far_ref, out_ref, keys_ref, acc_ref):
@@ -618,7 +620,7 @@
 
         def fetch(at, rows, holder, start):
             place = code ^ holder
-            start = pl.multiple_of(place // 2 * HALF + start, FACE)
+            start = pl.multiple_of(place // 2 * PART + start, REST)
 
             @pl.when(place % 2 == 0)
             def _():
@@ -628,13 +630,15 @@
             def _():
                 keys_ref[pl.ds(at, rows), :] = far_ref[pl.ds(start, rows), :]
 
-        fetch(0, HALF, 0, 0)
-        fetch(HALF, HALF, 1, 0)
+        fetch(0, PART, 0, 0)
+        fetch(PART, PART, 1, 0)
+        fetch(2 * PART, REST, 6, FACE)
+        fetch(2 * PART + REST, REST, 2, FACE)
         for block, holder in enumerate(HOLDERS):
             odd = (parity(0), parity(1), root % 2)[block // 2]
             face = jnp.where(odd == block % 2, block // 2 * 2 + 1, block // 2 * 2)
             at = pl.multiple_of(ATOMS + face * FACE, FACE)
-            fetch(at, FACE, holder, FACE if block >= 4 else 0)
+            fetch(at, FACE, holder, 0)
         acc_ref[...] = jnp.zeros_like(acc_ref)
 
     weight = jnp.concatenate([weight_ref[s] for s in range(WIDE)], axis=1)
@@ -660,8 +664,8 @@
             pl.BlockSpec(memory_space=pltpu.SMEM),
             whole(K, ATOMS),
             slots(COMPS * RH, ATOMS),
-            whole(4 * HALF, COMPS * RH),
-            whole(4 * HALF, COMPS * RH),
+            whole(4 * PART, COMPS * RH),
+            whole(4 * PART, COMPS * RH),
         ],
         out_specs=whole(1, ATOMS),
         scratch_shapes=[pltpu.VMEM((TABLE, COMPS * RH), bf16), pltpu.VMEM((8, ATOMS), f32)],
@@ -685,7 +689,7 @@
     return lax.ppermute(block, "gz", [(i, i ^ code) for i in range(lax.axis_size("gz"))])
 
 
-def column_keys(slab, blocks, low, high, probe_weight):
+def column_keys(slab, blocks, low, high, rest, probe_weight):
     landed = [None] * BLOCKS
     inner = lax.axis_size("gz")
     for block in SENT:
@@ -701,7 +705,7 @@
                 for j in range(inner)
             ]
             landed[block] = lax.ppermute(blocks[block], (axis, "gz"), pairs)
-    mine = collect(slab, landed, low, along_column(high, 1))
+    mine = collect(slab, landed, low, along_column(high, 1), along_column(rest, 2))
     moved = [along_column(mine, code) for code in (6, 4, 2)][::-1]
     *moved, probe_weight = lax.optimization_barrier((*moved, probe_weight))
     near = jnp.concatenate([mine] + moved, axis=0)
@@ -764,6 +768,7 @@
         outs[1:7],
         outs[7],
         outs[8],
+        outs[9],
         probe_weights(probe_vectors, probe_count.reshape(1, ATOMS), later),
     )
     density = readout(slab_index, probe_index, probe_weight, near, far)

time: 127 us -> 125 us (0.984)
  waiting for transfers between devices: 18.1 us -> 14 us
  starting transfers between devices: 59.8 us -> 61.8 us
    ppermute x2, starting transfers between devices: 0.67 us -> 3.75 us  [column_keys(): landed[block] = lax.ppermute(blocks[block], axis, pairs)]
    ppermute x2, waiting for transfers between devices: 2.78 us -> 0.01 us  [column_keys(): landed[block] = lax.ppermute(blocks[block], axis, pairs)]
    ppermute x5 -> x6, waiting for transfers between devices: 8.4 us -> 5.79 us  [along_column(): lax.ppermute(block, 'gz', [(i, i ^ code) for i in range(lax.axis_size('gz...]
    ppermute x4, waiting for transfers between devices: 3.18 us -> 4.75 us  [column_keys(): landed[block] = lax.ppermute(blocks[block], (axis, 'gz'), pairs)]
    ppermute x5 -> x6, starting transfers between devices: 4.59 us -> 4.12 us  [along_column(): lax.ppermute(block, 'gz', [(i, i ^ code) for i in range(lax.axis_size('gz...]
  transfers between devices with their start and end apart: 29 -> 30, of which waited for: 9 -> 8; matrix products, arithmetic and copies ran while one was open for 0% -> 0% of each run, Pallas kernels for 7% -> 7%
where the time goes in v4:
time: 125 us
  starting transfers between devices  61.8 us (49%)
  Pallas kernels  46 us (37%)
  waiting for transfers between devices  14 us (11%)
  local copies, waits for them, and re-layouts  2.33 us (2%)
    ppermute x18, starting transfers between devices, exchange(): landed[block] = lax.ppermute(blocks[block], axis, pairs)  40.6 us
    pallas_call x3, Pallas kernels, layer(): pl.pallas_call(functools.partial(layer_kernel, t), grid=(1,), in_specs=[w...  30.3 us
    ppermute x4, starting transfers between devices, column_keys(): landed[block] = lax.ppermute(blocks[block], (axis, 'gz'), pairs)  13.4 us
    ppermute x6, waiting for transfers between devices, along_column(): lax.ppermute(block, 'gz', [(i, i ^ code) for i in range(lax.axis_size('gz...  5.79 us
    ppermute x4, waiting for transfers between devices, column_keys(): landed[block] = lax.ppermute(blocks[block], (axis, 'gz'), pairs)  4.75 us
    pallas_call x1, Pallas kernels, readout(): pl.pallas_call(readout_kernel, grid=(STEPS,), in_specs=[pl.BlockSpec(memo...  4.39 us
    ppermute x6, starting transfers between devices, along_column(): lax.ppermute(block, 'gz', [(i, i ^ code) for i in range(lax.axis_size('gz...  4.12 us
    pallas_call x1, Pallas kernels, prepare(): pl.pallas_call(prepare_kernel, grid=(1,), in_specs=in_hbm(INPUTS), out_sp...  3.87 us
  transfers between devices with their start and end apart: 30, of which 8 were waited for; matrix products, arithmetic and copies ran while one was open for 0% of the time, Pallas kernels for 7%

profile of v4, /device:TPU:1, one launch (start us, length us, event | category | flops | bytes accessed | tf_op | source)
XLA Modules:
  0.0 125.0 jit_solution(10367327015177099737)
XLA Ops:
  0.6 2.2 %pick.1 = (bf16[192,128]{1,0:T(8,128)(2,1)}, bf16[32,1536]{1,0:T(8,128)(2,1)}, bf16[32,1536]{1,0:T(8,128)(2,1)}, bf16[32,1536]{1,0:T(8,128)(2,1)}, bf16[32,1536]...) custom-call(s32[2,2,2,8]{3,2,1,0:T(2,128)} %lists_hbm.1, bf16[128,1536]{1,0:T(8,128)(2,1)} %refs_3_.1), custom_call_target="tpu_custom_call" | custom-call | tf_op jit(solution)/shard_map/pick/pallas_call | solution.py:180
  2.8 10.3 %collective-permute-start = (bf16[32,1536]{1,0:T(8,128)(2,1)}, bf16[32,1536]{1,0:T(8,128)(2,1)S(1)}, u32[]{:S(2)}, u32[]{:S(2)}) collective-permute-start(bf16[32,1536]{1,0:T(8,128)(2,1)} %get-tuple-element.44), channel_id=1, source_target_pairs={{0,56},{8,16},{16,8},{24,32},{32,24},{40,48},{48,40},{56,0},{1,57}... | collective-permute-start | bytes 294920 | tf_op jit(solution)/shard_map/ppermute | solution.py:684
  13.1 1.6 %collective-permute-start.1 = (bf16[32,1536]{1,0:T(8,128)(2,1)}, bf16[32,1536]{1,0:T(8,128)(2,1)S(1)}, u32[]{:S(2)}, u32[]{:S(2)}) collective-permute-start(bf16[32,1536]{1,0:T(8,128)(2,1)} %get-tuple-element.45), channel_id=1, source_target_pairs={{0,7},{1,2},{2,1},{3,4},{4,3},{5,6},{6,5},{7,0},{8,15},{9,10},{10,... | collective-permute-start | bytes 294920 | tf_op jit(solution)/shard_map/ppermute | solution.py:684
  14.6 0.0 collective-permute-start.2
  14.6 1.2 collective-permute-start.3
  15.9 1.8 %collective-permute-start.4 = (bf16[32,1536]{1,0:T(8,128)(2,1)}, bf16[32,1536]{1,0:T(8,128)(2,1)S(1)}, u32[]{:S(2)}, u32[]{:S(2)}) collective-permute-start(bf16[32,1536]{1,0:T(8,128)(2,1)} %get-tuple-element.48), channel_id=1, source_target_pairs={{0,192},{64,128},{128,64},{192,0},{1,193},{65,129},{129,65},{193,1... | collective-permute-start | bytes 294920 | tf_op jit(solution)/shard_map/ppermute | solution.py:684
  17.7 1.3 %collective-permute-start.5 = (bf16[32,1536]{1,0:T(8,128)(2,1)}, bf16[32,1536]{1,0:T(8,128)(2,1)S(1)}, u32[]{:S(2)}, u32[]{:S(2)}) collective-permute-start(bf16[32,1536]{1,0:T(8,128)(2,1)} %get-tuple-element.49), channel_id=1, source_target_pairs={{0,1},{1,0},{2,3},{3,2},{4,5},{5,4},{6,7},{7,6},{8,9},{9,8},{10,11... | collective-permute-start | bytes 294920 | tf_op jit(solution)/shard_map/ppermute | solution.py:684
  19.0 3.9 %prepare.1 = (f32[32,32,128]{2,1,0:T(8,128)}, bf16[4592,128]{1,0:T(8,128)(2,1)}, bf16[2160,128]{1,0:T(8,128)(2,1)}) custom-call(s32[32,128]{1,0:T(8,128)} %refs_0_.1, f32[3,32,128]{2,1,0:T(8,128)} %refs_1_.1, s32[1,128]{1,0:T(1,128)} %bitcast.12, bf16[128,1536]{1,0:T(8,128)(2,1)} %refs_3_.1, s32[1,128]{1,0:T(1,128)} %bitcast.6, ...), custom_call_target="tpu_custom_call" | custom-call | flops 10000000 | bytes 9000000 | tf_op jit(solution)/shard_map/prepare/pallas_call | solution.py:323
  22.8 0.0 collective-permute-done.1.refs_3_
  22.8 0.0 collective-permute-done.2.refs_4_
  22.9 0.0 collective-permute-done.4.refs_6_
  22.9 0.0 collective-permute-done.5.refs_7_
  22.9 1.0 copy-done.1
  23.9 1.3 %copy-done.6 = bf16[4592,128]{1,0:T(8,128)(2,1)S(1)} copy-done((bf16[4592,128]{1,0:T(8,128)(2,1)S(1)}, bf16[4592,128]{1,0:T(8,128)(2,1)}, u32[]{:S(2)}) %copy-start.6) | copy-done | bytes 1175576
  25.2 9.7 %layer.3 = (bf16[1536,128]{1,0:T(8,128)(2,1)S(1)}, bf16[32,1536]{1,0:T(8,128)(2,1)S(1)}, bf16[32,1536]{1,0:T(8,128)(2,1)S(1)}, bf16[32,1536]{1,0:T(8,128)(2,1)S(...) custom-call(f32[32,32,128]{2,1,0:T(8,128)S(1)} %copy-done.1, ...), custom_call_target="tpu_custom_call" | custom-call | flops 6442450944 | bytes 3000000 | tf_op jit(solution)/shard_map/layer/pallas_call | solution.py:508
  34.9 8.2 %collective-permute-start.6 = (bf16[32,1536]{1,0:T(8,128)(2,1)S(1)}, bf16[32,1536]{1,0:T(8,128)(2,1)S(1)}, u32[]{:S(2)}, u32[]{:S(2)}) collective-permute-start(bf16[32,1536]{1,0:T(8,128)(2,1)S(1)} %get-tuple-element.50), channel_id=1, source_target_pairs={{0,56},{8,16},{16,8},{24,32},{32,24},{40,48},{48,40},{56,0},{1,57}... | collective-permute-start | bytes 294920 | tf_op jit(solution)/shard_map/ppermute | solution.py:684
  43.1 1.4 %collective-permute-start.7 = (bf16[32,1536]{1,0:T(8,128)(2,1)S(1)}, bf16[32,1536]{1,0:T(8,128)(2,1)S(1)}, u32[]{:S(2)}, u32[]{:S(2)}) collective-permute-start(bf16[32,1536]{1,0:T(8,128)(2,1)S(1)} %get-tuple-element.51), channel_id=1, source_target_pairs={{0,7},{1,2},{2,1},{3,4},{4,3},{5,6},{6,5},{7,0},{8,15},{9,10},{10,... | collective-permute-start | bytes 294920 | tf_op jit(solution)/shard_map/ppermute | solution.py:684
  44.5 1.2 collective-permute-start.9
  45.7 1.8 %collective-permute-start.10 = (bf16[32,1536]{1,0:T(8,128)(2,1)S(1)}, bf16[32,1536]{1,0:T(8,128)(2,1)S(1)}, u32[]{:S(2)}, u32[]{:S(2)}) collective-permute-start(bf16[32,1536]{1,0:T(8,128)(2,1)S(1)} %get-tuple-element.54), channel_id=1, source_target_pairs={{0,192},{64,128},{128,64},{192,0},{1,193},{65,129},{129,65},{193,1... | collective-permute-start | bytes 294920 | tf_op jit(solution)/shard_map/ppermute | solution.py:684
  47.5 0.0 collective-permute-start.11
  47.5 1.0 hidden_units.2.refs_9_
  48.6 2.2 %collective-permute-done.7.refs_3_ = bf16[32,1536]{1,0:T(8,128)(2,1)S(1)} collective-permute-done((bf16[32,1536]{1,0:T(8,128)(2,1)S(1)}, bf16[32,1536]{1,0:T(8,128)(2,1)S(1)}, u32[]{:S(2)}, u32[]{:S(2)}) %collective-permute-start.7) | collective-permute-done | bytes 98336 | tf_op jit(solution)/shard_map/ppermute | solution.py:684
  50.8 0.0 collective-permute-done.9.refs_5_
  50.8 0.3 collective-permute-done.10.refs_6_
  51.1 9.9 %layer.4 = (bf16[1536,128]{1,0:T(8,128)(2,1)S(1)}, bf16[32,1536]{1,0:T(8,128)(2,1)S(1)}, bf16[32,1536]{1,0:T(8,128)(2,1)S(1)}, bf16[32,1536]{1,0:T(8,128)(2,1)S(...) custom-call(f32[32,32,128]{2,1,0:T(8,128)S(1)} %copy-done.2, ...), custom_call_target="tpu_custom_call" | custom-call | flops 6442450944 | bytes 3000000 | tf_op jit(solution)/shard_map/layer/pallas_call | solution.py:508
  61.0 5.1 %collective-permute-start.12 = (bf16[32,1536]{1,0:T(8,128)(2,1)S(1)}, bf16[32,1536]{1,0:T(8,128)(2,1)S(1)}, u32[]{:S(2)}, u32[]{:S(2)}) collective-permute-start(bf16[32,1536]{1,0:T(8,128)(2,1)S(1)} %get-tuple-element.57), channel_id=1, source_target_pairs={{0,56},{8,16},{16,8},{24,32},{32,24},{40,48},{48,40},{56,0},{1,57}... | collective-permute-start | bytes 294920 | tf_op jit(solution)/shard_map/ppermute | solution.py:684
  66.2 2.9 %collective-permute-start.13 = (bf16[32,1536]{1,0:T(8,128)(2,1)S(1)}, bf16[32,1536]{1,0:T(8,128)(2,1)S(1)}, u32[]{:S(2)}, u32[]{:S(2)}) collective-permute-start(bf16[32,1536]{1,0:T(8,128)(2,1)S(1)} %get-tuple-element.58), channel_id=1, source_target_pairs={{0,7},{1,2},{2,1},{3,4},{4,3},{5,6},{6,5},{7,0},{8,15},{9,10},{10,... | collective-permute-start | bytes 294920 | tf_op jit(solution)/shard_map/ppermute | solution.py:684
  69.1 1.0 collective-permute-start.15
  70.1 2.0 %collective-permute-start.16 = (bf16[32,1536]{1,0:T(8,128)(2,1)S(1)}, bf16[32,1536]{1,0:T(8,128)(2,1)S(1)}, u32[]{:S(2)}, u32[]{:S(2)}) collective-permute-start(bf16[32,1536]{1,0:T(8,128)(2,1)S(1)} %get-tuple-element.61), channel_id=1, source_target_pairs={{0,192},{64,128},{128,64},{192,0},{1,193},{65,129},{129,65},{193,1... | collective-permute-start | bytes 294920 | tf_op jit(solution)/shard_map/ppermute | solution.py:684
  72.1 0.7 collective-permute-start.17
  72.8 1.0 hidden_units.3.refs_9_
  73.9 0.7 collective-permute-done.13.refs_3_
  74.6 0.1 collective-permute-done.16.refs_6_
  74.7 10.7 %layer.5 = (bf16[128,1536]{1,0:T(8,128)(2,1)}, bf16[32,1024]{1,0:T(8,128)(2,1)S(1)}, bf16[32,1024]{1,0:T(8,128)(2,1)S(1)}, bf16[32,1024]{1,0:T(8,128)(2,1)S(1)},...) custom-call(f32[32,32,128]{2,1,0:T(8,128)S(1)} %copy-done.2, ...), custom_call_target="tpu_custom_call" | custom-call | flops 6442450944 | bytes 3000000 | tf_op jit(solution)/shard_map/layer/pallas_call | solution.py:508
  85.4 7.6 %collective-permute-start.18 = (bf16[32,1024]{1,0:T(8,128)(2,1)S(1)}, bf16[32,1024]{1,0:T(8,128)(2,1)S(1)}, u32[]{:S(2)}, u32[]{:S(2)}) collective-permute-start(bf16[32,1024]{1,0:T(8,128)(2,1)S(1)} %get-tuple-element.65), channel_id=1, source_target_pairs={{0,61},{1,60},{2,63},{3,62},{4,57},{5,56},{6,59},{7,58},{8,21},{9,... | collective-permute-start | bytes 196616 | tf_op jit(solution)/shard_map/ppermute | solution.py:707
  93.0 3.7 %collective-permute-start.23 = (bf16[48,1024]{1,0:T(8,128)(2,1)S(1)}, bf16[48,1024]{1,0:T(8,128)(2,1)S(1)}, u32[]{:S(2)}, u32[]{:S(2)}) collective-permute-start(bf16[48,1024]{1,0:T(8,128)(2,1)S(1)} %get-tuple-element.70), channel_id=1, source_target_pairs={{0,6},{1,7},{2,4},{3,5},{4,2},{5,3},{6,0},{7,1},{8,14},{9,15},{10,... | collective-permute-start | bytes 294920 | tf_op jit(solution)/shard_map/ppermute | solution.py:700
  96.8 1.9 %collective-permute-start.21 = (bf16[32,1024]{1,0:T(8,128)(2,1)S(1)}, bf16[32,1024]{1,0:T(8,128)(2,1)S(1)}, u32[]{:S(2)}, u32[]{:S(2)}) collective-permute-start(bf16[32,1024]{1,0:T(8,128)(2,1)S(1)} %get-tuple-element.68), channel_id=1, source_target_pairs={{0,66},{1,67},{2,64},{3,65},{4,70},{5,71},{6,68},{7,69},{64,2},{65... | collective-permute-start | bytes 196616 | tf_op jit(solution)/shard_map/ppermute | solution.py:707
  98.8 3.8 %collective-permute-start.22 = (bf16[32,1024]{1,0:T(8,128)(2,1)S(1)}, bf16[32,1024]{1,0:T(8,128)(2,1)S(1)}, u32[]{:S(2)}, u32[]{:S(2)}) collective-permute-start(bf16[32,1024]{1,0:T(8,128)(2,1)S(1)} %get-tuple-element.69), channel_id=1, source_target_pairs={{0,195},{1,194},{2,193},{3,192},{4,199},{5,198},{6,197},{7,196},{6... | collective-permute-start | bytes 196616 | tf_op jit(solution)/shard_map/ppermute | solution.py:707
  102.6 0.5 collective-permute-done.21.refs_3_
  103.1 4.2 %collective-permute-done.22.refs_4_ = bf16[32,1024]{1,0:T(8,128)(2,1)S(1)} collective-permute-done((bf16[32,1024]{1,0:T(8,128)(2,1)S(1)}, bf16[32,1024]{1,0:T(8,128)(2,1)S(1)}, u32[]{:S(2)}, u32[]{:S(2)}) %collective-permute-start.22) | collective-permute-done | bytes 65568 | tf_op jit(solution)/shard_map/ppermute | solution.py:707
  107.3 0.6 collect.1
  108.0 1.3 %collective-permute-start.28 = (bf16[48,1024]{1,0:T(8,128)(2,1)S(1)}, bf16[48,1024]{1,0:T(8,128)(2,1)S(1)}, u32[]{:S(2)}, u32[]{:S(2)}) collective-permute-start(bf16[48,1024]{1,0:T(8,128)(2,1)S(1)} %collect.1), channel_id=1, source_target_pairs={{0,6},{1,7},{2,4},{3,5},{4,2},{5,3},{6,0},{7,1},{8,14},{9,15},{10,... | collective-permute-start | bytes 294920 | tf_op jit(solution)/shard_map/ppermute | solution.py:689
  109.2 2.4 %collective-permute-start.26 = (bf16[48,1024]{1,0:T(8,128)(2,1)S(1)}, bf16[48,1024]{1,0:T(8,128)(2,1)S(1)}, u32[]{:S(2)}, u32[]{:S(2)}) collective-permute-start(bf16[48,1024]{1,0:T(8,128)(2,1)S(1)} %collect.1), channel_id=1, source_target_pairs={{0,2},{1,3},{2,0},{3,1},{4,6},{5,7},{6,4},{7,5},{8,10},{9,11},{10,... | collective-permute-start | bytes 294920 | tf_op jit(solution)/shard_map/ppermute | solution.py:689
  111.6 2.7 %probe_weights.1.weight_ref = bf16[32,1024,128]{2,1,0:T(8,128)(2,1)S(1)} custom-call(f32[3,32,128]{2,1,0:T(8,128)S(1)} %copy-done.7, s32[1,128]{1,0:T(1,128)S(1)} %bitcast.9, bf16[2160,128]{1,0:T(8,128)(2,1)S(1)} %copy-done), custom_call_target="tpu_custom_call" | custom-call | flops 3221225472 | bytes 9000000 | tf_op jit(solution)/shard_map/probe_weights/pallas_call | solution.py:555
  114.3 4.4 %collective-permute-done.27 = bf16[48,1024]{1,0:T(8,128)(2,1)S(1)} collective-permute-done((bf16[48,1024]{1,0:T(8,128)(2,1)S(1)}, bf16[48,1024]{1,0:T(8,128)(2,1)S(1)}, u32[]{:S(2)}, u32[]{:S(2)}) %collective-permute-start.27) | collective-permute-done | bytes 98336 | tf_op jit(solution)/shard_map/ppermute | solution.py:689
  118.7 0.5 collective-permute-start.29
  119.2 1.3 %collective-permute-done.29.far_ref = bf16[192,1024]{1,0:T(8,128)(2,1)S(1)} collective-permute-done((bf16[192,1024]{1,0:T(8,128)(2,1)S(1)}, bf16[192,1024]{1,0:T(8,128)(2,1)S(1)}, u32[]{:S(2)}, u32[]{:S(2)}) %collective-permute-start.29) | collective-permute-done | bytes 393248 | tf_op jit(solution)/shard_map/ppermute | solution.py:689
  120.6 4.4 %readout.1 = f32[1,128]{1,0:T(1,128)} custom-call(s32[32]{0:T(128)S(1)} %copy-done.5, s32[32,128]{1,0:T(8,128)S(1)} %copy-done.3, bf16[32,1024,128]{2,1,0:T(8,128)(2,1)S(1)} %probe_weights.1.weight_ref, bf16[192,1024]{1,0:T(8,128)(2,1)S(1)} %pad_maximum_fusion.near_ref, bf16[192,1024]{1,0:T(8,128)(2,1)S(1)} %collective-permute-done.29.far_ref), custom_call_target="tpu_custom_call" | custom-call | tf_op jit(solution)/shard_map/readout/pallas_call | solution.py:660
  (41 shorter events, 0.1 us)
Async XLA Ops:
  2.8 14.9 %collective-permute-start = (bf16[32,1536]{1,0:T(8,128)(2,1)}, bf16[32,1536]{1,0:T(8,128)(2,1)S(1)}, u32[]{:S(2)}, u32[]{:S(2)}) collective-permute-start(bf16[32,1536]{1,0:T(8,128)(2,1)} %get-tuple-element.44), channel_id=1, source_target_pairs={{0,56},{8,16},{16,8},{24,32},{32,24},{40,48},{48,40},{56,0},{1,57}... | collective-permute-start | bytes 294920 | tf_op jit(solution)/shard_map/ppermute | solution.py:684
  13.1 9.8 %collective-permute-start.1 = (bf16[32,1536]{1,0:T(8,128)(2,1)}, bf16[32,1536]{1,0:T(8,128)(2,1)S(1)}, u32[]{:S(2)}, u32[]{:S(2)}) collective-permute-start(bf16[32,1536]{1,0:T(8,128)(2,1)} %get-tuple-element.45), channel_id=1, source_target_pairs={{0,7},{1,2},{2,1},{3,4},{4,3},{5,6},{6,5},{7,0},{8,15},{9,10},{10,... | collective-permute-start | bytes 294920 | tf_op jit(solution)/shard_map/ppermute | solution.py:684
  14.6 8.2 %collective-permute-start.2 = (bf16[32,1536]{1,0:T(8,128)(2,1)}, bf16[32,1536]{1,0:T(8,128)(2,1)S(1)}, u32[]{:S(2)}, u32[]{:S(2)}) collective-permute-start(bf16[32,1536]{1,0:T(8,128)(2,1)} %get-tuple-element.46), channel_id=1, source_target_pairs={{0,8},{8,0},{16,24},{24,16},{32,40},{40,32},{48,56},{56,48},{1,9},... | collective-permute-start | bytes 294920 | tf_op jit(solution)/shard_map/ppermute | solution.py:684
  14.6 8.2 %collective-permute-start.3 = (bf16[32,1536]{1,0:T(8,128)(2,1)}, bf16[32,1536]{1,0:T(8,128)(2,1)S(1)}, u32[]{:S(2)}, u32[]{:S(2)}) collective-permute-start(bf16[32,1536]{1,0:T(8,128)(2,1)} %get-tuple-element.47), channel_id=1, source_target_pairs={{0,64},{64,0},{128,192},{192,128},{1,65},{65,1},{129,193},{193,129... | collective-permute-start | bytes 294920 | tf_op jit(solution)/shard_map/ppermute | solution.py:684
  15.9 7.0 %collective-permute-start.4 = (bf16[32,1536]{1,0:T(8,128)(2,1)}, bf16[32,1536]{1,0:T(8,128)(2,1)S(1)}, u32[]{:S(2)}, u32[]{:S(2)}) collective-permute-start(bf16[32,1536]{1,0:T(8,128)(2,1)} %get-tuple-element.48), channel_id=1, source_target_pairs={{0,192},{64,128},{128,64},{192,0},{1,193},{65,129},{129,65},{193,1... | collective-permute-start | bytes 294920 | tf_op jit(solution)/shard_map/ppermute | solution.py:684
  17.7 5.2 %collective-permute-start.5 = (bf16[32,1536]{1,0:T(8,128)(2,1)}, bf16[32,1536]{1,0:T(8,128)(2,1)S(1)}, u32[]{:S(2)}, u32[]{:S(2)}) collective-permute-start(bf16[32,1536]{1,0:T(8,128)(2,1)} %get-tuple-element.49), channel_id=1, source_target_pairs={{0,1},{1,0},{2,3},{3,2},{4,5},{5,4},{6,7},{7,6},{8,9},{9,8},{10,11... | collective-permute-start | bytes 294920 | tf_op jit(solution)/shard_map/ppermute | solution.py:684
  22.9 1.0 copy-start.1
  23.9 1.3 %copy-start.6 = (bf16[4592,128]{1,0:T(8,128)(2,1)S(1)}, bf16[4592,128]{1,0:T(8,128)(2,1)}, u32[]{:S(2)}) copy-start(bf16[4592,128]{1,0:T(8,128)(2,1)} %get-tuple-element.43.refs_1_) | copy-start | bytes 3526660
  25.2 22.3 %copy-start = (bf16[2160,128]{1,0:T(8,128)(2,1)S(1)}, bf16[2160,128]{1,0:T(8,128)(2,1)}, u32[]{:S(2)}) copy-start(bf16[2160,128]{1,0:T(8,128)(2,1)} %get-tuple-element.42.pack_ref.refs_1_) | copy-start | bytes 1658884
  25.2 22.3 %copy-start.2 = (f32[32,32,128]{2,1,0:T(8,128)S(1)}, f32[32,32,128]{2,1,0:T(8,128)}, u32[]{:S(2)}) copy-start(f32[32,32,128]{2,1,0:T(8,128)} %get-tuple-element.41.refs_0_.geo_ref) | copy-start | bytes 1572868
  25.2 22.3 %copy-start.4 = (s32[128]{0:T(128)S(1)}, s32[128]{0:T(128)}, u32[]{:S(2)}) copy-start(s32[128]{0:T(128)} %param.20) | copy-start | bytes 1540
  34.9 12.6 %collective-permute-start.6 = (bf16[32,1536]{1,0:T(8,128)(2,1)S(1)}, bf16[32,1536]{1,0:T(8,128)(2,1)S(1)}, u32[]{:S(2)}, u32[]{:S(2)}) collective-permute-start(bf16[32,1536]{1,0:T(8,128)(2,1)S(1)} %get-tuple-element.50), channel_id=1, source_target_pairs={{0,56},{8,16},{16,8},{24,32},{32,24},{40,48},{48,40},{56,0},{1,57}... | collective-permute-start | bytes 294920 | tf_op jit(solution)/shard_map/ppermute | solution.py:684
  43.1 7.6 %collective-permute-start.7 = (bf16[32,1536]{1,0:T(8,128)(2,1)S(1)}, bf16[32,1536]{1,0:T(8,128)(2,1)S(1)}, u32[]{:S(2)}, u32[]{:S(2)}) collective-permute-start(bf16[32,1536]{1,0:T(8,128)(2,1)S(1)} %get-tuple-element.51), channel_id=1, source_target_pairs={{0,7},{1,2},{2,1},{3,4},{4,3},{5,6},{6,5},{7,0},{8,15},{9,10},{10,... | collective-permute-start | bytes 294920 | tf_op jit(solution)/shard_map/ppermute | solution.py:684
  44.5 6.3 %collective-permute-start.8 = (bf16[32,1536]{1,0:T(8,128)(2,1)S(1)}, bf16[32,1536]{1,0:T(8,128)(2,1)S(1)}, u32[]{:S(2)}, u32[]{:S(2)}) collective-permute-start(bf16[32,1536]{1,0:T(8,128)(2,1)S(1)} %get-tuple-element.52), channel_id=1, source_target_pairs={{0,8},{8,0},{16,24},{24,16},{32,40},{40,32},{48,56},{56,48},{1,9},... | collective-permute-start | bytes 294920 | tf_op jit(solution)/shard_map/ppermute | solution.py:684
  44.5 6.3 %collective-permute-start.9 = (bf16[32,1536]{1,0:T(8,128)(2,1)S(1)}, bf16[32,1536]{1,0:T(8,128)(2,1)S(1)}, u32[]{:S(2)}, u32[]{:S(2)}) collective-permute-start(bf16[32,1536]{1,0:T(8,128)(2,1)S(1)} %get-tuple-element.53), channel_id=1, source_target_pairs={{0,64},{64,0},{128,192},{192,128},{1,65},{65,1},{129,193},{193,129... | collective-permute-start | bytes 294920 | tf_op jit(solution)/shard_map/ppermute | solution.py:684
  45.7 5.4 %collective-permute-start.10 = (bf16[32,1536]{1,0:T(8,128)(2,1)S(1)}, bf16[32,1536]{1,0:T(8,128)(2,1)S(1)}, u32[]{:S(2)}, u32[]{:S(2)}) collective-permute-start(bf16[32,1536]{1,0:T(8,128)(2,1)S(1)} %get-tuple-element.54), channel_id=1, source_target_pairs={{0,192},{64,128},{128,64},{192,0},{1,193},{65,129},{129,65},{193,1... | collective-permute-start | bytes 294920 | tf_op jit(solution)/shard_map/ppermute | solution.py:684
  47.5 3.6 %collective-permute-start.11 = (bf16[32,1536]{1,0:T(8,128)(2,1)S(1)}, bf16[32,1536]{1,0:T(8,128)(2,1)S(1)}, u32[]{:S(2)}, u32[]{:S(2)}) collective-permute-start(bf16[32,1536]{1,0:T(8,128)(2,1)S(1)} %get-tuple-element.55), channel_id=1, source_target_pairs={{0,1},{1,0},{2,3},{3,2},{4,5},{5,4},{6,7},{7,6},{8,9},{9,8},{10,11... | collective-permute-start | bytes 294920 | tf_op jit(solution)/shard_map/ppermute | solution.py:684
  61.0 11.1 %collective-permute-start.12 = (bf16[32,1536]{1,0:T(8,128)(2,1)S(1)}, bf16[32,1536]{1,0:T(8,128)(2,1)S(1)}, u32[]{:S(2)}, u32[]{:S(2)}) collective-permute-start(bf16[32,1536]{1,0:T(8,128)(2,1)S(1)} %get-tuple-element.57), channel_id=1, source_target_pairs={{0,56},{8,16},{16,8},{24,32},{32,24},{40,48},{48,40},{56,0},{1,57}... | collective-permute-start | bytes 294920 | tf_op jit(solution)/shard_map/ppermute | solution.py:684
  66.2 8.4 %collective-permute-start.13 = (bf16[32,1536]{1,0:T(8,128)(2,1)S(1)}, bf16[32,1536]{1,0:T(8,128)(2,1)S(1)}, u32[]{:S(2)}, u32[]{:S(2)}) collective-permute-start(bf16[32,1536]{1,0:T(8,128)(2,1)S(1)} %get-tuple-element.58), channel_id=1, source_target_pairs={{0,7},{1,2},{2,1},{3,4},{4,3},{5,6},{6,5},{7,0},{8,15},{9,10},{10,... | collective-permute-start | bytes 294920 | tf_op jit(solution)/shard_map/ppermute | solution.py:684
  69.1 5.5 %collective-permute-start.14 = (bf16[32,1536]{1,0:T(8,128)(2,1)S(1)}, bf16[32,1536]{1,0:T(8,128)(2,1)S(1)}, u32[]{:S(2)}, u32[]{:S(2)}) collective-permute-start(bf16[32,1536]{1,0:T(8,128)(2,1)S(1)} %get-tuple-element.59), channel_id=1, source_target_pairs={{0,8},{8,0},{16,24},{24,16},{32,40},{40,32},{48,56},{56,48},{1,9},... | collective-permute-start | bytes 294920 | tf_op jit(solution)/shard_map/ppermute | solution.py:684
  69.1 5.5 %collective-permute-start.15 = (bf16[32,1536]{1,0:T(8,128)(2,1)S(1)}, bf16[32,1536]{1,0:T(8,128)(2,1)S(1)}, u32[]{:S(2)}, u32[]{:S(2)}) collective-permute-start(bf16[32,1536]{1,0:T(8,128)(2,1)S(1)} %get-tuple-element.60), channel_id=1, source_target_pairs={{0,64},{64,0},{128,192},{192,128},{1,65},{65,1},{129,193},{193,129... | collective-permute-start | bytes 294920 | tf_op jit(solution)/shard_map/ppermute | solution.py:684
  70.1 4.7 %collective-permute-start.16 = (bf16[32,1536]{1,0:T(8,128)(2,1)S(1)}, bf16[32,1536]{1,0:T(8,128)(2,1)S(1)}, u32[]{:S(2)}, u32[]{:S(2)}) collective-permute-start(bf16[32,1536]{1,0:T(8,128)(2,1)S(1)} %get-tuple-element.61), channel_id=1, source_target_pairs={{0,192},{64,128},{128,64},{192,0},{1,193},{65,129},{129,65},{193,1... | collective-permute-start | bytes 294920 | tf_op jit(solution)/shard_map/ppermute | solution.py:684
  72.1 2.6 %collective-permute-start.17 = (bf16[32,1536]{1,0:T(8,128)(2,1)S(1)}, bf16[32,1536]{1,0:T(8,128)(2,1)S(1)}, u32[]{:S(2)}, u32[]{:S(2)}) collective-permute-start(bf16[32,1536]{1,0:T(8,128)(2,1)S(1)} %get-tuple-element.62), channel_id=1, source_target_pairs={{0,1},{1,0},{2,3},{3,2},{4,5},{5,4},{6,7},{7,6},{8,9},{9,8},{10,11... | collective-permute-start | bytes 294920 | tf_op jit(solution)/shard_map/ppermute | solution.py:684
  74.7 32.6 %copy-start.5 = (s32[32]{0:T(128)S(1)}, s32[32]{0:T(128)}, u32[]{:S(2)}) copy-start(s32[32]{0:T(128)} %slab_ref.3) | copy-start | bytes 388
  74.7 36.9 %copy-start.7 = (f32[3,32,128]{2,1,0:T(8,128)S(1)}, f32[3,32,128]{2,1,0:T(8,128)}, u32[]{:S(2)}) copy-start(f32[3,32,128]{2,1,0:T(8,128)} %vec_ref.1) | copy-start | bytes 147460
  74.7 36.9 %copy-start.8 = (s32[128]{0:T(128)S(1)}, s32[128]{0:T(128)}, u32[]{:S(2)}) copy-start(s32[128]{0:T(128)} %param.36) | copy-start | bytes 1540
  85.4 35.2 %copy-start.3 = (s32[32,128]{1,0:T(8,128)S(1)}, s32[32,128]{1,0:T(8,128)}, u32[]{:S(2)}) copy-start(s32[32,128]{1,0:T(8,128)} %idx_ref.1) | copy-start | bytes 49156
  85.4 11.4 %collective-permute-start.18 = (bf16[32,1024]{1,0:T(8,128)(2,1)S(1)}, bf16[32,1024]{1,0:T(8,128)(2,1)S(1)}, u32[]{:S(2)}, u32[]{:S(2)}) collective-permute-start(bf16[32,1024]{1,0:T(8,128)(2,1)S(1)} %get-tuple-element.65), channel_id=1, source_target_pairs={{0,61},{1,60},{2,63},{3,62},{4,57},{5,56},{6,59},{7,58},{8,21},{9,... | collective-permute-start | bytes 196616 | tf_op jit(solution)/shard_map/ppermute | solution.py:707
  93.0 5.7 %collective-permute-start.19 = (bf16[32,1024]{1,0:T(8,128)(2,1)S(1)}, bf16[32,1024]{1,0:T(8,128)(2,1)S(1)}, u32[]{:S(2)}, u32[]{:S(2)}) collective-permute-start(bf16[32,1024]{1,0:T(8,128)(2,1)S(1)} %get-tuple-element.66), channel_id=1, source_target_pairs={{0,1},{1,4},{2,7},{3,2},{4,5},{5,0},{6,3},{7,6},{8,9},{9,12},{10,1... | collective-permute-start | bytes 196616 | tf_op jit(solution)/shard_map/ppermute | solution.py:700
  93.0 3.8 %collective-permute-start.25 = (bf16[16,1024]{1,0:T(8,128)(2,1)S(1)}, bf16[16,1024]{1,0:T(8,128)(2,1)S(1)}, u32[]{:S(2)}, u32[]{:S(2)}) collective-permute-start(bf16[16,1024]{1,0:T(8,128)(2,1)S(1)} %get-tuple-element.73), channel_id=1, source_target_pairs={{0,2},{1,3},{2,0},{3,1},{4,6},{5,7},{6,4},{7,5},{8,10},{9,11},{10,... | collective-permute-start | bytes 98312 | tf_op jit(solution)/shard_map/ppermute | solution.py:689
  93.0 14.3 %collective-permute-start.23 = (bf16[48,1024]{1,0:T(8,128)(2,1)S(1)}, bf16[48,1024]{1,0:T(8,128)(2,1)S(1)}, u32[]{:S(2)}, u32[]{:S(2)}) collective-permute-start(bf16[48,1024]{1,0:T(8,128)(2,1)S(1)} %get-tuple-element.70), channel_id=1, source_target_pairs={{0,6},{1,7},{2,4},{3,5},{4,2},{5,3},{6,0},{7,1},{8,14},{9,15},{10,... | collective-permute-start | bytes 294920 | tf_op jit(solution)/shard_map/ppermute | solution.py:700
  96.8 10.5 %collective-permute-start.24 = (bf16[48,1024]{1,0:T(8,128)(2,1)S(1)}, bf16[48,1024]{1,0:T(8,128)(2,1)S(1)}, u32[]{:S(2)}, u32[]{:S(2)}) collective-permute-start(bf16[48,1024]{1,0:T(8,128)(2,1)S(1)} %get-tuple-element.72), channel_id=1, source_target_pairs={{0,1},{1,0},{2,3},{3,2},{4,5},{5,4},{6,7},{7,6},{8,9},{9,8},{10,11... | collective-permute-start | bytes 294920 | tf_op jit(solution)/shard_map/ppermute | solution.py:689
  96.8 5.8 %collective-permute-start.20 = (bf16[32,1024]{1,0:T(8,128)(2,1)S(1)}, bf16[32,1024]{1,0:T(8,128)(2,1)S(1)}, u32[]{:S(2)}, u32[]{:S(2)}) collective-permute-start(bf16[32,1024]{1,0:T(8,128)(2,1)S(1)} %get-tuple-element.67), channel_id=1, source_target_pairs={{0,12},{1,13},{2,14},{3,15},{4,8},{5,9},{6,10},{7,11},{8,4},{9,5},... | collective-permute-start | bytes 196616 | tf_op jit(solution)/shard_map/ppermute | solution.py:707
  96.8 6.3 %collective-permute-start.21 = (bf16[32,1024]{1,0:T(8,128)(2,1)S(1)}, bf16[32,1024]{1,0:T(8,128)(2,1)S(1)}, u32[]{:S(2)}, u32[]{:S(2)}) collective-permute-start(bf16[32,1024]{1,0:T(8,128)(2,1)S(1)} %get-tuple-element.68), channel_id=1, source_target_pairs={{0,66},{1,67},{2,64},{3,65},{4,70},{5,71},{6,68},{7,69},{64,2},{65... | collective-permute-start | bytes 196616 | tf_op jit(solution)/shard_map/ppermute | solution.py:707
  98.8 8.6 %collective-permute-start.22 = (bf16[32,1024]{1,0:T(8,128)(2,1)S(1)}, bf16[32,1024]{1,0:T(8,128)(2,1)S(1)}, u32[]{:S(2)}, u32[]{:S(2)}) collective-permute-start(bf16[32,1024]{1,0:T(8,128)(2,1)S(1)} %get-tuple-element.69), channel_id=1, source_target_pairs={{0,195},{1,194},{2,193},{3,192},{4,199},{5,198},{6,197},{7,196},{6... | collective-permute-start | bytes 196616 | tf_op jit(solution)/shard_map/ppermute | solution.py:707
  108.0 6.3 %collective-permute-start.28 = (bf16[48,1024]{1,0:T(8,128)(2,1)S(1)}, bf16[48,1024]{1,0:T(8,128)(2,1)S(1)}, u32[]{:S(2)}, u32[]{:S(2)}) collective-permute-start(bf16[48,1024]{1,0:T(8,128)(2,1)S(1)} %collect.1), channel_id=1, source_target_pairs={{0,6},{1,7},{2,4},{3,5},{4,2},{5,3},{6,0},{7,1},{8,14},{9,15},{10,... | collective-permute-start | bytes 294920 | tf_op jit(solution)/shard_map/ppermute | solution.py:689
  109.2 9.5 %collective-permute-start.27 = (bf16[48,1024]{1,0:T(8,128)(2,1)S(1)}, bf16[48,1024]{1,0:T(8,128)(2,1)S(1)}, u32[]{:S(2)}, u32[]{:S(2)}) collective-permute-start(bf16[48,1024]{1,0:T(8,128)(2,1)S(1)} %collect.1), channel_id=1, source_target_pairs={{0,4},{1,5},{2,6},{3,7},{4,0},{5,1},{6,2},{7,3},{8,12},{9,13},{10,... | collective-permute-start | bytes 294920 | tf_op jit(solution)/shard_map/ppermute | solution.py:689
  109.2 9.5 %collective-permute-start.26 = (bf16[48,1024]{1,0:T(8,128)(2,1)S(1)}, bf16[48,1024]{1,0:T(8,128)(2,1)S(1)}, u32[]{:S(2)}, u32[]{:S(2)}) collective-permute-start(bf16[48,1024]{1,0:T(8,128)(2,1)S(1)} %collect.1), channel_id=1, source_target_pairs={{0,2},{1,3},{2,0},{3,1},{4,6},{5,7},{6,4},{7,5},{8,10},{9,11},{10,... | collective-permute-start | bytes 294920 | tf_op jit(solution)/shard_map/ppermute | solution.py:689
  118.7 1.8 %collective-permute-start.29 = (bf16[192,1024]{1,0:T(8,128)(2,1)S(1)}, bf16[192,1024]{1,0:T(8,128)(2,1)S(1)}, u32[]{:S(2)}, u32[]{:S(2)}) collective-permute-start(bf16[192,1024]{1,0:T(8,128)(2,1)S(1)} %pad_maximum_fusion.near_ref), channel_id=1, source_target_pairs={{0,1},{1,0},{2,3},{3,2},{4,5},{5,4},{6,7},{7,6},{8,9},{9,8},{10,11... | collective-permute-start | bytes 1179656 | tf_op jit(solution)/shard_map/ppermute | solution.py:689

commit v5 on v4

--- a/solution.py
+++ b/solution.py
@@ -31,7 +31,7 @@
 STEP = 2
 PAIRS = K // (2 * STEP)
 PARTS = 3
-WIDE = 16
+WIDE = 8
 STEPS = K // WIDE
 ENV_ROW = 16
 INDEX_ROW = 17
@@ -610,67 +610,55 @@
     )(slab, *[blocks[b] for b in SENT], low, high, rest)
 
 
-def readout_kernel(slab_ref, idx_ref, weight_ref, near_ref, far_ref, out_ref, keys_ref, acc_ref):
-    step = pl.program_id(0)
-
-    @pl.when(step == 0)
-    def _():
-        root = column_root(slab_ref)
-        code = lax.axis_index("gz") ^ root
-
-        def fetch(at, rows, holder, start):
-            place = code ^ holder
-            start = pl.multiple_of(place // 2 * PART + start, REST)
-
-            @pl.when(place % 2 == 0)
-            def _():
-                keys_ref[pl.ds(at, rows), :] = near_ref[pl.ds(start, rows), :]
-
-            @pl.when(place % 2 == 1)
-            def _():
-                keys_ref[pl.ds(at, rows), :] = far_ref[pl.ds(start, rows), :]
-
-        fetch(0, PART, 0, 0)
-        fetch(PART, PART, 1, 0)
-        fetch(2 * PART, REST, 6, FACE)
-        fetch(2 * PART + REST, REST, 2, FACE)
-        for block, holder in enumerate(HOLDERS):
-            odd = (parity(0), parity(1), root % 2)[block // 2]
-            face = jnp.where(odd == block % 2, block // 2 * 2 + 1, block // 2 * 2)
-            at = pl.multiple_of(ATOMS + face * FACE, FACE)
-            fetch(at, FACE, holder, 0)
-        acc_ref[...] = jnp.zeros_like(acc_ref)
-
-    weight = jnp.concatenate([weight_ref[s] for s in range(WIDE)], axis=1)
-    product = dot(keys_ref[...], weight)
+def readout_kernel(slab_ref, idx_ref, weight_ref, near_ref, far_ref, out_ref, keys_ref):
+    root = column_root(slab_ref)
+    code = lax.axis_index("gz") ^ root
+
+    def fetch(at, rows, holder, start):
+        place = code ^ holder
+        start = pl.multiple_of(place // 2 * PART + start, REST)
+
+        @pl.when(place % 2 == 0)
+        def _():
+            keys_ref[pl.ds(at, rows), :] = near_ref[pl.ds(start, rows), :]
+
+        @pl.when(place % 2 == 1)
+        def _():
+            keys_ref[pl.ds(at, rows), :] = far_ref[pl.ds(start, rows), :]
+
+    fetch(0, PART, 0, 0)
+    fetch(PART, PART, 1, 0)
+    fetch(2 * PART, REST, 6, FACE)
+    fetch(2 * PART + REST, REST, 2, FACE)
+    for block, holder in enumerate(HOLDERS):
+        odd = (parity(0), parity(1), root % 2)[block // 2]
+        face = jnp.where(odd == block % 2, block // 2 * 2 + 1, block // 2 * 2)
+        at = pl.multiple_of(ATOMS + face * FACE, FACE)
+        fetch(at, FACE, holder, 0)
     rows = lax.broadcasted_iota(jnp.int32, (TABLE, ATOMS), 0)
-    total = acc_ref[...]
-    for s in range(WIDE):
-        chosen = rows == idx_ref[pl.ds(step * WIDE + s, 1), :]
-        part = jnp.where(chosen, product[:, s * ATOMS : (s + 1) * ATOMS], 0.0)
-        total = total + jnp.sum(part.reshape(TABLE // 8, 8, ATOMS), axis=0)
-    acc_ref[...] = total
-
-    @pl.when(step == STEPS - 1)
-    def _():
-        out_ref[...] = jnp.sum(acc_ref[...], axis=0, keepdims=True)
+
+    def one_step(step, total):
+        first = step * WIDE
+        weight = jnp.concatenate([weight_ref[first + s] for s in range(WIDE)], axis=1)
+        product = dot(keys_ref[...], weight)
+        for s in range(WIDE):
+            chosen = rows == idx_ref[pl.ds(first + s, 1), :]
+            part = jnp.where(chosen, product[:, s * ATOMS : (s + 1) * ATOMS], 0.0)
+            total = total + jnp.sum(part.reshape(TABLE // 8, 8, ATOMS), axis=0)
+        return total
+
+    total = lax.fori_loop(0, STEPS, one_step, jnp.zeros((8, ATOMS), f32))
+    out_ref[...] = jnp.sum(total, axis=0, keepdims=True)
 
 
 def readout(slab, idx, weight, near, far):
     return pl.pallas_call(
         readout_kernel,
-        grid=(STEPS,),
-        in_specs=[
-            pl.BlockSpec(memory_space=pltpu.SMEM),
-            whole(K, ATOMS),
-            slots(COMPS * RH, ATOMS),
-            whole(4 * PART, COMPS * RH),
-            whole(4 * PART, COMPS * RH),
-        ],
-        out_specs=whole(1, ATOMS),
-        scratch_shapes=[pltpu.VMEM((TABLE, COMPS * RH), bf16), pltpu.VMEM((8, ATOMS), f32)],
+        in_specs=[pl.BlockSpec(memory_space=pltpu.SMEM)] + in_vmem(4),
+        out_specs=pl.BlockSpec(memory_space=pltpu.VMEM),
+        scratch_shapes=[pltpu.VMEM((TABLE, COMPS * RH), bf16)],
         out_shape=jax.ShapeDtypeStruct((1, ATOMS), f32),
-        compiler_params=params(("arbitrary",)),
+        compiler_params=params(),
         name="readout",
     )(slab, idx, weight, near, far)
 

time: 125 us -> 126 us (level)
  no operation moved by 1% of the time
where the time goes in v5:
time: 126 us; the launch traced here: 125 us
  starting transfers between devices  61.8 us (49%)
  Pallas kernels  47 us (37%)
  waiting for transfers between devices  13.3 us (11%)
  local copies, waits for them, and re-layouts  2.33 us (2%)
    ppermute x18, starting transfers between devices, exchange(): landed[block] = lax.ppermute(blocks[block], axis, pairs)  40.6 us
    pallas_call x3, Pallas kernels, layer(): pl.pallas_call(functools.partial(layer_kernel, t), grid=(1,), in_specs=[w...  30.3 us
    ppermute x4, starting transfers between devices, column_keys(): landed[block] = lax.ppermute(blocks[block], (axis, 'gz'), pairs)  13.4 us
    ppermute x6, waiting for transfers between devices, along_column(): lax.ppermute(block, 'gz', [(i, i ^ code) for i in range(lax.axis_size('gz...  5.12 us
    ppermute x4, waiting for transfers between devices, column_keys(): landed[block] = lax.ppermute(blocks[block], (axis, 'gz'), pairs)  4.75 us
    pallas_call x1, Pallas kernels, readout(): pl.pallas_call(readout_kernel, in_specs=[pl.BlockSpec(memory_space=pltpu....  4.71 us
    ppermute x6, starting transfers between devices, along_column(): lax.ppermute(block, 'gz', [(i, i ^ code) for i in range(lax.axis_size('gz...  4.12 us
    pallas_call x1, Pallas kernels, prepare(): pl.pallas_call(prepare_kernel, grid=(1,), in_specs=in_hbm(INPUTS), out_sp...  3.87 us
  transfers between devices with their start and end apart: 30, of which 8 were waited for; matrix products, arithmetic and copies ran while one was open for 0% of the time, Pallas kernels for 7%

profile of v5, /device:TPU:1, one launch (start us, length us, event | category | flops | bytes accessed | tf_op | source)
XLA Modules:
  0.0 125.3 jit_solution(16097370972182935882)
XLA Ops:
  0.6 2.2 %pick.1 = (bf16[192,128]{1,0:T(8,128)(2,1)}, bf16[32,1536]{1,0:T(8,128)(2,1)}, bf16[32,1536]{1,0:T(8,128)(2,1)}, bf16[32,1536]{1,0:T(8,128)(2,1)}, bf16[32,1536]...) custom-call(s32[2,2,2,8]{3,2,1,0:T(2,128)} %lists_hbm.1, bf16[128,1536]{1,0:T(8,128)(2,1)} %refs_3_.1), custom_call_target="tpu_custom_call" | custom-call | tf_op jit(solution)/shard_map/pick/pallas_call | solution.py:180
  2.8 10.3 %collective-permute-start = (bf16[32,1536]{1,0:T(8,128)(2,1)}, bf16[32,1536]{1,0:T(8,128)(2,1)S(1)}, u32[]{:S(2)}, u32[]{:S(2)}) collective-permute-start(bf16[32,1536]{1,0:T(8,128)(2,1)} %get-tuple-element.44), channel_id=1, source_target_pairs={{0,56},{8,16},{16,8},{24,32},{32,24},{40,48},{48,40},{56,0},{1,57}... | collective-permute-start | bytes 294920 | tf_op jit(solution)/shard_map/ppermute | solution.py:672
  13.1 1.6 %collective-permute-start.1 = (bf16[32,1536]{1,0:T(8,128)(2,1)}, bf16[32,1536]{1,0:T(8,128)(2,1)S(1)}, u32[]{:S(2)}, u32[]{:S(2)}) collective-permute-start(bf16[32,1536]{1,0:T(8,128)(2,1)} %get-tuple-element.45), channel_id=1, source_target_pairs={{0,7},{1,2},{2,1},{3,4},{4,3},{5,6},{6,5},{7,0},{8,15},{9,10},{10,... | collective-permute-start | bytes 294920 | tf_op jit(solution)/shard_map/ppermute | solution.py:672
  14.6 0.0 collective-permute-start.2
  14.6 1.2 collective-permute-start.3
  15.9 1.8 %collective-permute-start.4 = (bf16[32,1536]{1,0:T(8,128)(2,1)}, bf16[32,1536]{1,0:T(8,128)(2,1)S(1)}, u32[]{:S(2)}, u32[]{:S(2)}) collective-permute-start(bf16[32,1536]{1,0:T(8,128)(2,1)} %get-tuple-element.48), channel_id=1, source_target_pairs={{0,192},{64,128},{128,64},{192,0},{1,193},{65,129},{129,65},{193,1... | collective-permute-start | bytes 294920 | tf_op jit(solution)/shard_map/ppermute | solution.py:672
  17.7 1.3 %collective-permute-start.5 = (bf16[32,1536]{1,0:T(8,128)(2,1)}, bf16[32,1536]{1,0:T(8,128)(2,1)S(1)}, u32[]{:S(2)}, u32[]{:S(2)}) collective-permute-start(bf16[32,1536]{1,0:T(8,128)(2,1)} %get-tuple-element.49), channel_id=1, source_target_pairs={{0,1},{1,0},{2,3},{3,2},{4,5},{5,4},{6,7},{7,6},{8,9},{9,8},{10,11... | collective-permute-start | bytes 294920 | tf_op jit(solution)/shard_map/ppermute | solution.py:672
  19.0 3.9 %prepare.1 = (f32[32,32,128]{2,1,0:T(8,128)}, bf16[4592,128]{1,0:T(8,128)(2,1)}, bf16[2160,128]{1,0:T(8,128)(2,1)}) custom-call(s32[32,128]{1,0:T(8,128)} %refs_0_.1, f32[3,32,128]{2,1,0:T(8,128)} %refs_1_.1, s32[1,128]{1,0:T(1,128)} %bitcast.12, bf16[128,1536]{1,0:T(8,128)(2,1)} %refs_3_.1, s32[1,128]{1,0:T(1,128)} %bitcast.6, ...), custom_call_target="tpu_custom_call" | custom-call | flops 10000000 | bytes 9000000 | tf_op jit(solution)/shard_map/prepare/pallas_call | solution.py:323
  22.8 0.0 collective-permute-done.1.refs_3_
  22.8 0.0 collective-permute-done.2.refs_4_
  22.9 0.0 collective-permute-done.4.refs_6_
  22.9 0.0 collective-permute-done.5.refs_7_
  22.9 1.0 copy-done.1
  23.9 1.3 %copy-done.6 = bf16[4592,128]{1,0:T(8,128)(2,1)S(1)} copy-done((bf16[4592,128]{1,0:T(8,128)(2,1)S(1)}, bf16[4592,128]{1,0:T(8,128)(2,1)}, u32[]{:S(2)}) %copy-start.6) | copy-done | bytes 1175576
  25.2 9.7 %layer.3 = (bf16[1536,128]{1,0:T(8,128)(2,1)S(1)}, bf16[32,1536]{1,0:T(8,128)(2,1)S(1)}, bf16[32,1536]{1,0:T(8,128)(2,1)S(1)}, bf16[32,1536]{1,0:T(8,128)(2,1)S(...) custom-call(f32[32,32,128]{2,1,0:T(8,128)S(1)} %copy-done.1, ...), custom_call_target="tpu_custom_call" | custom-call | flops 6442450944 | bytes 3000000 | tf_op jit(solution)/shard_map/layer/pallas_call | solution.py:508
  34.9 8.2 %collective-permute-start.6 = (bf16[32,1536]{1,0:T(8,128)(2,1)S(1)}, bf16[32,1536]{1,0:T(8,128)(2,1)S(1)}, u32[]{:S(2)}, u32[]{:S(2)}) collective-permute-start(bf16[32,1536]{1,0:T(8,128)(2,1)S(1)} %get-tuple-element.50), channel_id=1, source_target_pairs={{0,56},{8,16},{16,8},{24,32},{32,24},{40,48},{48,40},{56,0},{1,57}... | collective-permute-start | bytes 294920 | tf_op jit(solution)/shard_map/ppermute | solution.py:672
  43.1 1.4 %collective-permute-start.7 = (bf16[32,1536]{1,0:T(8,128)(2,1)S(1)}, bf16[32,1536]{1,0:T(8,128)(2,1)S(1)}, u32[]{:S(2)}, u32[]{:S(2)}) collective-permute-start(bf16[32,1536]{1,0:T(8,128)(2,1)S(1)} %get-tuple-element.51), channel_id=1, source_target_pairs={{0,7},{1,2},{2,1},{3,4},{4,3},{5,6},{6,5},{7,0},{8,15},{9,10},{10,... | collective-permute-start | bytes 294920 | tf_op jit(solution)/shard_map/ppermute | solution.py:672
  44.5 1.2 collective-permute-start.9
  45.7 1.8 %collective-permute-start.10 = (bf16[32,1536]{1,0:T(8,128)(2,1)S(1)}, bf16[32,1536]{1,0:T(8,128)(2,1)S(1)}, u32[]{:S(2)}, u32[]{:S(2)}) collective-permute-start(bf16[32,1536]{1,0:T(8,128)(2,1)S(1)} %get-tuple-element.54), channel_id=1, source_target_pairs={{0,192},{64,128},{128,64},{192,0},{1,193},{65,129},{129,65},{193,1... | collective-permute-start | bytes 294920 | tf_op jit(solution)/shard_map/ppermute | solution.py:672
  47.5 0.0 collective-permute-start.11
  47.5 1.0 hidden_units.2.refs_9_
  48.6 2.2 %collective-permute-done.7.refs_3_ = bf16[32,1536]{1,0:T(8,128)(2,1)S(1)} collective-permute-done((bf16[32,1536]{1,0:T(8,128)(2,1)S(1)}, bf16[32,1536]{1,0:T(8,128)(2,1)S(1)}, u32[]{:S(2)}, u32[]{:S(2)}) %collective-permute-start.7) | collective-permute-done | bytes 98336 | tf_op jit(solution)/shard_map/ppermute | solution.py:672
  50.8 0.0 collective-permute-done.9.refs_5_
  50.8 0.3 collective-permute-done.10.refs_6_
  51.1 9.9 %layer.4 = (bf16[1536,128]{1,0:T(8,128)(2,1)S(1)}, bf16[32,1536]{1,0:T(8,128)(2,1)S(1)}, bf16[32,1536]{1,0:T(8,128)(2,1)S(1)}, bf16[32,1536]{1,0:T(8,128)(2,1)S(...) custom-call(f32[32,32,128]{2,1,0:T(8,128)S(1)} %copy-done.2, ...), custom_call_target="tpu_custom_call" | custom-call | flops 6442450944 | bytes 3000000 | tf_op jit(solution)/shard_map/layer/pallas_call | solution.py:508
  61.0 5.1 %collective-permute-start.12 = (bf16[32,1536]{1,0:T(8,128)(2,1)S(1)}, bf16[32,1536]{1,0:T(8,128)(2,1)S(1)}, u32[]{:S(2)}, u32[]{:S(2)}) collective-permute-start(bf16[32,1536]{1,0:T(8,128)(2,1)S(1)} %get-tuple-element.57), channel_id=1, source_target_pairs={{0,56},{8,16},{16,8},{24,32},{32,24},{40,48},{48,40},{56,0},{1,57}... | collective-permute-start | bytes 294920 | tf_op jit(solution)/shard_map/ppermute | solution.py:672
  66.2 2.9 %collective-permute-start.13 = (bf16[32,1536]{1,0:T(8,128)(2,1)S(1)}, bf16[32,1536]{1,0:T(8,128)(2,1)S(1)}, u32[]{:S(2)}, u32[]{:S(2)}) collective-permute-start(bf16[32,1536]{1,0:T(8,128)(2,1)S(1)} %get-tuple-element.58), channel_id=1, source_target_pairs={{0,7},{1,2},{2,1},{3,4},{4,3},{5,6},{6,5},{7,0},{8,15},{9,10},{10,... | collective-permute-start | bytes 294920 | tf_op jit(solution)/shard_map/ppermute | solution.py:672
  69.1 1.0 collective-permute-start.15
  70.1 2.0 %collective-permute-start.16 = (bf16[32,1536]{1,0:T(8,128)(2,1)S(1)}, bf16[32,1536]{1,0:T(8,128)(2,1)S(1)}, u32[]{:S(2)}, u32[]{:S(2)}) collective-permute-start(bf16[32,1536]{1,0:T(8,128)(2,1)S(1)} %get-tuple-element.61), channel_id=1, source_target_pairs={{0,192},{64,128},{128,64},{192,0},{1,193},{65,129},{129,65},{193,1... | collective-permute-start | bytes 294920 | tf_op jit(solution)/shard_map/ppermute | solution.py:672
  72.1 0.7 collective-permute-start.17
  72.8 1.0 hidden_units.3.refs_9_
  73.9 0.7 collective-permute-done.13.refs_3_
  74.6 0.1 collective-permute-done.16.refs_6_
  74.7 10.7 %layer.5 = (bf16[128,1536]{1,0:T(8,128)(2,1)}, bf16[32,1024]{1,0:T(8,128)(2,1)S(1)}, bf16[32,1024]{1,0:T(8,128)(2,1)S(1)}, bf16[32,1024]{1,0:T(8,128)(2,1)S(1)},...) custom-call(f32[32,32,128]{2,1,0:T(8,128)S(1)} %copy-done.2, ...), custom_call_target="tpu_custom_call" | custom-call | flops 6442450944 | bytes 3000000 | tf_op jit(solution)/shard_map/layer/pallas_call | solution.py:508
  85.4 7.6 %collective-permute-start.18 = (bf16[32,1024]{1,0:T(8,128)(2,1)S(1)}, bf16[32,1024]{1,0:T(8,128)(2,1)S(1)}, u32[]{:S(2)}, u32[]{:S(2)}) collective-permute-start(bf16[32,1024]{1,0:T(8,128)(2,1)S(1)} %get-tuple-element.65), channel_id=1, source_target_pairs={{0,61},{1,60},{2,63},{3,62},{4,57},{5,56},{6,59},{7,58},{8,21},{9,... | collective-permute-start | bytes 196616 | tf_op jit(solution)/shard_map/ppermute | solution.py:695
  93.0 3.7 %collective-permute-start.23 = (bf16[48,1024]{1,0:T(8,128)(2,1)S(1)}, bf16[48,1024]{1,0:T(8,128)(2,1)S(1)}, u32[]{:S(2)}, u32[]{:S(2)}) collective-permute-start(bf16[48,1024]{1,0:T(8,128)(2,1)S(1)} %get-tuple-element.70), channel_id=1, source_target_pairs={{0,6},{1,7},{2,4},{3,5},{4,2},{5,3},{6,0},{7,1},{8,14},{9,15},{10,... | collective-permute-start | bytes 294920 | tf_op jit(solution)/shard_map/ppermute | solution.py:688
  96.8 1.9 %collective-permute-start.21 = (bf16[32,1024]{1,0:T(8,128)(2,1)S(1)}, bf16[32,1024]{1,0:T(8,128)(2,1)S(1)}, u32[]{:S(2)}, u32[]{:S(2)}) collective-permute-start(bf16[32,1024]{1,0:T(8,128)(2,1)S(1)} %get-tuple-element.68), channel_id=1, source_target_pairs={{0,66},{1,67},{2,64},{3,65},{4,70},{5,71},{6,68},{7,69},{64,2},{65... | collective-permute-start | bytes 196616 | tf_op jit(solution)/shard_map/ppermute | solution.py:695
  98.8 3.8 %collective-permute-start.22 = (bf16[32,1024]{1,0:T(8,128)(2,1)S(1)}, bf16[32,1024]{1,0:T(8,128)(2,1)S(1)}, u32[]{:S(2)}, u32[]{:S(2)}) collective-permute-start(bf16[32,1024]{1,0:T(8,128)(2,1)S(1)} %get-tuple-element.69), channel_id=1, source_target_pairs={{0,195},{1,194},{2,193},{3,192},{4,199},{5,198},{6,197},{7,196},{6... | collective-permute-start | bytes 196616 | tf_op jit(solution)/shard_map/ppermute | solution.py:695
  102.6 0.5 collective-permute-done.21.refs_3_
  103.1 4.2 %collective-permute-done.22.refs_4_ = bf16[32,1024]{1,0:T(8,128)(2,1)S(1)} collective-permute-done((bf16[32,1024]{1,0:T(8,128)(2,1)S(1)}, bf16[32,1024]{1,0:T(8,128)(2,1)S(1)}, u32[]{:S(2)}, u32[]{:S(2)}) %collective-permute-start.22) | collective-permute-done | bytes 65568 | tf_op jit(solution)/shard_map/ppermute | solution.py:695
  107.3 0.6 collect.1
  108.0 1.3 %collective-permute-start.28 = (bf16[48,1024]{1,0:T(8,128)(2,1)S(1)}, bf16[48,1024]{1,0:T(8,128)(2,1)S(1)}, u32[]{:S(2)}, u32[]{:S(2)}) collective-permute-start(bf16[48,1024]{1,0:T(8,128)(2,1)S(1)} %collect.1), channel_id=1, source_target_pairs={{0,6},{1,7},{2,4},{3,5},{4,2},{5,3},{6,0},{7,1},{8,14},{9,15},{10,... | collective-permute-start | bytes 294920 | tf_op jit(solution)/shard_map/ppermute | solution.py:677
  109.2 2.4 %collective-permute-start.26 = (bf16[48,1024]{1,0:T(8,128)(2,1)S(1)}, bf16[48,1024]{1,0:T(8,128)(2,1)S(1)}, u32[]{:S(2)}, u32[]{:S(2)}) collective-permute-start(bf16[48,1024]{1,0:T(8,128)(2,1)S(1)} %collect.1), channel_id=1, source_target_pairs={{0,2},{1,3},{2,0},{3,1},{4,6},{5,7},{6,4},{7,5},{8,10},{9,11},{10,... | collective-permute-start | bytes 294920 | tf_op jit(solution)/shard_map/ppermute | solution.py:677
  111.6 3.3 %probe_weights.1.weight_ref = bf16[32,1024,128]{2,1,0:T(8,128)(2,1)S(1)} custom-call(f32[3,32,128]{2,1,0:T(8,128)S(1)} %copy-done.7, s32[1,128]{1,0:T(1,128)S(1)} %bitcast.9, bf16[2160,128]{1,0:T(8,128)(2,1)S(1)} %copy-done), custom_call_target="tpu_custom_call" | custom-call | flops 3221225472 | bytes 9000000 | tf_op jit(solution)/shard_map/probe_weights/pallas_call | solution.py:555
  115.0 3.8 %collective-permute-done.27 = bf16[48,1024]{1,0:T(8,128)(2,1)S(1)} collective-permute-done((bf16[48,1024]{1,0:T(8,128)(2,1)S(1)}, bf16[48,1024]{1,0:T(8,128)(2,1)S(1)}, u32[]{:S(2)}, u32[]{:S(2)}) %collective-permute-start.27) | collective-permute-done | bytes 98336 | tf_op jit(solution)/shard_map/ppermute | solution.py:677
  118.7 0.5 collective-permute-start.29
  119.2 1.3 %collective-permute-done.29.far_ref = bf16[192,1024]{1,0:T(8,128)(2,1)S(1)} collective-permute-done((bf16[192,1024]{1,0:T(8,128)(2,1)S(1)}, bf16[192,1024]{1,0:T(8,128)(2,1)S(1)}, u32[]{:S(2)}, u32[]{:S(2)}) %collective-permute-start.29) | collective-permute-done | bytes 393248 | tf_op jit(solution)/shard_map/ppermute | solution.py:677
  120.6 4.7 %readout.1 = f32[1,128]{1,0:T(1,128)} custom-call(s32[32]{0:T(128)S(1)} %copy-done.5, s32[32,128]{1,0:T(8,128)S(1)} %copy-done.3, bf16[32,1024,128]{2,1,0:T(8,128)(2,1)S(1)} %probe_weights.1.weight_ref, bf16[192,1024]{1,0:T(8,128)(2,1)S(1)} %pad_maximum_fusion.near_ref, bf16[192,1024]{1,0:T(8,128)(2,1)S(1)} %collective-permute-done.29.far_ref), custom_call_target="tpu_custom_call" | custom-call | tf_op jit(solution)/shard_map/readout/pallas_call | solution.py:655
  (41 shorter events, 0.1 us)
Async XLA Ops:
  2.8 14.9 %collective-permute-start = (bf16[32,1536]{1,0:T(8,128)(2,1)}, bf16[32,1536]{1,0:T(8,128)(2,1)S(1)}, u32[]{:S(2)}, u32[]{:S(2)}) collective-permute-start(bf16[32,1536]{1,0:T(8,128)(2,1)} %get-tuple-element.44), channel_id=1, source_target_pairs={{0,56},{8,16},{16,8},{24,32},{32,24},{40,48},{48,40},{56,0},{1,57}... | collective-permute-start | bytes 294920 | tf_op jit(solution)/shard_map/ppermute | solution.py:672
  13.1 9.8 %collective-permute-start.1 = (bf16[32,1536]{1,0:T(8,128)(2,1)}, bf16[32,1536]{1,0:T(8,128)(2,1)S(1)}, u32[]{:S(2)}, u32[]{:S(2)}) collective-permute-start(bf16[32,1536]{1,0:T(8,128)(2,1)} %get-tuple-element.45), channel_id=1, source_target_pairs={{0,7},{1,2},{2,1},{3,4},{4,3},{5,6},{6,5},{7,0},{8,15},{9,10},{10,... | collective-permute-start | bytes 294920 | tf_op jit(solution)/shard_map/ppermute | solution.py:672
  14.6 8.2 %collective-permute-start.2 = (bf16[32,1536]{1,0:T(8,128)(2,1)}, bf16[32,1536]{1,0:T(8,128)(2,1)S(1)}, u32[]{:S(2)}, u32[]{:S(2)}) collective-permute-start(bf16[32,1536]{1,0:T(8,128)(2,1)} %get-tuple-element.46), channel_id=1, source_target_pairs={{0,8},{8,0},{16,24},{24,16},{32,40},{40,32},{48,56},{56,48},{1,9},... | collective-permute-start | bytes 294920 | tf_op jit(solution)/shard_map/ppermute | solution.py:672
  14.6 8.2 %collective-permute-start.3 = (bf16[32,1536]{1,0:T(8,128)(2,1)}, bf16[32,1536]{1,0:T(8,128)(2,1)S(1)}, u32[]{:S(2)}, u32[]{:S(2)}) collective-permute-start(bf16[32,1536]{1,0:T(8,128)(2,1)} %get-tuple-element.47), channel_id=1, source_target_pairs={{0,64},{64,0},{128,192},{192,128},{1,65},{65,1},{129,193},{193,129... | collective-permute-start | bytes 294920 | tf_op jit(solution)/shard_map/ppermute | solution.py:672
  15.9 7.0 %collective-permute-start.4 = (bf16[32,1536]{1,0:T(8,128)(2,1)}, bf16[32,1536]{1,0:T(8,128)(2,1)S(1)}, u32[]{:S(2)}, u32[]{:S(2)}) collective-permute-start(bf16[32,1536]{1,0:T(8,128)(2,1)} %get-tuple-element.48), channel_id=1, source_target_pairs={{0,192},{64,128},{128,64},{192,0},{1,193},{65,129},{129,65},{193,1... | collective-permute-start | bytes 294920 | tf_op jit(solution)/shard_map/ppermute | solution.py:672
  17.7 5.2 %collective-permute-start.5 = (bf16[32,1536]{1,0:T(8,128)(2,1)}, bf16[32,1536]{1,0:T(8,128)(2,1)S(1)}, u32[]{:S(2)}, u32[]{:S(2)}) collective-permute-start(bf16[32,1536]{1,0:T(8,128)(2,1)} %get-tuple-element.49), channel_id=1, source_target_pairs={{0,1},{1,0},{2,3},{3,2},{4,5},{5,4},{6,7},{7,6},{8,9},{9,8},{10,11... | collective-permute-start | bytes 294920 | tf_op jit(solution)/shard_map/ppermute | solution.py:672
  22.9 1.0 copy-start.1
  23.9 1.3 %copy-start.6 = (bf16[4592,128]{1,0:T(8,128)(2,1)S(1)}, bf16[4592,128]{1,0:T(8,128)(2,1)}, u32[]{:S(2)}) copy-start(bf16[4592,128]{1,0:T(8,128)(2,1)} %get-tuple-element.43.refs_1_) | copy-start | bytes 3526660
  25.2 22.3 %copy-start = (bf16[2160,128]{1,0:T(8,128)(2,1)S(1)}, bf16[2160,128]{1,0:T(8,128)(2,1)}, u32[]{:S(2)}) copy-start(bf16[2160,128]{1,0:T(8,128)(2,1)} %get-tuple-element.42.pack_ref.refs_1_) | copy-start | bytes 1658884
  25.2 22.3 %copy-start.2 = (f32[32,32,128]{2,1,0:T(8,128)S(1)}, f32[32,32,128]{2,1,0:T(8,128)}, u32[]{:S(2)}) copy-start(f32[32,32,128]{2,1,0:T(8,128)} %get-tuple-element.41.refs_0_.geo_ref) | copy-start | bytes 1572868
  25.2 22.3 %copy-start.4 = (s32[128]{0:T(128)S(1)}, s32[128]{0:T(128)}, u32[]{:S(2)}) copy-start(s32[128]{0:T(128)} %param.20) | copy-start | bytes 1540
  34.9 12.6 %collective-permute-start.6 = (bf16[32,1536]{1,0:T(8,128)(2,1)S(1)}, bf16[32,1536]{1,0:T(8,128)(2,1)S(1)}, u32[]{:S(2)}, u32[]{:S(2)}) collective-permute-start(bf16[32,1536]{1,0:T(8,128)(2,1)S(1)} %get-tuple-element.50), channel_id=1, source_target_pairs={{0,56},{8,16},{16,8},{24,32},{32,24},{40,48},{48,40},{56,0},{1,57}... | collective-permute-start | bytes 294920 | tf_op jit(solution)/shard_map/ppermute | solution.py:672
  43.1 7.6 %collective-permute-start.7 = (bf16[32,1536]{1,0:T(8,128)(2,1)S(1)}, bf16[32,1536]{1,0:T(8,128)(2,1)S(1)}, u32[]{:S(2)}, u32[]{:S(2)}) collective-permute-start(bf16[32,1536]{1,0:T(8,128)(2,1)S(1)} %get-tuple-element.51), channel_id=1, source_target_pairs={{0,7},{1,2},{2,1},{3,4},{4,3},{5,6},{6,5},{7,0},{8,15},{9,10},{10,... | collective-permute-start | bytes 294920 | tf_op jit(solution)/shard_map/ppermute | solution.py:672
  44.5 6.3 %collective-permute-start.8 = (bf16[32,1536]{1,0:T(8,128)(2,1)S(1)}, bf16[32,1536]{1,0:T(8,128)(2,1)S(1)}, u32[]{:S(2)}, u32[]{:S(2)}) collective-permute-start(bf16[32,1536]{1,0:T(8,128)(2,1)S(1)} %get-tuple-element.52), channel_id=1, source_target_pairs={{0,8},{8,0},{16,24},{24,16},{32,40},{40,32},{48,56},{56,48},{1,9},... | collective-permute-start | bytes 294920 | tf_op jit(solution)/shard_map/ppermute | solution.py:672
  44.5 6.3 %collective-permute-start.9 = (bf16[32,1536]{1,0:T(8,128)(2,1)S(1)}, bf16[32,1536]{1,0:T(8,128)(2,1)S(1)}, u32[]{:S(2)}, u32[]{:S(2)}) collective-permute-start(bf16[32,1536]{1,0:T(8,128)(2,1)S(1)} %get-tuple-element.53), channel_id=1, source_target_pairs={{0,64},{64,0},{128,192},{192,128},{1,65},{65,1},{129,193},{193,129... | collective-permute-start | bytes 294920 | tf_op jit(solution)/shard_map/ppermute | solution.py:672
  45.7 5.4 %collective-permute-start.10 = (bf16[32,1536]{1,0:T(8,128)(2,1)S(1)}, bf16[32,1536]{1,0:T(8,128)(2,1)S(1)}, u32[]{:S(2)}, u32[]{:S(2)}) collective-permute-start(bf16[32,1536]{1,0:T(8,128)(2,1)S(1)} %get-tuple-element.54), channel_id=1, source_target_pairs={{0,192},{64,128},{128,64},{192,0},{1,193},{65,129},{129,65},{193,1... | collective-permute-start | bytes 294920 | tf_op jit(solution)/shard_map/ppermute | solution.py:672
  47.5 3.6 %collective-permute-start.11 = (bf16[32,1536]{1,0:T(8,128)(2,1)S(1)}, bf16[32,1536]{1,0:T(8,128)(2,1)S(1)}, u32[]{:S(2)}, u32[]{:S(2)}) collective-permute-start(bf16[32,1536]{1,0:T(8,128)(2,1)S(1)} %get-tuple-element.55), channel_id=1, source_target_pairs={{0,1},{1,0},{2,3},{3,2},{4,5},{5,4},{6,7},{7,6},{8,9},{9,8},{10,11... | collective-permute-start | bytes 294920 | tf_op jit(solution)/shard_map/ppermute | solution.py:672
  61.0 11.1 %collective-permute-start.12 = (bf16[32,1536]{1,0:T(8,128)(2,1)S(1)}, bf16[32,1536]{1,0:T(8,128)(2,1)S(1)}, u32[]{:S(2)}, u32[]{:S(2)}) collective-permute-start(bf16[32,1536]{1,0:T(8,128)(2,1)S(1)} %get-tuple-element.57), channel_id=1, source_target_pairs={{0,56},{8,16},{16,8},{24,32},{32,24},{40,48},{48,40},{56,0},{1,57}... | collective-permute-start | bytes 294920 | tf_op jit(solution)/shard_map/ppermute | solution.py:672
  66.2 8.4 %collective-permute-start.13 = (bf16[32,1536]{1,0:T(8,128)(2,1)S(1)}, bf16[32,1536]{1,0:T(8,128)(2,1)S(1)}, u32[]{:S(2)}, u32[]{:S(2)}) collective-permute-start(bf16[32,1536]{1,0:T(8,128)(2,1)S(1)} %get-tuple-element.58), channel_id=1, source_target_pairs={{0,7},{1,2},{2,1},{3,4},{4,3},{5,6},{6,5},{7,0},{8,15},{9,10},{10,... | collective-permute-start | bytes 294920 | tf_op jit(solution)/shard_map/ppermute | solution.py:672
  69.1 5.5 %collective-permute-start.14 = (bf16[32,1536]{1,0:T(8,128)(2,1)S(1)}, bf16[32,1536]{1,0:T(8,128)(2,1)S(1)}, u32[]{:S(2)}, u32[]{:S(2)}) collective-permute-start(bf16[32,1536]{1,0:T(8,128)(2,1)S(1)} %get-tuple-element.59), channel_id=1, source_target_pairs={{0,8},{8,0},{16,24},{24,16},{32,40},{40,32},{48,56},{56,48},{1,9},... | collective-permute-start | bytes 294920 | tf_op jit(solution)/shard_map/ppermute | solution.py:672
  69.1 5.5 %collective-permute-start.15 = (bf16[32,1536]{1,0:T(8,128)(2,1)S(1)}, bf16[32,1536]{1,0:T(8,128)(2,1)S(1)}, u32[]{:S(2)}, u32[]{:S(2)}) collective-permute-start(bf16[32,1536]{1,0:T(8,128)(2,1)S(1)} %get-tuple-element.60), channel_id=1, source_target_pairs={{0,64},{64,0},{128,192},{192,128},{1,65},{65,1},{129,193},{193,129... | collective-permute-start | bytes 294920 | tf_op jit(solution)/shard_map/ppermute | solution.py:672
  70.1 4.7 %collective-permute-start.16 = (bf16[32,1536]{1,0:T(8,128)(2,1)S(1)}, bf16[32,1536]{1,0:T(8,128)(2,1)S(1)}, u32[]{:S(2)}, u32[]{:S(2)}) collective-permute-start(bf16[32,1536]{1,0:T(8,128)(2,1)S(1)} %get-tuple-element.61), channel_id=1, source_target_pairs={{0,192},{64,128},{128,64},{192,0},{1,193},{65,129},{129,65},{193,1... | collective-permute-start | bytes 294920 | tf_op jit(solution)/shard_map/ppermute | solution.py:672
  72.1 2.6 %collective-permute-start.17 = (bf16[32,1536]{1,0:T(8,128)(2,1)S(1)}, bf16[32,1536]{1,0:T(8,128)(2,1)S(1)}, u32[]{:S(2)}, u32[]{:S(2)}) collective-permute-start(bf16[32,1536]{1,0:T(8,128)(2,1)S(1)} %get-tuple-element.62), channel_id=1, source_target_pairs={{0,1},{1,0},{2,3},{3,2},{4,5},{5,4},{6,7},{7,6},{8,9},{9,8},{10,11... | collective-permute-start | bytes 294920 | tf_op jit(solution)/shard_map/ppermute | solution.py:672
  74.7 32.6 %copy-start.5 = (s32[32]{0:T(128)S(1)}, s32[32]{0:T(128)}, u32[]{:S(2)}) copy-start(s32[32]{0:T(128)} %slab_ref.3) | copy-start | bytes 388
  74.7 36.9 %copy-start.7 = (f32[3,32,128]{2,1,0:T(8,128)S(1)}, f32[3,32,128]{2,1,0:T(8,128)}, u32[]{:S(2)}) copy-start(f32[3,32,128]{2,1,0:T(8,128)} %vec_ref.1) | copy-start | bytes 147460
  74.7 36.9 %copy-start.8 = (s32[128]{0:T(128)S(1)}, s32[128]{0:T(128)}, u32[]{:S(2)}) copy-start(s32[128]{0:T(128)} %param.36) | copy-start | bytes 1540
  85.4 35.2 %copy-start.3 = (s32[32,128]{1,0:T(8,128)S(1)}, s32[32,128]{1,0:T(8,128)}, u32[]{:S(2)}) copy-start(s32[32,128]{1,0:T(8,128)} %idx_ref.1) | copy-start | bytes 49156
  85.4 11.4 %collective-permute-start.18 = (bf16[32,1024]{1,0:T(8,128)(2,1)S(1)}, bf16[32,1024]{1,0:T(8,128)(2,1)S(1)}, u32[]{:S(2)}, u32[]{:S(2)}) collective-permute-start(bf16[32,1024]{1,0:T(8,128)(2,1)S(1)} %get-tuple-element.65), channel_id=1, source_target_pairs={{0,61},{1,60},{2,63},{3,62},{4,57},{5,56},{6,59},{7,58},{8,21},{9,... | collective-permute-start | bytes 196616 | tf_op jit(solution)/shard_map/ppermute | solution.py:695
  93.0 5.7 %collective-permute-start.19 = (bf16[32,1024]{1,0:T(8,128)(2,1)S(1)}, bf16[32,1024]{1,0:T(8,128)(2,1)S(1)}, u32[]{:S(2)}, u32[]{:S(2)}) collective-permute-start(bf16[32,1024]{1,0:T(8,128)(2,1)S(1)} %get-tuple-element.66), channel_id=1, source_target_pairs={{0,1},{1,4},{2,7},{3,2},{4,5},{5,0},{6,3},{7,6},{8,9},{9,12},{10,1... | collective-permute-start | bytes 196616 | tf_op jit(solution)/shard_map/ppermute | solution.py:688
  93.0 3.8 %collective-permute-start.25 = (bf16[16,1024]{1,0:T(8,128)(2,1)S(1)}, bf16[16,1024]{1,0:T(8,128)(2,1)S(1)}, u32[]{:S(2)}, u32[]{:S(2)}) collective-permute-start(bf16[16,1024]{1,0:T(8,128)(2,1)S(1)} %get-tuple-element.73), channel_id=1, source_target_pairs={{0,2},{1,3},{2,0},{3,1},{4,6},{5,7},{6,4},{7,5},{8,10},{9,11},{10,... | collective-permute-start | bytes 98312 | tf_op jit(solution)/shard_map/ppermute | solution.py:677
  93.0 14.3 %collective-permute-start.23 = (bf16[48,1024]{1,0:T(8,128)(2,1)S(1)}, bf16[48,1024]{1,0:T(8,128)(2,1)S(1)}, u32[]{:S(2)}, u32[]{:S(2)}) collective-permute-start(bf16[48,1024]{1,0:T(8,128)(2,1)S(1)} %get-tuple-element.70), channel_id=1, source_target_pairs={{0,6},{1,7},{2,4},{3,5},{4,2},{5,3},{6,0},{7,1},{8,14},{9,15},{10,... | collective-permute-start | bytes 294920 | tf_op jit(solution)/shard_map/ppermute | solution.py:688
  96.8 10.5 %collective-permute-start.24 = (bf16[48,1024]{1,0:T(8,128)(2,1)S(1)}, bf16[48,1024]{1,0:T(8,128)(2,1)S(1)}, u32[]{:S(2)}, u32[]{:S(2)}) collective-permute-start(bf16[48,1024]{1,0:T(8,128)(2,1)S(1)} %get-tuple-element.72), channel_id=1, source_target_pairs={{0,1},{1,0},{2,3},{3,2},{4,5},{5,4},{6,7},{7,6},{8,9},{9,8},{10,11... | collective-permute-start | bytes 294920 | tf_op jit(solution)/shard_map/ppermute | solution.py:677
  96.8 5.8 %collective-permute-start.20 = (bf16[32,1024]{1,0:T(8,128)(2,1)S(1)}, bf16[32,1024]{1,0:T(8,128)(2,1)S(1)}, u32[]{:S(2)}, u32[]{:S(2)}) collective-permute-start(bf16[32,1024]{1,0:T(8,128)(2,1)S(1)} %get-tuple-element.67), channel_id=1, source_target_pairs={{0,12},{1,13},{2,14},{3,15},{4,8},{5,9},{6,10},{7,11},{8,4},{9,5},... | collective-permute-start | bytes 196616 | tf_op jit(solution)/shard_map/ppermute | solution.py:695
  96.8 6.3 %collective-permute-start.21 = (bf16[32,1024]{1,0:T(8,128)(2,1)S(1)}, bf16[32,1024]{1,0:T(8,128)(2,1)S(1)}, u32[]{:S(2)}, u32[]{:S(2)}) collective-permute-start(bf16[32,1024]{1,0:T(8,128)(2,1)S(1)} %get-tuple-element.68), channel_id=1, source_target_pairs={{0,66},{1,67},{2,64},{3,65},{4,70},{5,71},{6,68},{7,69},{64,2},{65... | collective-permute-start | bytes 196616 | tf_op jit(solution)/shard_map/ppermute | solution.py:695
  98.8 8.6 %collective-permute-start.22 = (bf16[32,1024]{1,0:T(8,128)(2,1)S(1)}, bf16[32,1024]{1,0:T(8,128)(2,1)S(1)}, u32[]{:S(2)}, u32[]{:S(2)}) collective-permute-start(bf16[32,1024]{1,0:T(8,128)(2,1)S(1)} %get-tuple-element.69), channel_id=1, source_target_pairs={{0,195},{1,194},{2,193},{3,192},{4,199},{5,198},{6,197},{7,196},{6... | collective-permute-start | bytes 196616 | tf_op jit(solution)/shard_map/ppermute | solution.py:695
  108.0 7.0 %collective-permute-start.28 = (bf16[48,1024]{1,0:T(8,128)(2,1)S(1)}, bf16[48,1024]{1,0:T(8,128)(2,1)S(1)}, u32[]{:S(2)}, u32[]{:S(2)}) collective-permute-start(bf16[48,1024]{1,0:T(8,128)(2,1)S(1)} %collect.1), channel_id=1, source_target_pairs={{0,6},{1,7},{2,4},{3,5},{4,2},{5,3},{6,0},{7,1},{8,14},{9,15},{10,... | collective-permute-start | bytes 294920 | tf_op jit(solution)/shard_map/ppermute | solution.py:677
  109.2 9.5 %collective-permute-start.27 = (bf16[48,1024]{1,0:T(8,128)(2,1)S(1)}, bf16[48,1024]{1,0:T(8,128)(2,1)S(1)}, u32[]{:S(2)}, u32[]{:S(2)}) collective-permute-start(bf16[48,1024]{1,0:T(8,128)(2,1)S(1)} %collect.1), channel_id=1, source_target_pairs={{0,4},{1,5},{2,6},{3,7},{4,0},{5,1},{6,2},{7,3},{8,12},{9,13},{10,... | collective-permute-start | bytes 294920 | tf_op jit(solution)/shard_map/ppermute | solution.py:677
  109.2 9.5 %collective-permute-start.26 = (bf16[48,1024]{1,0:T(8,128)(2,1)S(1)}, bf16[48,1024]{1,0:T(8,128)(2,1)S(1)}, u32[]{:S(2)}, u32[]{:S(2)}) collective-permute-start(bf16[48,1024]{1,0:T(8,128)(2,1)S(1)} %collect.1), channel_id=1, source_target_pairs={{0,2},{1,3},{2,0},{3,1},{4,6},{5,7},{6,4},{7,5},{8,10},{9,11},{10,... | collective-permute-start | bytes 294920 | tf_op jit(solution)/shard_map/ppermute | solution.py:677
  118.7 1.8 %collective-permute-start.29 = (bf16[192,1024]{1,0:T(8,128)(2,1)S(1)}, bf16[192,1024]{1,0:T(8,128)(2,1)S(1)}, u32[]{:S(2)}, u32[]{:S(2)}) collective-permute-start(bf16[192,1024]{1,0:T(8,128)(2,1)S(1)} %pad_maximum_fusion.near_ref), channel_id=1, source_target_pairs={{0,1},{1,0},{2,3},{3,2},{4,5},{5,4},{6,7},{7,6},{8,9},{9,8},{10,11... | collective-permute-start | bytes 1179656 | tf_op jit(solution)/shard_map/ppermute | solution.py:677
